TPU v7x, 512 devices: a whole 4x8x8 slice. The times are simulated.
512 devices in a mesh: row: 8 (over y), col: 16 (over x_lo, z), layer: 4 (over x_hi, core).
Axes of the slice: x: 4 (x_hi: 2, x_lo: 2; x = x_hi * 2 + x_lo), y: 8, z: 8, core: 2. Of those that a mesh axis runs over, the one named last changes fastest.
Arguments:
- integrals: bfloat16 [64, 1024, 3072], P('layer', 'col', 'row'), may hold values from -0.0234375 to 0.0234375
- amplitudes: bfloat16 [64, 1024, 2048], P('layer', 'row', 'col'), may hold values from -6 to 6
- coulomb: bfloat16 [3072, 2048], P(('row', 'layer'), 'col'), may hold values from -6 to 6
- row_gap: float32 [3072], P(('row', 'layer')), may hold values from 0.5 to 4
- col_gap: float32 [2048], P('col'), may hold values from 0.5 to 4
Outputs:
- residual: float32 [3072, 2048], P(('row', 'layer'), 'col')
All inputs are finite; a program needn't handle non-finite values.
Results may differ from a plain program's by a relative error of at most 0.0003.
Values may be sent and summed in bfloat16 or wider, within the bound.
No kernel may reach another device: no remote copies, remote signals or barrier semaphores. Data moves between devices by JAX's collectives and lax.ppermute only.
A program may use at most 64 MiB of HBM per device.

v0:
```python
import jax
import jax.numpy as jnp
from jax import lax
from jax.sharding import PartitionSpec as P


def local(integrals, amplitudes, coulomb, row_gap, col_gap):
    contract = (((0, 1), (0, 1)), ((), ()))
    gathered = lax.all_gather(amplitudes, "row", axis=1, tiled=True)
    partial_sum = lax.dot_general(
        lax.all_gather(integrals, "col", axis=1, tiled=True),
        gathered,
        contract,
        preferred_element_type=jnp.float32,
    )
    share_rows = coulomb.shape[0]
    summed_all = lax.psum(partial_sum, "layer")
    own_rows = lax.dynamic_slice_in_dim(
        summed_all, lax.axis_index("layer") * share_rows, share_rows, 0
    )
    gap_sum = row_gap[:, None] + col_gap[None, :]
    return (coulomb.astype(jnp.float32) + own_rows) / gap_sum


def solution(mesh):
    placed = (
        P("layer", "col", "row"),
        P("layer", "row", "col"),
        P(("row", "layer"), "col"),
        P(("row", "layer")),
        P("col"),
    )
    return jax.shard_map(
        local, mesh=mesh, in_specs=placed, out_specs=P(("row", "layer"), "col"), check_vma=False
    )
```

profile of v0, /device:TPU:1, one launch (start us, length us, event | category | flops | bytes accessed | tf_op | source)
XLA Modules:
  0.0 286.8 jit_solution(3546155924513565021)
XLA Ops:
  6.5 0.0 copy-start
  6.5 0.0 copy-start.1
  6.5 0.0 copy-start.2
  6.5 0.0 all-gather.5.cloned.1.call-start
  6.5 0.7 all-gather.5.cloned.1.call-update
  7.3 0.0 all-gather.3.cloned.1.call-start
  7.3 0.7 all-gather.3.cloned.1.call-update
  8.0 0.0 all-reduce.2.cloned.1.call-start
  8.1 64.0 %all-gather.5.cloned.1.call-done = bf16[16,1024,128]{2,1,0:T(8,128)(2,1)} async-done(((bf16[16,128,128]{2,1,0:T(8,128)(2,1)}), bf16[16,1024,128]{2,1,0:T(8,128)(2,1)}) %all-gather.5.cloned.1.call-update) | async-done | bytes 4194320 | tf_op jit(solution)/shard_map/all_gather | solution.py:9
  72.1 147.7 %all-gather.3.cloned.1.call-done = bf16[16,1024,384]{2,1,0:T(8,128)(2,1)} async-done(((bf16[16,64,384]{2,1,0:T(8,128)(2,1)}), bf16[16,1024,384]{2,1,0:T(8,128)(2,1)}) %all-gather.3.cloned.1.call-update) | async-done | bytes 12582928 | tf_op jit(solution)/shard_map/all_gather | solution.py:11
  219.8 9.9 %convolution_bitcast_fusion = f32[384,128]{1,0:T(8,128)} fusion(bf16[16,1024,384]{2,1,0:T(8,128)(2,1)} %all-gather.3.cloned.1.call-done, bf16[16,1024,128]{2,1,0:T(8,128)(2,1)} %all-gather.5.cloned.1.call-done), kind=kOutput, calls=%fused_computation | convolution fusion | flops 1610612736 | bytes 16973824 | tf_op jit(solution)/shard_map/dot_general | solution.py:10
  229.7 0.0 all-reduce.2.cloned.1.call-update
  229.7 49.0 %all-reduce.2.cloned.1.call-done = f32[384,128]{1,0:T(8,128)} async-done(((f32[384,128]{1,0:T(8,128)}), f32[384,128]{1,0:T(8,128)}) %all-reduce.2.cloned.1.call-update) | async-done | bytes 196624 | tf_op jit(solution)/shard_map/psum | solution.py:17
  278.7 0.0 copy-done
  278.7 0.0 copy-done.1
  278.7 0.0 copy-done.2
  278.7 1.5 add_divide_fusion
Async XLA Ops:
  6.5 272.2 %copy-start = (bf16[96,128]{1,0:T(8,128)(2,1)S(1)}, bf16[96,128]{1,0:T(8,128)(2,1)}, u32[]{:S(2)}) copy-start(bf16[96,128]{1,0:T(8,128)(2,1)} %param.7) | copy-start | bytes 73732
  6.5 272.2 %copy-start.1 = (f32[128]{0:T(128)S(1)}, f32[128]{0:T(128)}, u32[]{:S(2)}) copy-start(f32[128]{0:T(128)} %param.9) | copy-start | bytes 1540
  6.5 272.2 %copy-start.2 = (f32[96]{0:T(128)S(1)}, f32[96]{0:T(128)}, u32[]{:S(2)}) copy-start(f32[96]{0:T(128)} %param.8) | copy-start | bytes 1156
  6.5 65.6 %all-gather.5.cloned.1.call-start = ((), (), s32[]{:S(2)}) async-start(), calls=%async_computation.1 | async-start | bytes 4718592 | tf_op jit(solution)/shard_map/all_gather | solution.py:9
  7.3 212.5 %all-gather.3.cloned.1.call-start = ((), (), s32[]{:S(2)}) async-start(), calls=%async_computation | async-start | bytes 13369344 | tf_op jit(solution)/shard_map/all_gather | solution.py:11
  8.0 270.7 %all-reduce.2.cloned.1.call-start = ((), (), s32[]{:S(2)}) async-start(), calls=%async_computation.2 | async-start | bytes 393216 | tf_op jit(solution)/shard_map/psum | solution.py:17
Sparse Core Ops, SparseCore 0:
  9.4 62.6 all-gather.4
  74.2 145.5 all-gather.2
  229.8 48.8 all-reduce.1
where the time goes:
time: 287 us
  waiting for transfers between devices  262 us (91%)
  between operations  13.1 us (5%)
  matrix products  9.89 us (3%)
    all_gather x1, waiting for transfers between devices, local(): lax.all_gather(integrals, 'col', axis=1, tiled=True)  148 us
    all_gather x1, waiting for transfers between devices, local(): gathered = lax.all_gather(amplitudes, 'row', axis=1, tiled=True)  64 us
    psum x1, waiting for transfers between devices, local(): summed_all = lax.psum(partial_sum, 'layer')  49 us
    dot_general x1, matrix products, local(): lax.dot_general(lax.all_gather(integrals, 'col', axis=1, tiled=True), gat...  9.89 us
  transfers between devices with their start and end apart: 3, of which 3 were waited for; matrix products, arithmetic and copies ran while one was open for 0% of the time, Pallas kernels for 0%

commit v1 on v0

v1 whole, which is shorter than its diff:
```python
import jax
import jax.numpy as jnp
from jax import lax
from jax.sharding import Mesh, PartitionSpec as P

NZ = 8
CONTRACT = (((0, 1, 2), (0, 1, 2)), ((), ()))


def local(integrals, amplitudes, coulomb, row_gap, col_gap):
    z = lax.axis_index("z")
    amp = lax.all_to_all(amplitudes.reshape(2, 8, 128, 128), "xl", 0, 0, tiled=True)
    mine = lax.all_to_all(integrals.reshape(2, 8, 64, 384), "xl", 0, 0, tiled=True)
    amps = lax.all_gather(amp, "y").reshape(2, 4, 2, 8, 2, 64, 128)

    def times(block, source):
        part = lax.dynamic_slice(
            amps, (0, source // 2, 0, 0, source % 2, 0, 0), (2, 1, 2, 8, 1, 64, 128)
        ).reshape(2, 2, 8, 64, 128)
        return [
            lax.dot_general(block, part[:, n], CONTRACT, preferred_element_type=jnp.float32)
            for n in range(2)
        ]

    up = [(i, (i + 1) % NZ) for i in range(NZ)]
    down = [(i, (i - 1) % NZ) for i in range(NZ)]
    total = times(mine, z)
    above = below = mine
    for step in range(1, 4):
        below = lax.ppermute(below, "z", up)
        above = lax.ppermute(above, "z", down)
        for block, source in ((below, (z - step) % NZ), (above, (z + step) % NZ)):
            total = [t + p for t, p in zip(total, times(block, source))]
    last = jnp.concatenate(
        [lax.ppermute(below[:1], "z", up), lax.ppermute(above[1:], "z", down)]
    )
    total = [t + p for t, p in zip(total, times(last, (z + 4) % NZ))]

    shares = jnp.stack(total).reshape(8, 96, 128)
    shares = lax.all_to_all(shares, ("xl", "xh", "core"), 0, 0, tiled=True)
    own = jnp.sum(shares, axis=0)
    gap_sum = row_gap[:, None] + col_gap[None, :]
    return (coulomb.astype(jnp.float32) + own) / gap_sum


def solution(mesh):
    fine = Mesh(mesh.devices.reshape(8, 2, 8, 2, 2), ("y", "xl", "z", "xh", "core"))
    layer, col = ("xh", "core"), ("xl", "z")
    placed = (
        P(layer, col, "y"),
        P(layer, "y", col),
        P(("y",) + layer, col),
        P(("y",) + layer),
        P(col),
    )
    return jax.shard_map(
        local, mesh=fine, in_specs=placed, out_specs=P(("y",) + layer, col), check_vma=False
    )
```

time: 287 us -> 145 us (0.51)
  waiting for transfers between devices: 262 us -> 42.6 us
  blocking collectives: 0 us -> 38.9 us
  starting transfers between devices: 0.08 us -> 36.2 us
  local copies, waits for them, and re-layouts: 0.01 us -> 6.46 us
  matrix products: 9.89 us -> 5.31 us
    all_gather x2 -> x1, waiting for transfers between devices: 212 us -> 0.02 us  [local(): amps = lax.all_gather(amp, 'y').reshape(2, 4, 2, 8, 2, 64, 128)]
    psum x1 -> x0, waiting for transfers between devices: 49 us -> none  [local(): summed_all = lax.psum(partial_sum, 'layer')]
    ppermute x0 -> x8, waiting for transfers between devices: none -> 42.6 us  [the longest x3 38 us: local(): below = lax.ppermute(below, 'z', up)]
    all_to_all x0 -> x3, blocking collectives: none -> 38.9 us  [the longest x1 17.8 us: local(): shares = lax.all_to_all(shares, ('xl', 'xh', 'core'), 0, 0, tiled=True)]
    ppermute x0 -> x8, starting transfers between devices: none -> 36.2 us  [the longest x3 17.7 us: local(): above = lax.ppermute(above, 'z', down)]
    dot_general x1 -> x16, matrix products: 9.89 us -> 5.31 us  [times(): lax.dot_general(block, part[:, n], CONTRACT, preferred_element_type=jnp.f...]
    dynamic_slice x0 -> x3, local copies, waits for them, and re-layouts: none -> 3.83 us  [times(): lax.dynamic_slice(amps, (0, source // 2, 0, 0, source % 2, 0, 0), (2, 1,...]
  transfers between devices with their start and end apart: 3 -> 9, of which waited for: 3 -> 5; matrix products, arithmetic and copies ran while one was open for 0% -> 1% of each run, Pallas kernels for 0% -> 0%
where the time goes in v1:
time: 145 us; the launch traced here: 144 us
  waiting for transfers between devices  42.6 us (29%)
  blocking collectives  38.9 us (27%)
  starting transfers between devices  36.2 us (25%)
  between operations  14.2 us (10%)
  local copies, waits for them, and re-layouts  6.46 us (4%)
  matrix products  5.31 us (4%)
    ppermute x3, waiting for transfers between devices, local(): below = lax.ppermute(below, 'z', up)  38 us
    all_to_all x1, blocking collectives, local(): shares = lax.all_to_all(shares, ('xl', 'xh', 'core'), 0, 0, tiled=True)  17.8 us
    ppermute x3, starting transfers between devices, local(): above = lax.ppermute(above, 'z', down)  17.7 us
    ppermute x3, starting transfers between devices, local(): below = lax.ppermute(below, 'z', up)  12 us
    all_to_all x1, blocking collectives, local(): lax.all_to_all(integrals.reshape(2, 8, 64, 384), 'xl', 0, 0, tiled=True)  10.8 us
    all_to_all x1, blocking collectives, local(): lax.all_to_all(amplitudes.reshape(2, 8, 128, 128), 'xl', 0, 0, tiled=True)  10.3 us
    dot_general x16, matrix products, times(): lax.dot_general(block, part[:, n], CONTRACT, preferred_element_type=jnp.f...  5.31 us
    ppermute x1, starting transfers between devices, local(): lax.ppermute(above[1:], 'z', down)  4.56 us
  transfers between devices with their start and end apart: 9, of which 5 were waited for; matrix products, arithmetic and copies ran while one was open for 1% of the time, Pallas kernels for 0%

profile of v1, /device:TPU:1, one launch (start us, length us, event | category | flops | bytes accessed | tf_op | source)
XLA Modules:
  0.0 144.5 jit_solution(596656635204507198)
XLA Ops:
  6.5 10.3 %all_to_all.15 = bf16[2,8,128,128]{3,2,1,0:T(8,128)(2,1)} all-to-all(bf16[2,8,128,128]{3,2,1,0:T(8,128)(2,1)} %bitcast.205), channel_id=1, replica_groups=mesh['y'=8,'xl'=2,'z'=8,'xh'=2,'core'=2] {'xl'}, dimensions={0} | all-to-all | bytes 1048576 | tf_op jit(solution)/shard_map/all_to_all | solution.py:12
  16.9 10.8 %all_to_all.16 = bf16[2,8,64,384]{3,2,1,0:T(8,128)(2,1)S(1)} all-to-all(bf16[2,8,64,384]{3,2,1,0:T(8,128)(2,1)} %bitcast.204), channel_id=1, replica_groups=mesh['y'=8,'xl'=2,'z'=8,'xh'=2,'core'=2] {'xl'}, dimensions={0} | all-to-all | bytes 1572864 | tf_op jit(solution)/shard_map/all_to_all | solution.py:13
  27.7 8.1 %collective-permute-start = (bf16[2,8,64,384]{3,2,1,0:T(8,128)(2,1)S(1)}, bf16[2,8,64,384]{3,2,1,0:T(8,128)(2,1)S(1)}, u32[]{:S(2)}, u32[]{:S(2)}) collective-permute-start(bf16[2,8,64,384]{3,2,1,0:T(8,128)(2,1)S(1)} %all_to_all.16), channel_id=1, source_target_pairs={{0,4},{4,8},{8,12},{12,16},{16,20},{20,24},{24,28},{28,0},{1,5},{5... | collective-permute-start | bytes 2359304 | tf_op jit(solution)/shard_map/ppermute | solution.py:30
  35.9 8.6 %collective-permute-start.1 = (bf16[2,8,64,384]{3,2,1,0:T(8,128)(2,1)S(1)}, bf16[2,8,64,384]{3,2,1,0:T(8,128)(2,1)S(1)}, u32[]{:S(2)}, u32[]{:S(2)}) collective-permute-start(bf16[2,8,64,384]{3,2,1,0:T(8,128)(2,1)S(1)} %all_to_all.16), channel_id=1, source_target_pairs={{0,28},{4,0},{8,4},{12,8},{16,12},{20,16},{24,20},{28,24},{1,29},{... | collective-permute-start | bytes 2359304 | tf_op jit(solution)/shard_map/ppermute | solution.py:31
  44.4 13.5 %collective-permute-done = bf16[2,8,64,384]{3,2,1,0:T(8,128)(2,1)S(1)} collective-permute-done((bf16[2,8,64,384]{3,2,1,0:T(8,128)(2,1)S(1)}, bf16[2,8,64,384]{3,2,1,0:T(8,128)(2,1)S(1)}, u32[]{:S(2)}, u32[]{:S(2)}) %collective-permute-start) | collective-permute-done | bytes 786464 | tf_op jit(solution)/shard_map/ppermute | solution.py:30
  58.0 1.9 %collective-permute-start.2 = (bf16[2,8,64,384]{3,2,1,0:T(8,128)(2,1)S(1)}, bf16[2,8,64,384]{3,2,1,0:T(8,128)(2,1)S(1)}, u32[]{:S(2)}, u32[]{:S(2)}) collective-permute-start(bf16[2,8,64,384]{3,2,1,0:T(8,128)(2,1)S(1)} %collective-permute-done), channel_id=1, source_target_pairs={{0,4},{4,8},{8,12},{12,16},{16,20},{20,24},{24,28},{28,0},{1,5},{5... | collective-permute-start | bytes 2359304 | tf_op jit(solution)/shard_map/ppermute | solution.py:30
  59.9 4.6 %collective-permute-start.3 = (bf16[2,8,64,384]{3,2,1,0:T(8,128)(2,1)S(1)}, bf16[2,8,64,384]{3,2,1,0:T(8,128)(2,1)S(1)}, u32[]{:S(2)}, u32[]{:S(2)}) collective-permute-start(bf16[2,8,64,384]{3,2,1,0:T(8,128)(2,1)S(1)} %collective-permute-done.1), channel_id=1, source_target_pairs={{0,28},{4,0},{8,4},{12,8},{16,12},{20,16},{24,20},{28,24},{1,29},{... | collective-permute-start | bytes 2359304 | tf_op jit(solution)/shard_map/ppermute | solution.py:31
  64.5 12.7 %collective-permute-done.2 = bf16[2,8,64,384]{3,2,1,0:T(8,128)(2,1)S(1)} collective-permute-done((bf16[2,8,64,384]{3,2,1,0:T(8,128)(2,1)S(1)}, bf16[2,8,64,384]{3,2,1,0:T(8,128)(2,1)S(1)}, u32[]{:S(2)}, u32[]{:S(2)}) %collective-permute-start.2) | collective-permute-done | bytes 786464 | tf_op jit(solution)/shard_map/ppermute | solution.py:30
  77.2 1.9 %collective-permute-start.4 = (bf16[2,8,64,384]{3,2,1,0:T(8,128)(2,1)S(1)}, bf16[2,8,64,384]{3,2,1,0:T(8,128)(2,1)S(1)}, u32[]{:S(2)}, u32[]{:S(2)}) collective-permute-start(bf16[2,8,64,384]{3,2,1,0:T(8,128)(2,1)S(1)} %collective-permute-done.2), channel_id=1, source_target_pairs={{0,4},{4,8},{8,12},{12,16},{16,20},{20,24},{24,28},{28,0},{1,5},{5... | collective-permute-start | bytes 2359304 | tf_op jit(solution)/shard_map/ppermute | solution.py:30
  79.2 4.6 %collective-permute-start.5 = (bf16[2,8,64,384]{3,2,1,0:T(8,128)(2,1)S(1)}, bf16[2,8,64,384]{3,2,1,0:T(8,128)(2,1)S(1)}, u32[]{:S(2)}, u32[]{:S(2)}) collective-permute-start(bf16[2,8,64,384]{3,2,1,0:T(8,128)(2,1)S(1)} %collective-permute-done.3), channel_id=1, source_target_pairs={{0,28},{4,0},{8,4},{12,8},{16,12},{20,16},{24,20},{28,24},{1,29},{... | collective-permute-start | bytes 2359304 | tf_op jit(solution)/shard_map/ppermute | solution.py:31
  83.8 11.8 %collective-permute-done.4 = bf16[2,8,64,384]{3,2,1,0:T(8,128)(2,1)S(1)} collective-permute-done((bf16[2,8,64,384]{3,2,1,0:T(8,128)(2,1)S(1)}, bf16[2,8,64,384]{3,2,1,0:T(8,128)(2,1)S(1)}, u32[]{:S(2)}, u32[]{:S(2)}) %collective-permute-start.4) | collective-permute-done | bytes 786464 | tf_op jit(solution)/shard_map/ppermute | solution.py:30
  95.6 1.9 %collective-permute-start.6 = (bf16[1,8,64,384]{3,2,1,0:T(8,128)(2,1)S(1)}, bf16[1,8,64,384]{3,2,1,0:T(8,128)(2,1)S(1)}, u32[]{:S(2)}, u32[]{:S(2)}) collective-permute-start(bf16[1,8,64,384]{3,2,1,0:T(8,128)(2,1)S(1)} %slice.79), channel_id=1, source_target_pairs={{0,4},{4,8},{8,12},{12,16},{16,20},{20,24},{24,28},{28,0},{1,5},{5... | collective-permute-start | bytes 1179656 | tf_op jit(solution)/shard_map/ppermute | solution.py:35
  97.5 0.8 slice.80
  98.4 4.6 %collective-permute-start.7 = (bf16[1,8,64,384]{3,2,1,0:T(8,128)(2,1)}, bf16[1,8,64,384]{3,2,1,0:T(8,128)(2,1)}, u32[]{:S(2)}, u32[]{:S(2)}) collective-permute-start(bf16[1,8,64,384]{3,2,1,0:T(8,128)(2,1)} %slice.80), channel_id=1, source_target_pairs={{0,28},{4,0},{8,4},{12,8},{16,12},{20,16},{24,20},{28,24},{1,29},{... | collective-permute-start | bytes 1179656 | tf_op jit(solution)/shard_map/ppermute | solution.py:35
  103.3 2.0 %collective-permute-done.6 = bf16[1,8,64,384]{3,2,1,0:T(8,128)(2,1)S(1)} collective-permute-done((bf16[1,8,64,384]{3,2,1,0:T(8,128)(2,1)S(1)}, bf16[1,8,64,384]{3,2,1,0:T(8,128)(2,1)S(1)}, u32[]{:S(2)}, u32[]{:S(2)}) %collective-permute-start.6) | collective-permute-done | bytes 393248 | tf_op jit(solution)/shard_map/ppermute | solution.py:35
  105.4 2.6 %collective-permute-done.7 = bf16[1,8,64,384]{3,2,1,0:T(8,128)(2,1)} collective-permute-done((bf16[1,8,64,384]{3,2,1,0:T(8,128)(2,1)}, bf16[1,8,64,384]{3,2,1,0:T(8,128)(2,1)}, u32[]{:S(2)}, u32[]{:S(2)}) %collective-permute-start.7) | collective-permute-done | bytes 393248 | tf_op jit(solution)/shard_map/ppermute | solution.py:35
  108.0 1.1 constant_dynamic-update-slice_fusion
  109.0 3.8 %constant_dynamic-slice_fusion.2 = (bf16[2,1,2,8,1,64,128]{6,5,4,3,2,1,0:T(8,128)(2,1)S(1)}, bf16[2,1,2,8,1,64,128]{6,5,4,3,2,1,0:T(8,128)(2,1)S(1)}, bf16[2,1,2...) fusion(bf16[2,4,2,8,2,64,128]{6,5,4,3,2,1,0:T(8,128)(2,1)} %bit, ...), kind=kLoop, calls=%fused_computation.64 | loop fusion | bytes 8388672 | tf_op jit(solution)/shard_map/dynamic_slice | solution.py:17
  112.9 0.4 convolution_bitcast_fusion
  113.3 0.4 convolution_bitcast_fusion.8
  114.3 0.3 convolution_bitcast_fusion.9
  115.1 0.3 convolution_bitcast_fusion.11
  115.8 0.3 convolution_bitcast_fusion.13
  116.1 0.3 convolution_bitcast_fusion.7
  116.8 0.3 fusion.1
  117.1 0.3 fusion.10
  117.5 0.3 fusion.12
  117.9 0.3 fusion.3
  118.2 0.3 fusion.8
  118.6 0.3 fusion.17
  119.1 17.8 %all_to_all.17 = f32[8,96,128]{2,1,0:T(8,128)S(1)} all-to-all(f32[8,96,128]{2,1,0:T(8,128)S(1)} %bitcast.203), channel_id=1, replica_groups=mesh['y'=8,'xl'=2,'z'=8,'xh'=2,'core'=2] {'xl','xh','core'}, dimensions={0} | all-to-all | bytes 786432 | tf_op jit(solution)/shard_map/all_to_all | solution.py:40
  136.9 0.7 add_divide_fusion
  (42 shorter events, 2.2 us)
Async XLA Ops:
  6.5 102.5 %all-gather.3.cloned.1.call-start = ((), (), s32[]{:S(2)}) async-start(), calls=%async_computation.3 | async-start | bytes 4718592 | tf_op jit(solution)/shard_map/all_gather | solution.py:14
  27.7 30.3 %collective-permute-start = (bf16[2,8,64,384]{3,2,1,0:T(8,128)(2,1)S(1)}, bf16[2,8,64,384]{3,2,1,0:T(8,128)(2,1)S(1)}, u32[]{:S(2)}, u32[]{:S(2)}) collective-permute-start(bf16[2,8,64,384]{3,2,1,0:T(8,128)(2,1)S(1)} %all_to_all.16), channel_id=1, source_target_pairs={{0,4},{4,8},{8,12},{12,16},{16,20},{20,24},{24,28},{28,0},{1,5},{5... | collective-permute-start | bytes 2359304 | tf_op jit(solution)/shard_map/ppermute | solution.py:30
  35.9 24.1 %collective-permute-start.1 = (bf16[2,8,64,384]{3,2,1,0:T(8,128)(2,1)S(1)}, bf16[2,8,64,384]{3,2,1,0:T(8,128)(2,1)S(1)}, u32[]{:S(2)}, u32[]{:S(2)}) collective-permute-start(bf16[2,8,64,384]{3,2,1,0:T(8,128)(2,1)S(1)} %all_to_all.16), channel_id=1, source_target_pairs={{0,28},{4,0},{8,4},{12,8},{16,12},{20,16},{24,20},{28,24},{1,29},{... | collective-permute-start | bytes 2359304 | tf_op jit(solution)/shard_map/ppermute | solution.py:31
  58.0 6.5 %copy-start = (bf16[2,8,64,384]{3,2,1,0:T(8,128)(2,1)}, bf16[2,8,64,384]{3,2,1,0:T(8,128)(2,1)S(1)}, u32[]{:S(2)}) copy-start(bf16[2,8,64,384]{3,2,1,0:T(8,128)(2,1)S(1)} %collective-permute-done) | copy-start | bytes 2359300
  58.0 19.2 %collective-permute-start.2 = (bf16[2,8,64,384]{3,2,1,0:T(8,128)(2,1)S(1)}, bf16[2,8,64,384]{3,2,1,0:T(8,128)(2,1)S(1)}, u32[]{:S(2)}, u32[]{:S(2)}) collective-permute-start(bf16[2,8,64,384]{3,2,1,0:T(8,128)(2,1)S(1)} %collective-permute-done), channel_id=1, source_target_pairs={{0,4},{4,8},{8,12},{12,16},{16,20},{20,24},{24,28},{28,0},{1,5},{5... | collective-permute-start | bytes 2359304 | tf_op jit(solution)/shard_map/ppermute | solution.py:30
  59.9 19.2 %copy-start.4 = (bf16[2,8,64,384]{3,2,1,0:T(8,128)(2,1)}, bf16[2,8,64,384]{3,2,1,0:T(8,128)(2,1)S(1)}, u32[]{:S(2)}) copy-start(bf16[2,8,64,384]{3,2,1,0:T(8,128)(2,1)S(1)} %collective-permute-done.1) | copy-start | bytes 2359300
  59.9 19.2 %collective-permute-start.3 = (bf16[2,8,64,384]{3,2,1,0:T(8,128)(2,1)S(1)}, bf16[2,8,64,384]{3,2,1,0:T(8,128)(2,1)S(1)}, u32[]{:S(2)}, u32[]{:S(2)}) collective-permute-start(bf16[2,8,64,384]{3,2,1,0:T(8,128)(2,1)S(1)} %collective-permute-done.1), channel_id=1, source_target_pairs={{0,28},{4,0},{8,4},{12,8},{16,12},{20,16},{24,20},{28,24},{1,29},{... | collective-permute-start | bytes 2359304 | tf_op jit(solution)/shard_map/ppermute | solution.py:31
  77.2 1.9 %copy-start.2 = (bf16[2,8,64,384]{3,2,1,0:T(8,128)(2,1)}, bf16[2,8,64,384]{3,2,1,0:T(8,128)(2,1)S(1)}, u32[]{:S(2)}) copy-start(bf16[2,8,64,384]{3,2,1,0:T(8,128)(2,1)S(1)} %collective-permute-done.2) | copy-start | bytes 2359300
  77.2 18.3 %collective-permute-start.4 = (bf16[2,8,64,384]{3,2,1,0:T(8,128)(2,1)S(1)}, bf16[2,8,64,384]{3,2,1,0:T(8,128)(2,1)S(1)}, u32[]{:S(2)}, u32[]{:S(2)}) collective-permute-start(bf16[2,8,64,384]{3,2,1,0:T(8,128)(2,1)S(1)} %collective-permute-done.2), channel_id=1, source_target_pairs={{0,4},{4,8},{8,12},{12,16},{16,20},{20,24},{24,28},{28,0},{1,5},{5... | collective-permute-start | bytes 2359304 | tf_op jit(solution)/shard_map/ppermute | solution.py:30
  79.2 18.3 %copy-start.6 = (bf16[2,8,64,384]{3,2,1,0:T(8,128)(2,1)}, bf16[2,8,64,384]{3,2,1,0:T(8,128)(2,1)S(1)}, u32[]{:S(2)}) copy-start(bf16[2,8,64,384]{3,2,1,0:T(8,128)(2,1)S(1)} %collective-permute-done.3) | copy-start | bytes 2359300
  79.2 18.3 %collective-permute-start.5 = (bf16[2,8,64,384]{3,2,1,0:T(8,128)(2,1)S(1)}, bf16[2,8,64,384]{3,2,1,0:T(8,128)(2,1)S(1)}, u32[]{:S(2)}, u32[]{:S(2)}) collective-permute-start(bf16[2,8,64,384]{3,2,1,0:T(8,128)(2,1)S(1)} %collective-permute-done.3), channel_id=1, source_target_pairs={{0,28},{4,0},{8,4},{12,8},{16,12},{20,16},{24,20},{28,24},{1,29},{... | collective-permute-start | bytes 2359304 | tf_op jit(solution)/shard_map/ppermute | solution.py:31
  95.6 9.7 %collective-permute-start.6 = (bf16[1,8,64,384]{3,2,1,0:T(8,128)(2,1)S(1)}, bf16[1,8,64,384]{3,2,1,0:T(8,128)(2,1)S(1)}, u32[]{:S(2)}, u32[]{:S(2)}) collective-permute-start(bf16[1,8,64,384]{3,2,1,0:T(8,128)(2,1)S(1)} %slice.79), channel_id=1, source_target_pairs={{0,4},{4,8},{8,12},{12,16},{16,20},{20,24},{24,28},{28,0},{1,5},{5... | collective-permute-start | bytes 1179656 | tf_op jit(solution)/shard_map/ppermute | solution.py:35
  98.4 9.6 %collective-permute-start.7 = (bf16[1,8,64,384]{3,2,1,0:T(8,128)(2,1)}, bf16[1,8,64,384]{3,2,1,0:T(8,128)(2,1)}, u32[]{:S(2)}, u32[]{:S(2)}) collective-permute-start(bf16[1,8,64,384]{3,2,1,0:T(8,128)(2,1)} %slice.80), channel_id=1, source_target_pairs={{0,28},{4,0},{8,4},{12,8},{16,12},{20,16},{24,20},{28,24},{1,29},{... | collective-permute-start | bytes 1179656 | tf_op jit(solution)/shard_map/ppermute | solution.py:35
  113.6 1.1 copy-start.7
  113.7 1.7 %copy-start.5 = (bf16[2,8,64,384]{3,2,1,0:T(8,128)(2,1)S(1)}, bf16[2,8,64,384]{3,2,1,0:T(8,128)(2,1)}, u32[]{:S(2)}) copy-start(bf16[2,8,64,384]{3,2,1,0:T(8,128)(2,1)} %copy-done.4) | copy-start | bytes 2359300
  114.3 2.5 %copy-start.1 = (bf16[2,8,64,384]{3,2,1,0:T(8,128)(2,1)S(1)}, bf16[2,8,64,384]{3,2,1,0:T(8,128)(2,1)}, u32[]{:S(2)}) copy-start(bf16[2,8,64,384]{3,2,1,0:T(8,128)(2,1)} %copy-done) | copy-start | bytes 2359300
  115.4 2.0 %copy-start.3 = (bf16[2,8,64,384]{3,2,1,0:T(8,128)(2,1)S(1)}, bf16[2,8,64,384]{3,2,1,0:T(8,128)(2,1)}, u32[]{:S(2)}) copy-start(bf16[2,8,64,384]{3,2,1,0:T(8,128)(2,1)} %copy-done.2) | copy-start | bytes 2359300
  117.8 19.1 %copy-start.8 = (bf16[96,128]{1,0:T(8,128)(2,1)S(1)}, bf16[96,128]{1,0:T(8,128)(2,1)}, u32[]{:S(2)}) copy-start(bf16[96,128]{1,0:T(8,128)(2,1)} %param.7) | copy-start | bytes 73732
  117.8 19.1 %copy-start.9 = (f32[128]{0:T(128)S(1)}, f32[128]{0:T(128)}, u32[]{:S(2)}) copy-start(f32[128]{0:T(128)} %param.9) | copy-start | bytes 1540
  117.9 19.1 %copy-start.10 = (f32[96]{0:T(128)S(1)}, f32[96]{0:T(128)}, u32[]{:S(2)}) copy-start(f32[96]{0:T(128)} %param.8) | copy-start | bytes 1156
Sparse Core Ops, SparseCore 0:
  17.0 64.8 all-gather.2

commit v2 on v1

v2 whole, which is shorter than its diff:
```python
import jax
import jax.numpy as jnp
from jax import lax
from jax.experimental import pallas as pl
from jax.experimental.pallas import tpu as pltpu
from jax.sharding import Mesh, PartitionSpec as P

UP = [(i, (i + 1) % 8) for i in range(8)]
DOWN = [(i, (i - 1) % 8) for i in range(8)]
SWAP = [(0, 1), (1, 0)]
VMEM = pl.BlockSpec(memory_space=pltpu.VMEM)
HBM = pl.BlockSpec(memory_space=pltpu.HBM)
SMEM = pl.BlockSpec(memory_space=pltpu.SMEM)
FLOAT = jnp.float32


def piece(amp_ref, chunk, block):
    y = chunk // 2
    rows = pl.ds(pl.multiple_of((chunk % 2) * 64, 64), 64)
    amp = jnp.concatenate(
        [amp_ref[y, n, :, rows, :].reshape(512, 128) for n in range(2)], axis=1
    )
    return lax.dot_general(
        amp, block.reshape(512, 384), (((0,), (0,)), ((), ())), preferred_element_type=FLOAT
    )


def early_kernel(place, *refs):
    amps, blocks, (amp, out, held, sems) = refs[:8], refs[8:15], refs[15:]
    x, y, z = place[0], place[1], place[2]
    copies = [
        pltpu.make_async_copy(ref, amp.at[lax.rem(y + j, 8)], sems.at[j])
        for j, ref in enumerate(amps)
    ] + [
        pltpu.make_async_copy(ref, held.at[j], sems.at[8 + j]) for j, ref in enumerate(blocks)
    ]
    for copy in copies:
        copy.start()
    for copy in copies[:8]:
        copy.wait()
    total = None
    for j, shift in enumerate((0, 1, 2, 3, -1, -2, -3)):
        copies[8 + j].wait()
        source = lax.rem(z + shift + 8, 8)
        for half in range(2):
            part = piece(amp, lax.rem(x + half, 2) * 8 + source, held[j, half])
            total = part if total is None else total + part
    out[...] = total


def late_kernel(place, early, amp, last_own, last_other, out):
    x, z = place[0], place[2]
    source = lax.rem(z + 4, 8)
    total = early[...]
    for half, ref in enumerate((last_own, last_other)):
        total = total + piece(amp, lax.rem(x + half, 2) * 8 + source, ref[...])
    for n in range(2):
        out[lax.rem(x + n, 2)] = total[n * 128 : (n + 1) * 128].T


def local(integrals, amplitudes, coulomb, row_gap, col_gap):
    x, y, z = (lax.axis_index(a) for a in ("xl", "y", "z"))
    place = jnp.stack([x, y, z])

    def swap(block):
        keep = lax.dynamic_slice_in_dim(block, x * 8, 8, 0)
        give = lax.dynamic_slice_in_dim(block, (1 - x) * 8, 8, 0)
        return jnp.stack([keep, lax.ppermute(give, "xl", SWAP)])

    def ring(own, axis):
        above, below = [own], [own]
        for _ in range(3):
            below.append(lax.ppermute(below[-1], axis, UP))
            above.append(lax.ppermute(above[-1], axis, DOWN))
        far = lax.ppermute(below[3][0], axis, UP), lax.ppermute(above[3][1], axis, DOWN)
        return above, below, far

    above, below, far = ring(swap(integrals), "z")
    a_above, a_below, a_far = ring(swap(amplitudes), "y")
    amps = a_above + [jnp.stack(a_far)] + a_below[:0:-1]
    early, amp = pl.pallas_call(
        early_kernel,
        out_shape=(
            jax.ShapeDtypeStruct((8, 2, 8, 128, 128), jnp.bfloat16),
            jax.ShapeDtypeStruct((256, 384), FLOAT),
        ),
        in_specs=[SMEM] + [HBM] * 15,
        out_specs=(VMEM, VMEM),
        scratch_shapes=[
            pltpu.VMEM((7, 2, 8, 64, 384), jnp.bfloat16),
            pltpu.SemaphoreType.DMA((15,)),
        ],
        compiler_params=pltpu.CompilerParams(vmem_limit_bytes=24 << 20),
        cost_estimate=pl.CostEstimate(flops=1 << 30, bytes_accessed=16 << 20, transcendentals=0),
    )(place, *amps, *above, *below[1:])[::-1]
    shares = pl.pallas_call(
        late_kernel,
        out_shape=jax.ShapeDtypeStruct((2, 384, 128), FLOAT),
        in_specs=[SMEM] + [VMEM] * 4,
        out_specs=VMEM,
        compiler_params=pltpu.CompilerParams(vmem_limit_bytes=6 << 20),
    )(place, early, amp, *far)
    shares = lax.all_to_all(
        shares.reshape(8, 96, 128), ("xl", "xh", "core"), 0, 0, tiled=True
    )
    own = jnp.sum(shares, axis=0)
    gap_sum = row_gap[:, None] + col_gap[None, :]
    return (coulomb.astype(FLOAT) + own) / gap_sum


def solution(mesh):
    fine = Mesh(mesh.devices.reshape(8, 2, 8, 2, 2), ("y", "xl", "z", "xh", "core"))
    layer, col = ("xh", "core"), ("xl", "z")
    placed = (
        P(layer, col, "y"),
        P(layer, "y", col),
        P(("y",) + layer, col),
        P(("y",) + layer),
        P(col),
    )
    return jax.shard_map(
        local, mesh=fine, in_specs=placed, out_specs=P(("y",) + layer, col), check_vma=False
    )
```

time: 145 us -> 128 us (0.88)
  waiting for transfers between devices: 42.6 us -> 9.98 us
  starting transfers between devices: 36.2 us -> 67.6 us
  blocking collectives: 38.9 us -> 18 us
  local copies, waits for them, and re-layouts: 6.46 us -> 21.9 us
  between operations: 14.2 us -> 0.39 us
  Pallas kernels: 0 us -> 6.45 us
  matrix products: 5.31 us -> 0 us
    ppermute x8 -> x18, waiting for transfers between devices: 42.6 us -> 9.98 us  [the longest x6 6.13 us: ring(): below.append(lax.ppermute(below[-1], axis, UP))]
    ppermute x8 -> x18, starting transfers between devices: 36.2 us -> 67.6 us  [the longest x6 28.9 us: ring(): above.append(lax.ppermute(above[-1], axis, DOWN))]
    all_to_all x3 -> x1, blocking collectives: 38.9 us -> 18 us  [local(): lax.all_to_all(shares.reshape(8, 96, 128), ('xl', 'xh', 'core'), 0, 0, ti...]
    unnamed x23 -> x42, local copies, waits for them, and re-layouts: 0.22 us -> 16.5 us
    pallas_call x0 -> x2, Pallas kernels: none -> 6.45 us  [the longest x1 4.74 us: local(): pl.pallas_call(early_kernel, out_shape=(jax.ShapeDtypeStruct((8, 2, 8, 12...]
    dot_general x16 -> x0, matrix products: 5.31 us -> none  [times(): lax.dot_general(block, part[:, n], CONTRACT, preferred_element_type=jnp.f...]
    dynamic_slice x3 -> x0, local copies, waits for them, and re-layouts: 3.83 us -> none  [times(): lax.dynamic_slice(amps, (0, source // 2, 0, 0, source % 2, 0, 0), (2, 1,...]
    squeeze x0 -> x4, local copies, waits for them, and re-layouts: none -> 3.12 us  [the longest x2 1.56 us: ring(): above[3][1]]
  transfers between devices with their start and end apart: 9 -> 18, of which waited for: 5 -> 4; matrix products, arithmetic and copies ran while one was open for 1% -> 4% of each run, Pallas kernels for 0% -> 4%
where the time goes in v2:
time: 128 us; the launch traced here: 126 us
  starting transfers between devices  67.6 us (53%)
  local copies, waits for them, and re-layouts  21.9 us (17%)
  blocking collectives  18 us (14%)
  waiting for transfers between devices  9.98 us (8%)
  Pallas kernels  6.45 us (5%)
  other arithmetic  2.03 us (2%)
    ppermute x6, starting transfers between devices, ring(): above.append(lax.ppermute(above[-1], axis, DOWN))  28.9 us
    ppermute x6, starting transfers between devices, ring(): below.append(lax.ppermute(below[-1], axis, UP))  19.7 us
    all_to_all x1, blocking collectives, local(): lax.all_to_all(shares.reshape(8, 96, 128), ('xl', 'xh', 'core'), 0, 0, ti...  18 us
    unnamed x42, local copies, waits for them, and re-layouts  16.5 us
    ppermute x2, starting transfers between devices, ring(): lax.ppermute(above[3][1], axis, DOWN)  8.79 us
    ppermute x6, waiting for transfers between devices, ring(): below.append(lax.ppermute(below[-1], axis, UP))  6.13 us
    ppermute x2, starting transfers between devices, swap(): return jnp.stack([keep, lax.ppermute(give, 'xl', SWAP)])  5.87 us
    pallas_call x1, Pallas kernels, local(): pl.pallas_call(early_kernel, out_shape=(jax.ShapeDtypeStruct((8, 2, 8, 12...  4.74 us
  transfers between devices with their start and end apart: 18, of which 4 were waited for; matrix products, arithmetic and copies ran while one was open for 4% of the time, Pallas kernels for 4%

profile of v2, /device:TPU:1, one launch (start us, length us, event | category | flops | bytes accessed | tf_op | source)
XLA Modules:
  0.0 126.4 jit_solution(3301299249564697854)
XLA Ops:
  0.0 1.2 dynamic-slice_bitcast_fusion
  1.2 3.9 %collective-permute-start.9 = (bf16[8,64,384]{2,1,0:T(8,128)(2,1)S(1)}, bf16[8,64,384]{2,1,0:T(8,128)(2,1)S(1)}, u32[]{:S(2)}, u32[]{:S(2)}) collective-permute-start(bf16[8,64,384]{2,1,0:T(8,128)(2,1)S(1)} %get-tuple-element.10), channel_id=1, source_target_pairs={{0,32},{32,0},{1,33},{33,1},{2,34},{34,2},{3,35},{35,3},{4,36},{36... | collective-permute-start | bytes 1179656 | tf_op jit(solution)/shard_map/ppermute | solution.py:68
  5.2 1.1 dynamic-slice_bitcast_fusion.1
  6.2 1.9 %collective-permute-start = (bf16[8,128,128]{2,1,0:T(8,128)(2,1)S(1)}, bf16[8,128,128]{2,1,0:T(8,128)(2,1)S(1)}, u32[]{:S(2)}, u32[]{:S(2)}) collective-permute-start(bf16[8,128,128]{2,1,0:T(8,128)(2,1)S(1)} %get-tuple-element.12), channel_id=1, source_target_pairs={{0,32},{32,0},{1,33},{33,1},{2,34},{34,2},{3,35},{35,3},{4,36},{36... | collective-permute-start | bytes 786440 | tf_op jit(solution)/shard_map/ppermute | solution.py:68
  8.2 2.1 %collective-permute-done.9 = bf16[8,64,384]{2,1,0:T(8,128)(2,1)S(1)} collective-permute-done((bf16[8,64,384]{2,1,0:T(8,128)(2,1)S(1)}, bf16[8,64,384]{2,1,0:T(8,128)(2,1)S(1)}, u32[]{:S(2)}, u32[]{:S(2)}) %collective-permute-start.9) | collective-permute-done | bytes 393248 | tf_op jit(solution)/shard_map/ppermute | solution.py:68
  10.4 7.6 %collective-permute-start.13 = (bf16[2,8,64,384]{3,2,1,0:T(8,128)(2,1)S(1)}, bf16[2,8,64,384]{3,2,1,0:T(8,128)(2,1)S(1)}, u32[]{:S(2)}, u32[]{:S(2)}) collective-permute-start(bf16[2,8,64,384]{3,2,1,0:T(8,128)(2,1)S(1)} %pad_maximum_fusion.refs_8_), channel_id=1, source_target_pairs={{0,4},{4,8},{8,12},{12,16},{16,20},{20,24},{24,28},{28,0},{1,5},{5... | collective-permute-start | bytes 2359304 | tf_op jit(solution)/shard_map/ppermute | solution.py:73
  18.0 8.6 %collective-permute-start.10 = (bf16[2,8,64,384]{3,2,1,0:T(8,128)(2,1)S(1)}, bf16[2,8,64,384]{3,2,1,0:T(8,128)(2,1)S(1)}, u32[]{:S(2)}, u32[]{:S(2)}) collective-permute-start(bf16[2,8,64,384]{3,2,1,0:T(8,128)(2,1)S(1)} %pad_maximum_fusion.refs_8_), channel_id=1, source_target_pairs={{0,28},{4,0},{8,4},{12,8},{16,12},{20,16},{24,20},{28,24},{1,29},{... | collective-permute-start | bytes 2359304 | tf_op jit(solution)/shard_map/ppermute | solution.py:74
  26.7 3.2 %collective-permute-start.4 = (bf16[2,8,128,128]{3,2,1,0:T(8,128)(2,1)S(1)}, bf16[2,8,128,128]{3,2,1,0:T(8,128)(2,1)S(1)}, u32[]{:S(2)}, u32[]{:S(2)}) collective-permute-start(bf16[2,8,128,128]{3,2,1,0:T(8,128)(2,1)S(1)} %pad_maximum_fusion.1.refs_0_), channel_id=1, source_target_pairs={{0,64},{64,128},{128,192},{192,256},{256,320},{320,384},{384,448},... | collective-permute-start | bytes 1572872 | tf_op jit(solution)/shard_map/ppermute | solution.py:73
  29.9 3.8 %collective-permute-start.1 = (bf16[2,8,128,128]{3,2,1,0:T(8,128)(2,1)S(1)}, bf16[2,8,128,128]{3,2,1,0:T(8,128)(2,1)S(1)}, u32[]{:S(2)}, u32[]{:S(2)}) collective-permute-start(bf16[2,8,128,128]{3,2,1,0:T(8,128)(2,1)S(1)} %pad_maximum_fusion.1.refs_0_), channel_id=1, source_target_pairs={{0,448},{64,0},{128,64},{192,128},{256,192},{320,256},{384,320},{4... | collective-permute-start | bytes 1572872 | tf_op jit(solution)/shard_map/ppermute | solution.py:74
  33.7 6.1 %collective-permute-done.13.refs_12_ = bf16[2,8,64,384]{3,2,1,0:T(8,128)(2,1)S(1)} collective-permute-done((bf16[2,8,64,384]{3,2,1,0:T(8,128)(2,1)S(1)}, bf16[2,8,64,384]{3,2,1,0:T(8,128)(2,1)S(1)}, u32[]{:S(2)}, u32[]{:S(2)}) %collective-permute-start.13) | collective-permute-done | bytes 786464 | tf_op jit(solution)/shard_map/ppermute | solution.py:73
  39.8 1.9 %collective-permute-start.14 = (bf16[2,8,64,384]{3,2,1,0:T(8,128)(2,1)S(1)}, bf16[2,8,64,384]{3,2,1,0:T(8,128)(2,1)S(1)}, u32[]{:S(2)}, u32[]{:S(2)}) collective-permute-start(bf16[2,8,64,384]{3,2,1,0:T(8,128)(2,1)S(1)} %collective-permute-done.13.refs_12_), channel_id=1, source_target_pairs={{0,4},{4,8},{8,12},{12,16},{16,20},{20,24},{24,28},{28,0},{1,5},{5... | collective-permute-start | bytes 2359304 | tf_op jit(solution)/shard_map/ppermute | solution.py:73
  42.6 3.2 %collective-permute-start.5 = (bf16[2,8,128,128]{3,2,1,0:T(8,128)(2,1)S(1)}, bf16[2,8,128,128]{3,2,1,0:T(8,128)(2,1)S(1)}, u32[]{:S(2)}, u32[]{:S(2)}) collective-permute-start(bf16[2,8,128,128]{3,2,1,0:T(8,128)(2,1)S(1)} %collective-permute-done.4.refs_7_), channel_id=1, source_target_pairs={{0,64},{64,128},{128,192},{192,256},{256,320},{320,384},{384,448},... | collective-permute-start | bytes 1572872 | tf_op jit(solution)/shard_map/ppermute | solution.py:73
  46.6 4.6 %collective-permute-start.11 = (bf16[2,8,64,384]{3,2,1,0:T(8,128)(2,1)S(1)}, bf16[2,8,64,384]{3,2,1,0:T(8,128)(2,1)S(1)}, u32[]{:S(2)}, u32[]{:S(2)}) collective-permute-start(bf16[2,8,64,384]{3,2,1,0:T(8,128)(2,1)S(1)} %collective-permute-done.10.refs_9_), channel_id=1, source_target_pairs={{0,28},{4,0},{8,4},{12,8},{16,12},{20,16},{24,20},{28,24},{1,29},{... | collective-permute-start | bytes 2359304 | tf_op jit(solution)/shard_map/ppermute | solution.py:74
  52.1 3.8 %collective-permute-start.2 = (bf16[2,8,128,128]{3,2,1,0:T(8,128)(2,1)S(1)}, bf16[2,8,128,128]{3,2,1,0:T(8,128)(2,1)S(1)}, u32[]{:S(2)}, u32[]{:S(2)}) collective-permute-start(bf16[2,8,128,128]{3,2,1,0:T(8,128)(2,1)S(1)} %collective-permute-done.1.refs_1_), channel_id=1, source_target_pairs={{0,448},{64,0},{128,64},{192,128},{256,192},{320,256},{384,320},{4... | collective-permute-start | bytes 1572872 | tf_op jit(solution)/shard_map/ppermute | solution.py:74
  56.7 1.9 %collective-permute-start.6 = (bf16[2,8,128,128]{3,2,1,0:T(8,128)(2,1)S(1)}, bf16[2,8,128,128]{3,2,1,0:T(8,128)(2,1)S(1)}, u32[]{:S(2)}, u32[]{:S(2)}) collective-permute-start(bf16[2,8,128,128]{3,2,1,0:T(8,128)(2,1)S(1)} %collective-permute-done.5.refs_6_), channel_id=1, source_target_pairs={{0,64},{64,128},{128,192},{192,256},{256,320},{320,384},{384,448},... | collective-permute-start | bytes 1572872 | tf_op jit(solution)/shard_map/ppermute | solution.py:73
  59.4 1.9 %collective-permute-start.15 = (bf16[2,8,64,384]{3,2,1,0:T(8,128)(2,1)S(1)}, bf16[2,8,64,384]{3,2,1,0:T(8,128)(2,1)S(1)}, u32[]{:S(2)}, u32[]{:S(2)}) collective-permute-start(bf16[2,8,64,384]{3,2,1,0:T(8,128)(2,1)S(1)} %collective-permute-done.14.refs_13_), channel_id=1, source_target_pairs={{0,4},{4,8},{8,12},{12,16},{16,20},{20,24},{24,28},{28,0},{1,5},{5... | collective-permute-start | bytes 2359304 | tf_op jit(solution)/shard_map/ppermute | solution.py:73
  63.2 5.3 %collective-permute-start.3 = (bf16[2,8,128,128]{3,2,1,0:T(8,128)(2,1)S(1)}, bf16[2,8,128,128]{3,2,1,0:T(8,128)(2,1)S(1)}, u32[]{:S(2)}, u32[]{:S(2)}) collective-permute-start(bf16[2,8,128,128]{3,2,1,0:T(8,128)(2,1)S(1)} %collective-permute-done.2.refs_2_), channel_id=1, source_target_pairs={{0,448},{64,0},{128,64},{192,128},{256,192},{320,256},{384,320},{4... | collective-permute-start | bytes 1572872 | tf_op jit(solution)/shard_map/ppermute | solution.py:74
  69.3 2.8 %collective-permute-start.12 = (bf16[2,8,64,384]{3,2,1,0:T(8,128)(2,1)S(1)}, bf16[2,8,64,384]{3,2,1,0:T(8,128)(2,1)S(1)}, u32[]{:S(2)}, u32[]{:S(2)}) collective-permute-start(bf16[2,8,64,384]{3,2,1,0:T(8,128)(2,1)S(1)} %collective-permute-done.11.refs_10_), channel_id=1, source_target_pairs={{0,28},{4,0},{8,4},{12,8},{16,12},{20,16},{24,20},{28,24},{1,29},{... | collective-permute-start | bytes 2359304 | tf_op jit(solution)/shard_map/ppermute | solution.py:74
  73.8 1.9 %collective-permute-start.7 = (bf16[8,128,128]{2,1,0:T(8,128)(2,1)}, bf16[8,128,128]{2,1,0:T(8,128)(2,1)}, u32[]{:S(2)}, u32[]{:S(2)}) collective-permute-start(bf16[8,128,128]{2,1,0:T(8,128)(2,1)} %slice_bitcast_fusion.3), channel_id=1, source_target_pairs={{0,64},{64,128},{128,192},{192,256},{256,320},{320,384},{384,448},... | collective-permute-start | bytes 786440 | tf_op jit(solution)/shard_map/ppermute | solution.py:75
  76.7 4.6 %collective-permute-start.8 = (bf16[8,128,128]{2,1,0:T(8,128)(2,1)}, bf16[8,128,128]{2,1,0:T(8,128)(2,1)}, u32[]{:S(2)}, u32[]{:S(2)}) collective-permute-start(bf16[8,128,128]{2,1,0:T(8,128)(2,1)} %slice_bitcast_fusion.2), channel_id=1, source_target_pairs={{0,448},{64,0},{128,64},{192,128},{256,192},{320,256},{384,320},{4... | collective-permute-start | bytes 786440 | tf_op jit(solution)/shard_map/ppermute | solution.py:75
  82.0 2.4 %collective-permute-start.16 = (bf16[8,64,384]{2,1,0:T(8,128)(2,1)}, bf16[8,64,384]{2,1,0:T(8,128)(2,1)}, u32[]{:S(2)}, u32[]{:S(2)}) collective-permute-start(bf16[8,64,384]{2,1,0:T(8,128)(2,1)} %slice_bitcast_fusion.1), channel_id=1, source_target_pairs={{0,4},{4,8},{8,12},{12,16},{16,20},{20,24},{24,28},{28,0},{1,5},{5... | collective-permute-start | bytes 1179656 | tf_op jit(solution)/shard_map/ppermute | solution.py:75
  85.9 4.2 %collective-permute-start.17 = (bf16[8,64,384]{2,1,0:T(8,128)(2,1)}, bf16[8,64,384]{2,1,0:T(8,128)(2,1)}, u32[]{:S(2)}, u32[]{:S(2)}) collective-permute-start(bf16[8,64,384]{2,1,0:T(8,128)(2,1)} %slice_bitcast_fusion), channel_id=1, source_target_pairs={{0,28},{4,0},{8,4},{12,8},{16,12},{20,16},{24,20},{28,24},{1,29},{... | collective-permute-start | bytes 1179656 | tf_op jit(solution)/shard_map/ppermute | solution.py:75
  90.3 1.1 pad_maximum_fusion.2.refs_4_
  92.4 1.1 copy-done.3
  93.5 1.1 copy-done.5
  94.7 1.1 copy-done.7
  95.8 1.1 copy-done.9
  96.9 1.0 copy-done.11
  99.0 1.0 copy-done.15
  101.1 4.7 %shard_map.55 = (bf16[8,2,8,128,128]{4,3,2,1,0:T(8,128)(2,1)S(1)}, f32[256,384]{1,0:T(8,128)S(1)}) custom-call(s32[3]{0:T(128)S(1)} %pad_add_fusion.place, bf16[2,8,128,128]{3,2,1,0:T(8,128)(2,1)S(1)} %pad_maximum_fusion.1.refs_0_, bf16[2,8,128,128]{3,2,1,0:T(8,128)(2,1)S(1)} %copy-done.13, bf16[2,8,128,128]{3,2,1,0:T(8,128)(2,1)S(1)} %copy-done.17, ...), custom_call_target="tpu_custom_call" | custom-call | flops 1073741824 | bytes 16777216 | tf_op jit(solution)/shard_map/pallas_call | solution.py:81
  105.9 1.7 %shard_map.56 = f32[2,384,128]{2,1,0:T(8,128)S(1)} custom-call(s32[3]{0:T(128)S(1)} %pad_add_fusion.place, f32[256,384]{1,0:T(8,128)S(1)} %get-tuple-element.7.early, bf16[8,2,8,128,128]{4,3,2,1,0:T(8,128)(2,1)S(1)} %get-tuple-element.8.amp, bf16[8,64,384]{2,1,0:T(8,128)(2,1)} %collective-permute-done.16.last_own, ...), custom_call_target="tpu_custom_call" | custom-call | tf_op jit(solution)/shard_map/pallas_call | solution.py:96
  107.6 18.0 %all_to_all.5 = f32[8,96,128]{2,1,0:T(8,128)S(1)} all-to-all(f32[8,96,128]{2,1,0:T(8,128)S(1)} %bitcast.20), channel_id=1, replica_groups=mesh['y'=8,'xl'=2,'z'=8,'xh'=2,'core'=2] {'xl','xh','core'}, dimensions={0} | all-to-all | bytes 786432 | tf_op jit(solution)/shard_map/all_to_all | solution.py:103
  (61 shorter events, 15.7 us)
Async XLA Ops:
  1.2 9.1 %collective-permute-start.9 = (bf16[8,64,384]{2,1,0:T(8,128)(2,1)S(1)}, bf16[8,64,384]{2,1,0:T(8,128)(2,1)S(1)}, u32[]{:S(2)}, u32[]{:S(2)}) collective-permute-start(bf16[8,64,384]{2,1,0:T(8,128)(2,1)S(1)} %get-tuple-element.10), channel_id=1, source_target_pairs={{0,32},{32,0},{1,33},{33,1},{2,34},{34,2},{3,35},{35,3},{4,36},{36... | collective-permute-start | bytes 1179656 | tf_op jit(solution)/shard_map/ppermute | solution.py:68
  6.2 20.4 %collective-permute-start = (bf16[8,128,128]{2,1,0:T(8,128)(2,1)S(1)}, bf16[8,128,128]{2,1,0:T(8,128)(2,1)S(1)}, u32[]{:S(2)}, u32[]{:S(2)}) collective-permute-start(bf16[8,128,128]{2,1,0:T(8,128)(2,1)S(1)} %get-tuple-element.12), channel_id=1, source_target_pairs={{0,32},{32,0},{1,33},{33,1},{2,34},{34,2},{3,35},{35,3},{4,36},{36... | collective-permute-start | bytes 786440 | tf_op jit(solution)/shard_map/ppermute | solution.py:68
  10.4 29.4 %collective-permute-start.13 = (bf16[2,8,64,384]{3,2,1,0:T(8,128)(2,1)S(1)}, bf16[2,8,64,384]{3,2,1,0:T(8,128)(2,1)S(1)}, u32[]{:S(2)}, u32[]{:S(2)}) collective-permute-start(bf16[2,8,64,384]{3,2,1,0:T(8,128)(2,1)S(1)} %pad_maximum_fusion.refs_8_), channel_id=1, source_target_pairs={{0,4},{4,8},{8,12},{12,16},{16,20},{20,24},{24,28},{28,0},{1,5},{5... | collective-permute-start | bytes 2359304 | tf_op jit(solution)/shard_map/ppermute | solution.py:73
  18.0 28.6 %collective-permute-start.10 = (bf16[2,8,64,384]{3,2,1,0:T(8,128)(2,1)S(1)}, bf16[2,8,64,384]{3,2,1,0:T(8,128)(2,1)S(1)}, u32[]{:S(2)}, u32[]{:S(2)}) collective-permute-start(bf16[2,8,64,384]{3,2,1,0:T(8,128)(2,1)S(1)} %pad_maximum_fusion.refs_8_), channel_id=1, source_target_pairs={{0,28},{4,0},{8,4},{12,8},{16,12},{20,16},{24,20},{28,24},{1,29},{... | collective-permute-start | bytes 2359304 | tf_op jit(solution)/shard_map/ppermute | solution.py:74
  26.7 16.0 %collective-permute-start.4 = (bf16[2,8,128,128]{3,2,1,0:T(8,128)(2,1)S(1)}, bf16[2,8,128,128]{3,2,1,0:T(8,128)(2,1)S(1)}, u32[]{:S(2)}, u32[]{:S(2)}) collective-permute-start(bf16[2,8,128,128]{3,2,1,0:T(8,128)(2,1)S(1)} %pad_maximum_fusion.1.refs_0_), channel_id=1, source_target_pairs={{0,64},{64,128},{128,192},{192,256},{256,320},{320,384},{384,448},... | collective-permute-start | bytes 1572872 | tf_op jit(solution)/shard_map/ppermute | solution.py:73
  29.9 22.2 %collective-permute-start.1 = (bf16[2,8,128,128]{3,2,1,0:T(8,128)(2,1)S(1)}, bf16[2,8,128,128]{3,2,1,0:T(8,128)(2,1)S(1)}, u32[]{:S(2)}, u32[]{:S(2)}) collective-permute-start(bf16[2,8,128,128]{3,2,1,0:T(8,128)(2,1)S(1)} %pad_maximum_fusion.1.refs_0_), channel_id=1, source_target_pairs={{0,448},{64,0},{128,64},{192,128},{256,192},{320,256},{384,320},{4... | collective-permute-start | bytes 1572872 | tf_op jit(solution)/shard_map/ppermute | solution.py:74
  39.8 19.6 %collective-permute-start.14 = (bf16[2,8,64,384]{3,2,1,0:T(8,128)(2,1)S(1)}, bf16[2,8,64,384]{3,2,1,0:T(8,128)(2,1)S(1)}, u32[]{:S(2)}, u32[]{:S(2)}) collective-permute-start(bf16[2,8,64,384]{3,2,1,0:T(8,128)(2,1)S(1)} %collective-permute-done.13.refs_12_), channel_id=1, source_target_pairs={{0,4},{4,8},{8,12},{12,16},{16,20},{20,24},{24,28},{28,0},{1,5},{5... | collective-permute-start | bytes 2359304 | tf_op jit(solution)/shard_map/ppermute | solution.py:73
  42.6 14.1 %collective-permute-start.5 = (bf16[2,8,128,128]{3,2,1,0:T(8,128)(2,1)S(1)}, bf16[2,8,128,128]{3,2,1,0:T(8,128)(2,1)S(1)}, u32[]{:S(2)}, u32[]{:S(2)}) collective-permute-start(bf16[2,8,128,128]{3,2,1,0:T(8,128)(2,1)S(1)} %collective-permute-done.4.refs_7_), channel_id=1, source_target_pairs={{0,64},{64,128},{128,192},{192,256},{256,320},{320,384},{384,448},... | collective-permute-start | bytes 1572872 | tf_op jit(solution)/shard_map/ppermute | solution.py:73
  46.6 22.7 %collective-permute-start.11 = (bf16[2,8,64,384]{3,2,1,0:T(8,128)(2,1)S(1)}, bf16[2,8,64,384]{3,2,1,0:T(8,128)(2,1)S(1)}, u32[]{:S(2)}, u32[]{:S(2)}) collective-permute-start(bf16[2,8,64,384]{3,2,1,0:T(8,128)(2,1)S(1)} %collective-permute-done.10.refs_9_), channel_id=1, source_target_pairs={{0,28},{4,0},{8,4},{12,8},{16,12},{20,16},{24,20},{28,24},{1,29},{... | collective-permute-start | bytes 2359304 | tf_op jit(solution)/shard_map/ppermute | solution.py:74
  51.2 0.9 copy-start.4
  52.1 11.1 %collective-permute-start.2 = (bf16[2,8,128,128]{3,2,1,0:T(8,128)(2,1)S(1)}, bf16[2,8,128,128]{3,2,1,0:T(8,128)(2,1)S(1)}, u32[]{:S(2)}, u32[]{:S(2)}) collective-permute-start(bf16[2,8,128,128]{3,2,1,0:T(8,128)(2,1)S(1)} %collective-permute-done.1.refs_1_), channel_id=1, source_target_pairs={{0,448},{64,0},{128,64},{192,128},{256,192},{320,256},{384,320},{4... | collective-permute-start | bytes 1572872 | tf_op jit(solution)/shard_map/ppermute | solution.py:74
  56.7 16.4 %collective-permute-start.6 = (bf16[2,8,128,128]{3,2,1,0:T(8,128)(2,1)S(1)}, bf16[2,8,128,128]{3,2,1,0:T(8,128)(2,1)S(1)}, u32[]{:S(2)}, u32[]{:S(2)}) collective-permute-start(bf16[2,8,128,128]{3,2,1,0:T(8,128)(2,1)S(1)} %collective-permute-done.5.refs_6_), channel_id=1, source_target_pairs={{0,64},{64,128},{128,192},{192,256},{256,320},{320,384},{384,448},... | collective-permute-start | bytes 1572872 | tf_op jit(solution)/shard_map/ppermute | solution.py:73
  59.4 21.8 %collective-permute-start.15 = (bf16[2,8,64,384]{3,2,1,0:T(8,128)(2,1)S(1)}, bf16[2,8,64,384]{3,2,1,0:T(8,128)(2,1)S(1)}, u32[]{:S(2)}, u32[]{:S(2)}) collective-permute-start(bf16[2,8,64,384]{3,2,1,0:T(8,128)(2,1)S(1)} %collective-permute-done.14.refs_13_), channel_id=1, source_target_pairs={{0,4},{4,8},{8,12},{12,16},{16,20},{20,24},{24,28},{28,0},{1,5},{5... | collective-permute-start | bytes 2359304 | tf_op jit(solution)/shard_map/ppermute | solution.py:73
  63.2 12.5 %collective-permute-start.3 = (bf16[2,8,128,128]{3,2,1,0:T(8,128)(2,1)S(1)}, bf16[2,8,128,128]{3,2,1,0:T(8,128)(2,1)S(1)}, u32[]{:S(2)}, u32[]{:S(2)}) collective-permute-start(bf16[2,8,128,128]{3,2,1,0:T(8,128)(2,1)S(1)} %collective-permute-done.2.refs_2_), channel_id=1, source_target_pairs={{0,448},{64,0},{128,64},{192,128},{256,192},{320,256},{384,320},{4... | collective-permute-start | bytes 1572872 | tf_op jit(solution)/shard_map/ppermute | solution.py:74
  69.3 15.8 %collective-permute-start.12 = (bf16[2,8,64,384]{3,2,1,0:T(8,128)(2,1)S(1)}, bf16[2,8,64,384]{3,2,1,0:T(8,128)(2,1)S(1)}, u32[]{:S(2)}, u32[]{:S(2)}) collective-permute-start(bf16[2,8,64,384]{3,2,1,0:T(8,128)(2,1)S(1)} %collective-permute-done.11.refs_10_), channel_id=1, source_target_pairs={{0,28},{4,0},{8,4},{12,8},{16,12},{20,16},{24,20},{28,24},{1,29},{... | collective-permute-start | bytes 2359304 | tf_op jit(solution)/shard_map/ppermute | solution.py:74
  73.8 16.4 %collective-permute-start.7 = (bf16[8,128,128]{2,1,0:T(8,128)(2,1)}, bf16[8,128,128]{2,1,0:T(8,128)(2,1)}, u32[]{:S(2)}, u32[]{:S(2)}) collective-permute-start(bf16[8,128,128]{2,1,0:T(8,128)(2,1)} %slice_bitcast_fusion.3), channel_id=1, source_target_pairs={{0,64},{64,128},{128,192},{192,256},{256,320},{320,384},{384,448},... | collective-permute-start | bytes 786440 | tf_op jit(solution)/shard_map/ppermute | solution.py:75
  75.8 0.9 copy-start
  76.7 13.6 %collective-permute-start.8 = (bf16[8,128,128]{2,1,0:T(8,128)(2,1)}, bf16[8,128,128]{2,1,0:T(8,128)(2,1)}, u32[]{:S(2)}, u32[]{:S(2)}) collective-permute-start(bf16[8,128,128]{2,1,0:T(8,128)(2,1)} %slice_bitcast_fusion.2), channel_id=1, source_target_pairs={{0,448},{64,0},{128,64},{192,128},{256,192},{320,256},{384,320},{4... | collective-permute-start | bytes 786440 | tf_op jit(solution)/shard_map/ppermute | solution.py:75
  82.0 23.9 %collective-permute-start.16 = (bf16[8,64,384]{2,1,0:T(8,128)(2,1)}, bf16[8,64,384]{2,1,0:T(8,128)(2,1)}, u32[]{:S(2)}, u32[]{:S(2)}) collective-permute-start(bf16[8,64,384]{2,1,0:T(8,128)(2,1)} %slice_bitcast_fusion.1), channel_id=1, source_target_pairs={{0,4},{4,8},{8,12},{12,16},{16,20},{20,24},{24,28},{28,0},{1,5},{5... | collective-permute-start | bytes 1179656 | tf_op jit(solution)/shard_map/ppermute | solution.py:75
  85.9 20.0 %collective-permute-start.17 = (bf16[8,64,384]{2,1,0:T(8,128)(2,1)}, bf16[8,64,384]{2,1,0:T(8,128)(2,1)}, u32[]{:S(2)}, u32[]{:S(2)}) collective-permute-start(bf16[8,64,384]{2,1,0:T(8,128)(2,1)} %slice_bitcast_fusion), channel_id=1, source_target_pairs={{0,28},{4,0},{8,4},{12,8},{16,12},{20,16},{24,20},{28,24},{1,29},{... | collective-permute-start | bytes 1179656 | tf_op jit(solution)/shard_map/ppermute | solution.py:75
  91.4 1.0 copy-start.1
  92.4 1.1 copy-start.3
  93.5 1.1 copy-start.5
  94.7 1.1 copy-start.7
  95.8 1.1 copy-start.9
  96.9 1.0 copy-start.11
  98.0 1.0 copy-start.13
  99.0 1.0 copy-start.15
  100.1 1.0 copy-start.17
  105.8 19.8 %copy-start.18 = (bf16[96,128]{1,0:T(8,128)(2,1)S(1)}, bf16[96,128]{1,0:T(8,128)(2,1)}, u32[]{:S(2)}) copy-start(bf16[96,128]{1,0:T(8,128)(2,1)} %param.7) | copy-start | bytes 73732
  105.9 19.8 %copy-start.19 = (f32[128]{0:T(128)S(1)}, f32[128]{0:T(128)}, u32[]{:S(2)}) copy-start(f32[128]{0:T(128)} %param.9) | copy-start | bytes 1540
  105.9 19.8 %copy-start.20 = (f32[96]{0:T(128)S(1)}, f32[96]{0:T(128)}, u32[]{:S(2)}) copy-start(f32[96]{0:T(128)} %param.8) | copy-start | bytes 1156
  (7 other events, 5.8 us)

commit v3 on v2

v3 whole, which is shorter than its diff:
```python
import jax
import jax.numpy as jnp
from jax import lax
from jax.experimental import pallas as pl
from jax.experimental.pallas import tpu as pltpu
from jax.sharding import Mesh, PartitionSpec as P

FORTH = [(2 * i + c, 2 * ((i + 1 - 2 * c) % 8) + c) for i in range(8) for c in range(2)]
BACK = [(j, i) for i, j in FORTH]
SWAP = [(0, 1), (1, 0)]
VMEM = pl.BlockSpec(memory_space=pltpu.VMEM)
ANY = pl.BlockSpec(memory_space=pl.ANY)
SMEM = pl.BlockSpec(memory_space=pltpu.SMEM)
FLOAT = jnp.float32


def piece(amp_ref, chunk, block):
    y = chunk // 2
    rows = pl.ds(pl.multiple_of((chunk % 2) * 64, 64), 64)
    amp = jnp.concatenate(
        [amp_ref[y, n, :, rows, :].reshape(512, 128) for n in range(2)], axis=1
    )
    return lax.dot_general(
        amp, block.reshape(512, 384), (((0,), (0,)), ((), ())), preferred_element_type=FLOAT
    )


def early_kernel(place, *refs):
    amps, blocks, (amp, out, held, sems) = refs[:8], refs[8:15], refs[15:]
    x, y, z, way = place[0], place[1], place[2], place[3]
    copies = [
        pltpu.make_async_copy(ref, amp.at[lax.rem(y + way * shift + 8, 8)], sems.at[j])
        for j, (ref, shift) in enumerate(zip(amps, (0, -1, -2, -3, -4, 1, 2, 3)))
    ] + [
        pltpu.make_async_copy(ref, held.at[j], sems.at[8 + j]) for j, ref in enumerate(blocks)
    ]
    for copy in copies:
        copy.start()
    for copy in copies[:8]:
        copy.wait()
    total = None
    for j, shift in enumerate((0, -1, -2, -3, 1, 2, 3)):
        copies[8 + j].wait()
        source = lax.rem(z + way * shift + 8, 8)
        for half in range(2):
            part = piece(amp, lax.rem(x + half, 2) * 8 + source, held[j, half])
            total = part if total is None else total + part
    out[...] = total


def late_kernel(place, early, amp, last, out):
    x, z = place[0], place[2]
    source = lax.rem(z + 4, 8)
    total = early[...]
    for half in range(2):
        total = total + piece(amp, lax.rem(x + half, 2) * 8 + source, last[half])
    for n in range(2):
        out[lax.rem(x + n, 2)] = total[n * 128 : (n + 1) * 128].T


def local(integrals, amplitudes, coulomb, row_gap, col_gap):
    place = [lax.axis_index(a) for a in ("xl", "y", "z")] + [1 - 2 * lax.axis_index("core")]
    place = lax.optimization_barrier(jnp.stack(place))
    x = place[0]

    def swap(block):
        keep = lax.dynamic_slice_in_dim(block, x * 8, 8, 0)
        give = lax.dynamic_slice_in_dim(block, (1 - x) * 8, 8, 0)
        return jnp.stack([keep, lax.ppermute(give, "xl", SWAP)])

    def ring(own, axis):
        forth, back = [own], [own]
        for _ in range(3):
            forth.append(lax.ppermute(forth[-1], (axis, "core"), FORTH))
            back.append(lax.ppermute(back[-1], (axis, "core"), BACK))
        return forth + [lax.ppermute(forth[3], (axis, "core"), FORTH)] + back[1:]

    blocks = ring(swap(integrals), "z")
    amps = ring(swap(amplitudes), "y")
    early, amp = pl.pallas_call(
        early_kernel,
        out_shape=(
            jax.ShapeDtypeStruct((8, 2, 8, 128, 128), jnp.bfloat16),
            jax.ShapeDtypeStruct((256, 384), FLOAT),
        ),
        in_specs=[SMEM] + [ANY] * 15,
        out_specs=(VMEM, VMEM),
        scratch_shapes=[
            pltpu.VMEM((7, 2, 8, 64, 384), jnp.bfloat16),
            pltpu.SemaphoreType.DMA((15,)),
        ],
        compiler_params=pltpu.CompilerParams(vmem_limit_bytes=24 << 20),
        cost_estimate=pl.CostEstimate(flops=1 << 30, bytes_accessed=16 << 20, transcendentals=0),
    )(place, *amps, *blocks[:4], *blocks[5:])[::-1]
    shares = pl.pallas_call(
        late_kernel,
        out_shape=jax.ShapeDtypeStruct((2, 384, 128), FLOAT),
        in_specs=[SMEM] + [VMEM] * 3,
        out_specs=VMEM,
        compiler_params=pltpu.CompilerParams(vmem_limit_bytes=6 << 20),
    )(place, early, amp, blocks[4])
    shares = lax.all_to_all(
        shares.reshape(8, 96, 128), ("xl", "xh", "core"), 0, 0, tiled=True
    )
    own = jnp.sum(shares, axis=0)
    gap_sum = row_gap[:, None] + col_gap[None, :]
    return (coulomb.astype(FLOAT) + own) / gap_sum


def solution(mesh):
    fine = Mesh(mesh.devices.reshape(8, 2, 8, 2, 2), ("y", "xl", "z", "xh", "core"))
    layer, col = ("xh", "core"), ("xl", "z")
    placed = (
        P(layer, col, "y"),
        P(layer, "y", col),
        P(("y",) + layer, col),
        P(("y",) + layer),
        P(col),
    )
    return jax.shard_map(
        local, mesh=fine, in_specs=placed, out_specs=P(("y",) + layer, col), check_vma=False
    )
```

time: 128 us -> 126 us (0.984)
  waiting for transfers between devices: 9.98 us -> 31.7 us
  local copies, waits for them, and re-layouts: 21.9 us -> 2.3 us
  starting transfers between devices: 67.6 us -> 66.3 us
    ppermute x16 -> x14, waiting for transfers between devices: 7.84 us -> 26.5 us  [the longest x6 16.3 us: ring(): forth.append(lax.ppermute(forth[-1], (axis, 'core'), FORTH))]
    unnamed x42 -> x6, local copies, waits for them, and re-layouts: 16.5 us -> 0.02 us
    squeeze x4 -> x0, local copies, waits for them, and re-layouts: 3.12 us -> none  [the longest x2 1.56 us: ring(): above[3][1]]
    ppermute x2, waiting for transfers between devices: 2.14 us -> 5.15 us  [swap(): return jnp.stack([keep, lax.ppermute(give, 'xl', SWAP)])]
    ppermute x16 -> x14, starting transfers between devices: 61.7 us -> 59.2 us  [the longest x6 38.8 us: ring(): forth.append(lax.ppermute(forth[-1], (axis, 'core'), FORTH))]
  transfers between devices with their start and end apart: 18 -> 16, of which waited for: 4 -> 7; matrix products, arithmetic and copies ran while one was open for 4% -> 1% of each run, Pallas kernels for 4% -> 4%
where the time goes in v3:
time: 126 us; the launch traced here: 125 us
  starting transfers between devices  66.3 us (53%)
  waiting for transfers between devices  31.7 us (25%)
  blocking collectives  17.4 us (14%)
  Pallas kernels  5.88 us (5%)
  local copies, waits for them, and re-layouts  2.3 us (2%)
    ppermute x6, starting transfers between devices, ring(): forth.append(lax.ppermute(forth[-1], (axis, 'core'), FORTH))  38.8 us
    all_to_all x1, blocking collectives, local(): lax.all_to_all(shares.reshape(8, 96, 128), ('xl', 'xh', 'core'), 0, 0, ti...  17.4 us
    ppermute x6, waiting for transfers between devices, ring(): forth.append(lax.ppermute(forth[-1], (axis, 'core'), FORTH))  16.3 us
    ppermute x6, starting transfers between devices, ring(): back.append(lax.ppermute(back[-1], (axis, 'core'), BACK))  11.5 us
    ppermute x2, starting transfers between devices, ring(): return forth + [lax.ppermute(forth[3], (axis, 'core'), FORTH)] + back[1:]  8.85 us
    ppermute x2, starting transfers between devices, swap(): return jnp.stack([keep, lax.ppermute(give, 'xl', SWAP)])  7.07 us
    ppermute x6, waiting for transfers between devices, ring(): back.append(lax.ppermute(back[-1], (axis, 'core'), BACK))  5.82 us
    ppermute x2, waiting for transfers between devices, swap(): return jnp.stack([keep, lax.ppermute(give, 'xl', SWAP)])  5.15 us
  transfers between devices with their start and end apart: 16, of which 7 were waited for; matrix products, arithmetic and copies ran while one was open for 1% of the time, Pallas kernels for 4%

profile of v3, /device:TPU:1, one launch (start us, length us, event | category | flops | bytes accessed | tf_op | source)
XLA Modules:
  0.0 124.9 jit_solution(5134371200875069311)
XLA Ops:
  0.0 0.1 pad_add_fusion.place
  0.2 1.2 dynamic-slice_bitcast_fusion
  1.4 3.9 %collective-permute-start.8 = (bf16[8,64,384]{2,1,0:T(8,128)(2,1)S(1)}, bf16[8,64,384]{2,1,0:T(8,128)(2,1)S(1)}, u32[]{:S(2)}, u32[]{:S(2)}) collective-permute-start(bf16[8,64,384]{2,1,0:T(8,128)(2,1)S(1)} %get-tuple-element.10), channel_id=1, source_target_pairs={{0,32},{32,0},{1,33},{33,1},{2,34},{34,2},{3,35},{35,3},{4,36},{36... | collective-permute-start | bytes 1179656 | tf_op jit(solution)/shard_map/ppermute | solution.py:69
  5.3 5.2 %collective-permute-done.8 = bf16[8,64,384]{2,1,0:T(8,128)(2,1)S(1)} collective-permute-done((bf16[8,64,384]{2,1,0:T(8,128)(2,1)S(1)}, bf16[8,64,384]{2,1,0:T(8,128)(2,1)S(1)}, u32[]{:S(2)}, u32[]{:S(2)}) %collective-permute-start.8) | collective-permute-done | bytes 393248 | tf_op jit(solution)/shard_map/ppermute | solution.py:69
  10.5 0.1 pad_maximum_fusion.refs_8_
  10.6 14.3 %collective-permute-start.9 = (bf16[2,8,64,384]{3,2,1,0:T(8,128)(2,1)S(1)}, bf16[2,8,64,384]{3,2,1,0:T(8,128)(2,1)S(1)}, u32[]{:S(2)}, u32[]{:S(2)}) collective-permute-start(bf16[2,8,64,384]{3,2,1,0:T(8,128)(2,1)S(1)} %pad_maximum_fusion.refs_8_), channel_id=1, source_target_pairs={{0,4},{1,29},{4,8},{5,1},{8,12},{9,5},{12,16},{13,9},{16,20},{17,1... | collective-permute-start | bytes 2359304 | tf_op jit(solution)/shard_map/ppermute | solution.py:74
  24.9 1.1 dynamic-slice_bitcast_fusion.1
  25.9 3.1 %collective-permute-start = (bf16[8,128,128]{2,1,0:T(8,128)(2,1)S(1)}, bf16[8,128,128]{2,1,0:T(8,128)(2,1)S(1)}, u32[]{:S(2)}, u32[]{:S(2)}) collective-permute-start(bf16[8,128,128]{2,1,0:T(8,128)(2,1)S(1)} %get-tuple-element.12), channel_id=1, source_target_pairs={{0,32},{32,0},{1,33},{33,1},{2,34},{34,2},{3,35},{35,3},{4,36},{36... | collective-permute-start | bytes 786440 | tf_op jit(solution)/shard_map/ppermute | solution.py:69
  29.1 1.9 %collective-permute-start.12 = (bf16[2,8,64,384]{3,2,1,0:T(8,128)(2,1)S(1)}, bf16[2,8,64,384]{3,2,1,0:T(8,128)(2,1)S(1)}, u32[]{:S(2)}, u32[]{:S(2)}) collective-permute-start(bf16[2,8,64,384]{3,2,1,0:T(8,128)(2,1)S(1)} %pad_maximum_fusion.refs_8_), channel_id=1, source_target_pairs={{4,0},{29,1},{8,4},{1,5},{12,8},{5,9},{16,12},{9,13},{20,16},{13,1... | collective-permute-start | bytes 2359304 | tf_op jit(solution)/shard_map/ppermute | solution.py:75
  31.0 2.8 %collective-permute-done.9.refs_9_ = bf16[2,8,64,384]{3,2,1,0:T(8,128)(2,1)S(1)} collective-permute-done((bf16[2,8,64,384]{3,2,1,0:T(8,128)(2,1)S(1)}, bf16[2,8,64,384]{3,2,1,0:T(8,128)(2,1)S(1)}, u32[]{:S(2)}, u32[]{:S(2)}) %collective-permute-start.9) | collective-permute-done | bytes 786464 | tf_op jit(solution)/shard_map/ppermute | solution.py:74
  33.8 5.0 %collective-permute-start.10 = (bf16[2,8,64,384]{3,2,1,0:T(8,128)(2,1)S(1)}, bf16[2,8,64,384]{3,2,1,0:T(8,128)(2,1)S(1)}, u32[]{:S(2)}, u32[]{:S(2)}) collective-permute-start(bf16[2,8,64,384]{3,2,1,0:T(8,128)(2,1)S(1)} %collective-permute-done.9.refs_9_), channel_id=1, source_target_pairs={{0,4},{1,29},{4,8},{5,1},{8,12},{9,5},{12,16},{13,9},{16,20},{17,1... | collective-permute-start | bytes 2359304 | tf_op jit(solution)/shard_map/ppermute | solution.py:74
  38.8 0.1 pad_maximum_fusion.1.refs_0_
  38.9 5.1 %collective-permute-start.1 = (bf16[2,8,128,128]{3,2,1,0:T(8,128)(2,1)S(1)}, bf16[2,8,128,128]{3,2,1,0:T(8,128)(2,1)S(1)}, u32[]{:S(2)}, u32[]{:S(2)}) collective-permute-start(bf16[2,8,128,128]{3,2,1,0:T(8,128)(2,1)S(1)} %pad_maximum_fusion.1.refs_0_), channel_id=1, source_target_pairs={{0,64},{1,449},{64,128},{65,1},{128,192},{129,65},{192,256},{193,1... | collective-permute-start | bytes 1572872 | tf_op jit(solution)/shard_map/ppermute | solution.py:74
  44.0 1.9 %collective-permute-start.5 = (bf16[2,8,128,128]{3,2,1,0:T(8,128)(2,1)S(1)}, bf16[2,8,128,128]{3,2,1,0:T(8,128)(2,1)S(1)}, u32[]{:S(2)}, u32[]{:S(2)}) collective-permute-start(bf16[2,8,128,128]{3,2,1,0:T(8,128)(2,1)S(1)} %pad_maximum_fusion.1.refs_0_), channel_id=1, source_target_pairs={{64,0},{449,1},{128,64},{1,65},{192,128},{65,129},{256,192},{129,1... | collective-permute-start | bytes 1572872 | tf_op jit(solution)/shard_map/ppermute | solution.py:75
  45.9 6.3 %collective-permute-done.1.refs_1_ = bf16[2,8,128,128]{3,2,1,0:T(8,128)(2,1)S(1)} collective-permute-done((bf16[2,8,128,128]{3,2,1,0:T(8,128)(2,1)S(1)}, bf16[2,8,128,128]{3,2,1,0:T(8,128)(2,1)S(1)}, u32[]{:S(2)}, u32[]{:S(2)}) %collective-permute-start.1) | collective-permute-done | bytes 524320 | tf_op jit(solution)/shard_map/ppermute | solution.py:74
  52.2 5.3 %collective-permute-start.2 = (bf16[2,8,128,128]{3,2,1,0:T(8,128)(2,1)S(1)}, bf16[2,8,128,128]{3,2,1,0:T(8,128)(2,1)S(1)}, u32[]{:S(2)}, u32[]{:S(2)}) collective-permute-start(bf16[2,8,128,128]{3,2,1,0:T(8,128)(2,1)S(1)} %collective-permute-done.1.refs_1_), channel_id=1, source_target_pairs={{0,64},{1,449},{64,128},{65,1},{128,192},{129,65},{192,256},{193,1... | collective-permute-start | bytes 1572872 | tf_op jit(solution)/shard_map/ppermute | solution.py:74
  57.5 1.9 %collective-permute-start.13 = (bf16[2,8,64,384]{3,2,1,0:T(8,128)(2,1)S(1)}, bf16[2,8,64,384]{3,2,1,0:T(8,128)(2,1)S(1)}, u32[]{:S(2)}, u32[]{:S(2)}) collective-permute-start(bf16[2,8,64,384]{3,2,1,0:T(8,128)(2,1)S(1)} %collective-permute-done.12.refs_12_), channel_id=1, source_target_pairs={{4,0},{29,1},{8,4},{1,5},{12,8},{5,9},{16,12},{9,13},{20,16},{13,1... | collective-permute-start | bytes 2359304 | tf_op jit(solution)/shard_map/ppermute | solution.py:75
  59.4 4.6 %collective-permute-start.11 = (bf16[2,8,64,384]{3,2,1,0:T(8,128)(2,1)S(1)}, bf16[2,8,64,384]{3,2,1,0:T(8,128)(2,1)S(1)}, u32[]{:S(2)}, u32[]{:S(2)}) collective-permute-start(bf16[2,8,64,384]{3,2,1,0:T(8,128)(2,1)S(1)} %collective-permute-done.10.refs_10_), channel_id=1, source_target_pairs={{0,4},{1,29},{4,8},{5,1},{8,12},{9,5},{12,16},{13,9},{16,20},{17,1... | collective-permute-start | bytes 2359304 | tf_op jit(solution)/shard_map/ppermute | solution.py:74
  64.0 1.9 %collective-permute-start.6 = (bf16[2,8,128,128]{3,2,1,0:T(8,128)(2,1)S(1)}, bf16[2,8,128,128]{3,2,1,0:T(8,128)(2,1)S(1)}, u32[]{:S(2)}, u32[]{:S(2)}) collective-permute-start(bf16[2,8,128,128]{3,2,1,0:T(8,128)(2,1)S(1)} %collective-permute-done.5.refs_5_), channel_id=1, source_target_pairs={{64,0},{449,1},{128,64},{1,65},{192,128},{65,129},{256,192},{129,1... | collective-permute-start | bytes 1572872 | tf_op jit(solution)/shard_map/ppermute | solution.py:75
  66.0 4.6 %collective-permute-start.3 = (bf16[2,8,128,128]{3,2,1,0:T(8,128)(2,1)S(1)}, bf16[2,8,128,128]{3,2,1,0:T(8,128)(2,1)S(1)}, u32[]{:S(2)}, u32[]{:S(2)}) collective-permute-start(bf16[2,8,128,128]{3,2,1,0:T(8,128)(2,1)S(1)} %collective-permute-done.2.refs_2_), channel_id=1, source_target_pairs={{0,64},{1,449},{64,128},{65,1},{128,192},{129,65},{192,256},{193,1... | collective-permute-start | bytes 1572872 | tf_op jit(solution)/shard_map/ppermute | solution.py:74
  70.5 0.9 collective-permute-done.13.refs_13_
  71.4 1.9 %collective-permute-start.14 = (bf16[2,8,64,384]{3,2,1,0:T(8,128)(2,1)S(1)}, bf16[2,8,64,384]{3,2,1,0:T(8,128)(2,1)S(1)}, u32[]{:S(2)}, u32[]{:S(2)}) collective-permute-start(bf16[2,8,64,384]{3,2,1,0:T(8,128)(2,1)S(1)} %collective-permute-done.13.refs_13_), channel_id=1, source_target_pairs={{4,0},{29,1},{8,4},{1,5},{12,8},{5,9},{16,12},{9,13},{20,16},{13,1... | collective-permute-start | bytes 2359304 | tf_op jit(solution)/shard_map/ppermute | solution.py:75
  73.4 7.2 %collective-permute-done.11.refs_11_ = bf16[2,8,64,384]{3,2,1,0:T(8,128)(2,1)S(1)} collective-permute-done((bf16[2,8,64,384]{3,2,1,0:T(8,128)(2,1)S(1)}, bf16[2,8,64,384]{3,2,1,0:T(8,128)(2,1)S(1)}, u32[]{:S(2)}, u32[]{:S(2)}) %collective-permute-start.11) | collective-permute-done | bytes 786464 | tf_op jit(solution)/shard_map/ppermute | solution.py:74
  80.6 4.3 %collective-permute-start.15 = (bf16[2,8,64,384]{3,2,1,0:T(8,128)(2,1)S(1)}, bf16[2,8,64,384]{3,2,1,0:T(8,128)(2,1)S(1)}, u32[]{:S(2)}, u32[]{:S(2)}) collective-permute-start(bf16[2,8,64,384]{3,2,1,0:T(8,128)(2,1)S(1)} %collective-permute-done.11.refs_11_), channel_id=1, source_target_pairs={{0,4},{1,29},{4,8},{5,1},{8,12},{9,5},{12,16},{13,9},{16,20},{17,1... | collective-permute-start | bytes 2359304 | tf_op jit(solution)/shard_map/ppermute | solution.py:76
  84.9 1.9 %collective-permute-start.7 = (bf16[2,8,128,128]{3,2,1,0:T(8,128)(2,1)S(1)}, bf16[2,8,128,128]{3,2,1,0:T(8,128)(2,1)S(1)}, u32[]{:S(2)}, u32[]{:S(2)}) collective-permute-start(bf16[2,8,128,128]{3,2,1,0:T(8,128)(2,1)S(1)} %collective-permute-done.6.refs_6_), channel_id=1, source_target_pairs={{64,0},{449,1},{128,64},{1,65},{192,128},{65,129},{256,192},{129,1... | collective-permute-start | bytes 1572872 | tf_op jit(solution)/shard_map/ppermute | solution.py:75
  86.8 4.6 %collective-permute-start.4 = (bf16[2,8,128,128]{3,2,1,0:T(8,128)(2,1)S(1)}, bf16[2,8,128,128]{3,2,1,0:T(8,128)(2,1)S(1)}, u32[]{:S(2)}, u32[]{:S(2)}) collective-permute-start(bf16[2,8,128,128]{3,2,1,0:T(8,128)(2,1)S(1)} %collective-permute-done.3.refs_3_), channel_id=1, source_target_pairs={{0,64},{1,449},{64,128},{65,1},{128,192},{129,65},{192,256},{193,1... | collective-permute-start | bytes 1572872 | tf_op jit(solution)/shard_map/ppermute | solution.py:76
  91.4 4.9 %collective-permute-done.7.refs_7_ = bf16[2,8,128,128]{3,2,1,0:T(8,128)(2,1)S(1)} collective-permute-done((bf16[2,8,128,128]{3,2,1,0:T(8,128)(2,1)S(1)}, bf16[2,8,128,128]{3,2,1,0:T(8,128)(2,1)S(1)}, u32[]{:S(2)}, u32[]{:S(2)}) %collective-permute-start.7) | collective-permute-done | bytes 524320 | tf_op jit(solution)/shard_map/ppermute | solution.py:75
  96.3 4.4 %collective-permute-done.4.refs_4_ = bf16[2,8,128,128]{3,2,1,0:T(8,128)(2,1)S(1)} collective-permute-done((bf16[2,8,128,128]{3,2,1,0:T(8,128)(2,1)S(1)}, bf16[2,8,128,128]{3,2,1,0:T(8,128)(2,1)S(1)}, u32[]{:S(2)}, u32[]{:S(2)}) %collective-permute-start.4) | collective-permute-done | bytes 524320 | tf_op jit(solution)/shard_map/ppermute | solution.py:76
  100.7 4.8 %shard_map.55 = (bf16[8,2,8,128,128]{4,3,2,1,0:T(8,128)(2,1)S(1)}, f32[256,384]{1,0:T(8,128)S(1)}) custom-call(s32[4]{0:T(128)S(1)} %pad_add_fusion.place, bf16[2,8,128,128]{3,2,1,0:T(8,128)(2,1)S(1)} %pad_maximum_fusion.1.refs_0_, bf16[2,8,128,128]{3,2,1,0:T(8,128)(2,1)S(1)} %collective-permute-done.1.refs_1_, ...), custom_call_target="tpu_custom_call" | custom-call | flops 1073741824 | bytes 16777216 | tf_op jit(solution)/shard_map/pallas_call | solution.py:80
  105.5 1.1 shard_map.56
  106.7 17.4 %all_to_all.5 = f32[8,96,128]{2,1,0:T(8,128)S(1)} all-to-all(f32[8,96,128]{2,1,0:T(8,128)S(1)} %bitcast.14), channel_id=1, replica_groups=mesh['y'=8,'xl'=2,'z'=8,'xh'=2,'core'=2] {'xl','xh','core'}, dimensions={0} | all-to-all | bytes 786432 | tf_op jit(solution)/shard_map/all_to_all | solution.py:102
  124.2 0.7 add_divide_fusion
  (16 shorter events, 0.1 us)
Async XLA Ops:
  1.4 9.1 %collective-permute-start.8 = (bf16[8,64,384]{2,1,0:T(8,128)(2,1)S(1)}, bf16[8,64,384]{2,1,0:T(8,128)(2,1)S(1)}, u32[]{:S(2)}, u32[]{:S(2)}) collective-permute-start(bf16[8,64,384]{2,1,0:T(8,128)(2,1)S(1)} %get-tuple-element.10), channel_id=1, source_target_pairs={{0,32},{32,0},{1,33},{33,1},{2,34},{34,2},{3,35},{35,3},{4,36},{36... | collective-permute-start | bytes 1179656 | tf_op jit(solution)/shard_map/ppermute | solution.py:69
  10.6 23.2 %collective-permute-start.9 = (bf16[2,8,64,384]{3,2,1,0:T(8,128)(2,1)S(1)}, bf16[2,8,64,384]{3,2,1,0:T(8,128)(2,1)S(1)}, u32[]{:S(2)}, u32[]{:S(2)}) collective-permute-start(bf16[2,8,64,384]{3,2,1,0:T(8,128)(2,1)S(1)} %pad_maximum_fusion.refs_8_), channel_id=1, source_target_pairs={{0,4},{1,29},{4,8},{5,1},{8,12},{9,5},{12,16},{13,9},{16,20},{17,1... | collective-permute-start | bytes 2359304 | tf_op jit(solution)/shard_map/ppermute | solution.py:74
  25.9 12.9 %collective-permute-start = (bf16[8,128,128]{2,1,0:T(8,128)(2,1)S(1)}, bf16[8,128,128]{2,1,0:T(8,128)(2,1)S(1)}, u32[]{:S(2)}, u32[]{:S(2)}) collective-permute-start(bf16[8,128,128]{2,1,0:T(8,128)(2,1)S(1)} %get-tuple-element.12), channel_id=1, source_target_pairs={{0,32},{32,0},{1,33},{33,1},{2,34},{34,2},{3,35},{35,3},{4,36},{36... | collective-permute-start | bytes 786440 | tf_op jit(solution)/shard_map/ppermute | solution.py:69
  29.1 28.4 %collective-permute-start.12 = (bf16[2,8,64,384]{3,2,1,0:T(8,128)(2,1)S(1)}, bf16[2,8,64,384]{3,2,1,0:T(8,128)(2,1)S(1)}, u32[]{:S(2)}, u32[]{:S(2)}) collective-permute-start(bf16[2,8,64,384]{3,2,1,0:T(8,128)(2,1)S(1)} %pad_maximum_fusion.refs_8_), channel_id=1, source_target_pairs={{4,0},{29,1},{8,4},{1,5},{12,8},{5,9},{16,12},{9,13},{20,16},{13,1... | collective-permute-start | bytes 2359304 | tf_op jit(solution)/shard_map/ppermute | solution.py:75
  33.8 25.7 %collective-permute-start.10 = (bf16[2,8,64,384]{3,2,1,0:T(8,128)(2,1)S(1)}, bf16[2,8,64,384]{3,2,1,0:T(8,128)(2,1)S(1)}, u32[]{:S(2)}, u32[]{:S(2)}) collective-permute-start(bf16[2,8,64,384]{3,2,1,0:T(8,128)(2,1)S(1)} %collective-permute-done.9.refs_9_), channel_id=1, source_target_pairs={{0,4},{1,29},{4,8},{5,1},{8,12},{9,5},{12,16},{13,9},{16,20},{17,1... | collective-permute-start | bytes 2359304 | tf_op jit(solution)/shard_map/ppermute | solution.py:74
  38.9 13.3 %collective-permute-start.1 = (bf16[2,8,128,128]{3,2,1,0:T(8,128)(2,1)S(1)}, bf16[2,8,128,128]{3,2,1,0:T(8,128)(2,1)S(1)}, u32[]{:S(2)}, u32[]{:S(2)}) collective-permute-start(bf16[2,8,128,128]{3,2,1,0:T(8,128)(2,1)S(1)} %pad_maximum_fusion.1.refs_0_), channel_id=1, source_target_pairs={{0,64},{1,449},{64,128},{65,1},{128,192},{129,65},{192,256},{193,1... | collective-permute-start | bytes 1572872 | tf_op jit(solution)/shard_map/ppermute | solution.py:74
  44.0 20.1 %collective-permute-start.5 = (bf16[2,8,128,128]{3,2,1,0:T(8,128)(2,1)S(1)}, bf16[2,8,128,128]{3,2,1,0:T(8,128)(2,1)S(1)}, u32[]{:S(2)}, u32[]{:S(2)}) collective-permute-start(bf16[2,8,128,128]{3,2,1,0:T(8,128)(2,1)S(1)} %pad_maximum_fusion.1.refs_0_), channel_id=1, source_target_pairs={{64,0},{449,1},{128,64},{1,65},{192,128},{65,129},{256,192},{129,1... | collective-permute-start | bytes 1572872 | tf_op jit(solution)/shard_map/ppermute | solution.py:75
  52.2 13.8 %collective-permute-start.2 = (bf16[2,8,128,128]{3,2,1,0:T(8,128)(2,1)S(1)}, bf16[2,8,128,128]{3,2,1,0:T(8,128)(2,1)S(1)}, u32[]{:S(2)}, u32[]{:S(2)}) collective-permute-start(bf16[2,8,128,128]{3,2,1,0:T(8,128)(2,1)S(1)} %collective-permute-done.1.refs_1_), channel_id=1, source_target_pairs={{0,64},{1,449},{64,128},{65,1},{128,192},{129,65},{192,256},{193,1... | collective-permute-start | bytes 1572872 | tf_op jit(solution)/shard_map/ppermute | solution.py:74
  57.5 13.9 %collective-permute-start.13 = (bf16[2,8,64,384]{3,2,1,0:T(8,128)(2,1)S(1)}, bf16[2,8,64,384]{3,2,1,0:T(8,128)(2,1)S(1)}, u32[]{:S(2)}, u32[]{:S(2)}) collective-permute-start(bf16[2,8,64,384]{3,2,1,0:T(8,128)(2,1)S(1)} %collective-permute-done.12.refs_12_), channel_id=1, source_target_pairs={{4,0},{29,1},{8,4},{1,5},{12,8},{5,9},{16,12},{9,13},{20,16},{13,1... | collective-permute-start | bytes 2359304 | tf_op jit(solution)/shard_map/ppermute | solution.py:75
  59.4 21.2 %collective-permute-start.11 = (bf16[2,8,64,384]{3,2,1,0:T(8,128)(2,1)S(1)}, bf16[2,8,64,384]{3,2,1,0:T(8,128)(2,1)S(1)}, u32[]{:S(2)}, u32[]{:S(2)}) collective-permute-start(bf16[2,8,64,384]{3,2,1,0:T(8,128)(2,1)S(1)} %collective-permute-done.10.refs_10_), channel_id=1, source_target_pairs={{0,4},{1,29},{4,8},{5,1},{8,12},{9,5},{12,16},{13,9},{16,20},{17,1... | collective-permute-start | bytes 2359304 | tf_op jit(solution)/shard_map/ppermute | solution.py:74
  64.0 20.9 %collective-permute-start.6 = (bf16[2,8,128,128]{3,2,1,0:T(8,128)(2,1)S(1)}, bf16[2,8,128,128]{3,2,1,0:T(8,128)(2,1)S(1)}, u32[]{:S(2)}, u32[]{:S(2)}) collective-permute-start(bf16[2,8,128,128]{3,2,1,0:T(8,128)(2,1)S(1)} %collective-permute-done.5.refs_5_), channel_id=1, source_target_pairs={{64,0},{449,1},{128,64},{1,65},{192,128},{65,129},{256,192},{129,1... | collective-permute-start | bytes 1572872 | tf_op jit(solution)/shard_map/ppermute | solution.py:75
  66.0 20.9 %collective-permute-start.3 = (bf16[2,8,128,128]{3,2,1,0:T(8,128)(2,1)S(1)}, bf16[2,8,128,128]{3,2,1,0:T(8,128)(2,1)S(1)}, u32[]{:S(2)}, u32[]{:S(2)}) collective-permute-start(bf16[2,8,128,128]{3,2,1,0:T(8,128)(2,1)S(1)} %collective-permute-done.2.refs_2_), channel_id=1, source_target_pairs={{0,64},{1,449},{64,128},{65,1},{128,192},{129,65},{192,256},{193,1... | collective-permute-start | bytes 1572872 | tf_op jit(solution)/shard_map/ppermute | solution.py:74
  71.4 29.3 %collective-permute-start.14 = (bf16[2,8,64,384]{3,2,1,0:T(8,128)(2,1)S(1)}, bf16[2,8,64,384]{3,2,1,0:T(8,128)(2,1)S(1)}, u32[]{:S(2)}, u32[]{:S(2)}) collective-permute-start(bf16[2,8,64,384]{3,2,1,0:T(8,128)(2,1)S(1)} %collective-permute-done.13.refs_13_), channel_id=1, source_target_pairs={{4,0},{29,1},{8,4},{1,5},{12,8},{5,9},{16,12},{9,13},{20,16},{13,1... | collective-permute-start | bytes 2359304 | tf_op jit(solution)/shard_map/ppermute | solution.py:75
  80.6 24.9 %collective-permute-start.15 = (bf16[2,8,64,384]{3,2,1,0:T(8,128)(2,1)S(1)}, bf16[2,8,64,384]{3,2,1,0:T(8,128)(2,1)S(1)}, u32[]{:S(2)}, u32[]{:S(2)}) collective-permute-start(bf16[2,8,64,384]{3,2,1,0:T(8,128)(2,1)S(1)} %collective-permute-done.11.refs_11_), channel_id=1, source_target_pairs={{0,4},{1,29},{4,8},{5,1},{8,12},{9,5},{12,16},{13,9},{16,20},{17,1... | collective-permute-start | bytes 2359304 | tf_op jit(solution)/shard_map/ppermute | solution.py:76
  84.9 11.4 %collective-permute-start.7 = (bf16[2,8,128,128]{3,2,1,0:T(8,128)(2,1)S(1)}, bf16[2,8,128,128]{3,2,1,0:T(8,128)(2,1)S(1)}, u32[]{:S(2)}, u32[]{:S(2)}) collective-permute-start(bf16[2,8,128,128]{3,2,1,0:T(8,128)(2,1)S(1)} %collective-permute-done.6.refs_6_), channel_id=1, source_target_pairs={{64,0},{449,1},{128,64},{1,65},{192,128},{65,129},{256,192},{129,1... | collective-permute-start | bytes 1572872 | tf_op jit(solution)/shard_map/ppermute | solution.py:75
  86.8 13.9 %collective-permute-start.4 = (bf16[2,8,128,128]{3,2,1,0:T(8,128)(2,1)S(1)}, bf16[2,8,128,128]{3,2,1,0:T(8,128)(2,1)S(1)}, u32[]{:S(2)}, u32[]{:S(2)}) collective-permute-start(bf16[2,8,128,128]{3,2,1,0:T(8,128)(2,1)S(1)} %collective-permute-done.3.refs_3_), channel_id=1, source_target_pairs={{0,64},{1,449},{64,128},{65,1},{128,192},{129,65},{192,256},{193,1... | collective-permute-start | bytes 1572872 | tf_op jit(solution)/shard_map/ppermute | solution.py:76
  105.5 18.7 %copy-start = (bf16[96,128]{1,0:T(8,128)(2,1)S(1)}, bf16[96,128]{1,0:T(8,128)(2,1)}, u32[]{:S(2)}) copy-start(bf16[96,128]{1,0:T(8,128)(2,1)} %param.7) | copy-start | bytes 73732
  105.5 18.7 %copy-start.1 = (f32[128]{0:T(128)S(1)}, f32[128]{0:T(128)}, u32[]{:S(2)}) copy-start(f32[128]{0:T(128)} %param.9) | copy-start | bytes 1540
  105.5 18.7 %copy-start.2 = (f32[96]{0:T(128)S(1)}, f32[96]{0:T(128)}, u32[]{:S(2)}) copy-start(f32[96]{0:T(128)} %param.8) | copy-start | bytes 1156

commit v4 on v2

v4 whole, which is shorter than its diff:
```python
import jax
import jax.numpy as jnp
from jax import lax
from jax.experimental import pallas as pl
from jax.experimental.pallas import tpu as pltpu
from jax.sharding import Mesh, PartitionSpec as P

UP = [(i, (i + 1) % 8) for i in range(8)]
DOWN = [(i, (i - 1) % 8) for i in range(8)]
TRADE = [
    (2 * y + x, 2 * y + x if y // 4 == x else 2 * (7 - y) + 1 - x) for y in range(8) for x in range(2)
]
SHIFTS = (0, -1, -2, -3, 1, 2, 3)
ANY = pl.BlockSpec(memory_space=pl.ANY)
SMEM = pl.BlockSpec(memory_space=pltpu.SMEM)
VMEM = pl.BlockSpec(memory_space=pltpu.VMEM)
FLOAT = jnp.float32


def piece(place, amp_ref, source, block, first):
    y = place[0] * 4 + source // 2
    rows = pl.ds(pl.multiple_of(lax.rem(source, 2) * 64, 64), 64)
    count = block.shape[0]
    amp = jnp.concatenate(
        [
            amp_ref[slot, first : first + count, rows, :].reshape(count * 64, 128)
            for slot in (y, 7 - y)
        ],
        axis=1,
    )
    return lax.dot_general(
        amp,
        block.reshape(count * 64, 384),
        (((0,), (0,)), ((), ())),
        preferred_element_type=FLOAT,
    )


def early_kernel(place, *refs):
    amps, far, blocks, (amp, out, held, sems) = refs[:7], refs[7:9], refs[9:16], refs[16:]
    y, z = place[1], place[2]
    targets = [amp.at[lax.rem(y + shift + 8, 8)] for shift in SHIFTS]
    opposite = amp.at[lax.rem(y + 4, 8)]
    targets += [opposite.at[pl.ds(0, 8)], opposite.at[pl.ds(8, 8)]]
    targets += [held.at[j] for j in range(7)]
    copies = [
        pltpu.make_async_copy(ref, target, sems.at[j])
        for j, (ref, target) in enumerate(zip(amps + far + blocks, targets))
    ]
    for copy in copies:
        copy.start()
    for copy in copies[:9]:
        copy.wait()
    total = None
    for j, shift in enumerate(SHIFTS):
        copies[9 + j].wait()
        part = piece(place, amp, lax.rem(z + shift + 8, 8), held[j], 0)
        total = part if total is None else total + part
    out[...] = total


def late_kernel(place, early, amp, far_low, far_high, out):
    source = lax.rem(place[2] + 4, 8)
    total = early[...]
    for first, far in ((0, far_low), (8, far_high)):
        total = total + piece(place, amp, source, far[...], first)
    for n in range(2):
        out[lax.rem(place[0] + n, 2)] = total[n * 128 : (n + 1) * 128].T


def ring(own, axis):
    below, above = [own], [own]
    for _ in range(3):
        below.append(lax.ppermute(below[-1], axis, UP))
        above.append(lax.ppermute(above[-1], axis, DOWN))
    far = [lax.ppermute(below[3][:8], axis, UP), lax.ppermute(above[3][8:], axis, DOWN)]
    return below + above[1:], far


def local(integrals, amplitudes, coulomb, row_gap, col_gap):
    place = jnp.stack([lax.axis_index(a) for a in ("xl", "y", "z")])
    place, integrals, amplitudes = lax.optimization_barrier((place, integrals, amplitudes))
    blocks, far = ring(integrals, "z")
    amps, a_far = ring(lax.ppermute(amplitudes, ("y", "xl"), TRADE), "y")
    early, amp = pl.pallas_call(
        early_kernel,
        out_shape=(
            jax.ShapeDtypeStruct((8, 16, 128, 128), jnp.bfloat16),
            jax.ShapeDtypeStruct((256, 384), FLOAT),
        ),
        in_specs=[SMEM] + [ANY] * 16,
        out_specs=(VMEM, VMEM),
        scratch_shapes=[
            pltpu.VMEM((7, 16, 64, 384), jnp.bfloat16),
            pltpu.SemaphoreType.DMA((16,)),
        ],
        compiler_params=pltpu.CompilerParams(vmem_limit_bytes=24 << 20),
        cost_estimate=pl.CostEstimate(flops=1 << 30, bytes_accessed=16 << 20, transcendentals=0),
    )(place, *amps, *a_far, *blocks)[::-1]
    shares = pl.pallas_call(
        late_kernel,
        out_shape=jax.ShapeDtypeStruct((2, 384, 128), FLOAT),
        in_specs=[SMEM] + [VMEM] * 4,
        out_specs=VMEM,
        compiler_params=pltpu.CompilerParams(vmem_limit_bytes=6 << 20),
    )(place, early, amp, *far)
    shares = lax.all_to_all(
        shares.reshape(8, 96, 128), ("xl", "xh", "core"), 0, 0, tiled=True
    )
    own = jnp.sum(shares, axis=0)
    gap_sum = row_gap[:, None] + col_gap[None, :]
    return (coulomb.astype(FLOAT) + own) / gap_sum


def solution(mesh):
    fine = Mesh(mesh.devices.reshape(8, 2, 8, 2, 2), ("y", "xl", "z", "xh", "core"))
    layer, col = ("xh", "core"), ("xl", "z")
    placed = (
        P(layer, col, "y"),
        P(layer, "y", col),
        P(("y",) + layer, col),
        P(("y",) + layer),
        P(col),
    )
    return jax.shard_map(
        local, mesh=fine, in_specs=placed, out_specs=P(("y",) + layer, col), check_vma=False
    )
```

time: 128 us -> 127 us (level)
  the two profiles are of different devices: /device:TPU:1 before, /device:TPU:24 now
where the time goes in v4:
time: 127 us
  starting transfers between devices  70.1 us (55%)
  waiting for transfers between devices  35.7 us (28%)
  blocking collectives  12.7 us (10%)
  Pallas kernels  5.79 us (5%)
  local copies, waits for them, and re-layouts  1.27 us (1%)
    ppermute x6, starting transfers between devices, ring(): below.append(lax.ppermute(below[-1], axis, UP))  29.9 us
    ppermute x6, waiting for transfers between devices, ring(): below.append(lax.ppermute(below[-1], axis, UP))  28.1 us
    ppermute x6, starting transfers between devices, ring(): above.append(lax.ppermute(above[-1], axis, DOWN))  24.6 us
    all_to_all x1, blocking collectives, local(): lax.all_to_all(shares.reshape(8, 96, 128), ('xl', 'xh', 'core'), 0, 0, ti...  12.7 us
    ppermute x2, starting transfers between devices, ring(): lax.ppermute(above[3][8:], axis, DOWN)  7.05 us
    ppermute x2, starting transfers between devices, ring(): lax.ppermute(below[3][:8], axis, UP)  6.77 us
    ppermute x2, waiting for transfers between devices, ring(): lax.ppermute(above[3][8:], axis, DOWN)  5.65 us
    pallas_call x1, Pallas kernels, local(): pl.pallas_call(early_kernel, out_shape=(jax.ShapeDtypeStruct((8, 16, 128,...  4.66 us
  transfers between devices with their start and end apart: 17, of which 6 were waited for; matrix products, arithmetic and copies ran while one was open for 0% of the time, Pallas kernels for 4%

profile of v4, /device:TPU:24, one launch (start us, length us, event | category | flops | bytes accessed | tf_op | source)
XLA Modules:
  0.0 126.7 jit_solution(15435473527088123199)
XLA Ops:
  0.0 0.1 pad_add_fusion.place
  0.1 4.3 %collective-permute-start.9 = (bf16[16,64,384]{2,1,0:T(8,128)(2,1)}, bf16[16,64,384]{2,1,0:T(8,128)(2,1)S(1)}, u32[]{:S(2)}, u32[]{:S(2)}) collective-permute-start(bf16[16,64,384]{2,1,0:T(8,128)(2,1)} %refs_9_), channel_id=1, source_target_pairs={{0,4},{4,8},{8,12},{12,16},{16,20},{20,24},{24,28},{28,0},{1,5},{5... | collective-permute-start | bytes 2359304 | tf_op jit(solution)/shard_map/ppermute | solution.py:74
  4.4 8.6 %collective-permute-start.12 = (bf16[16,64,384]{2,1,0:T(8,128)(2,1)}, bf16[16,64,384]{2,1,0:T(8,128)(2,1)S(1)}, u32[]{:S(2)}, u32[]{:S(2)}) collective-permute-start(bf16[16,64,384]{2,1,0:T(8,128)(2,1)} %refs_9_), channel_id=1, source_target_pairs={{0,28},{4,0},{8,4},{12,8},{16,12},{20,16},{24,20},{28,24},{1,29},{... | collective-permute-start | bytes 2359304 | tf_op jit(solution)/shard_map/ppermute | solution.py:75
  13.0 1.7 %collective-permute-start = (bf16[16,128,128]{2,1,0:T(8,128)(2,1)}, bf16[16,128,128]{2,1,0:T(8,128)(2,1)S(1)}, u32[]{:S(2)}, u32[]{:S(2)}) collective-permute-start(bf16[16,128,128]{2,1,0:T(8,128)(2,1)} %param.6), channel_id=1, source_target_pairs={{0,0},{32,448},{64,64},{96,384},{128,128},{160,320},{192,192},{224... | collective-permute-start | bytes 1572872 | tf_op jit(solution)/shard_map/ppermute | solution.py:84
  14.7 14.1 %collective-permute-done.9.refs_10_ = bf16[16,64,384]{2,1,0:T(8,128)(2,1)S(1)} collective-permute-done((bf16[16,64,384]{2,1,0:T(8,128)(2,1)}, bf16[16,64,384]{2,1,0:T(8,128)(2,1)S(1)}, u32[]{:S(2)}, u32[]{:S(2)}) %collective-permute-start.9) | collective-permute-done | bytes 786464 | tf_op jit(solution)/shard_map/ppermute | solution.py:74
  28.8 1.9 %collective-permute-start.10 = (bf16[16,64,384]{2,1,0:T(8,128)(2,1)S(1)}, bf16[16,64,384]{2,1,0:T(8,128)(2,1)S(1)}, u32[]{:S(2)}, u32[]{:S(2)}) collective-permute-start(bf16[16,64,384]{2,1,0:T(8,128)(2,1)S(1)} %collective-permute-done.9.refs_10_), channel_id=1, source_target_pairs={{0,4},{4,8},{8,12},{12,16},{16,20},{20,24},{24,28},{28,0},{1,5},{5... | collective-permute-start | bytes 2359304 | tf_op jit(solution)/shard_map/ppermute | solution.py:74
  30.7 5.1 %collective-permute-start.13 = (bf16[16,64,384]{2,1,0:T(8,128)(2,1)S(1)}, bf16[16,64,384]{2,1,0:T(8,128)(2,1)S(1)}, u32[]{:S(2)}, u32[]{:S(2)}) collective-permute-start(bf16[16,64,384]{2,1,0:T(8,128)(2,1)S(1)} %collective-permute-done.12.refs_13_), channel_id=1, source_target_pairs={{0,28},{4,0},{8,4},{12,8},{16,12},{20,16},{24,20},{28,24},{1,29},{... | collective-permute-start | bytes 2359304 | tf_op jit(solution)/shard_map/ppermute | solution.py:75
  35.8 10.6 %collective-permute-start.1 = (bf16[16,128,128]{2,1,0:T(8,128)(2,1)S(1)}, bf16[16,128,128]{2,1,0:T(8,128)(2,1)S(1)}, u32[]{:S(2)}, u32[]{:S(2)}) collective-permute-start(bf16[16,128,128]{2,1,0:T(8,128)(2,1)S(1)} %collective-permute-done.refs_0_), channel_id=1, source_target_pairs={{0,64},{64,128},{128,192},{192,256},{256,320},{320,384},{384,448},... | collective-permute-start | bytes 1572872 | tf_op jit(solution)/shard_map/ppermute | solution.py:74
  46.5 1.9 %collective-permute-start.4 = (bf16[16,128,128]{2,1,0:T(8,128)(2,1)S(1)}, bf16[16,128,128]{2,1,0:T(8,128)(2,1)S(1)}, u32[]{:S(2)}, u32[]{:S(2)}) collective-permute-start(bf16[16,128,128]{2,1,0:T(8,128)(2,1)S(1)} %collective-permute-done.refs_0_), channel_id=1, source_target_pairs={{0,448},{64,0},{128,64},{192,128},{256,192},{320,256},{384,320},{4... | collective-permute-start | bytes 1572872 | tf_op jit(solution)/shard_map/ppermute | solution.py:75
  48.4 8.3 %collective-permute-done.1.refs_1_ = bf16[16,128,128]{2,1,0:T(8,128)(2,1)S(1)} collective-permute-done((bf16[16,128,128]{2,1,0:T(8,128)(2,1)S(1)}, bf16[16,128,128]{2,1,0:T(8,128)(2,1)S(1)}, u32[]{:S(2)}, u32[]{:S(2)}) %collective-permute-start.1) | collective-permute-done | bytes 524320 | tf_op jit(solution)/shard_map/ppermute | solution.py:74
  56.8 5.6 %collective-permute-start.2 = (bf16[16,128,128]{2,1,0:T(8,128)(2,1)S(1)}, bf16[16,128,128]{2,1,0:T(8,128)(2,1)S(1)}, u32[]{:S(2)}, u32[]{:S(2)}) collective-permute-start(bf16[16,128,128]{2,1,0:T(8,128)(2,1)S(1)} %collective-permute-done.1.refs_1_), channel_id=1, source_target_pairs={{0,64},{64,128},{128,192},{192,256},{256,320},{320,384},{384,448},... | collective-permute-start | bytes 1572872 | tf_op jit(solution)/shard_map/ppermute | solution.py:74
  62.4 1.9 %collective-permute-start.5 = (bf16[16,128,128]{2,1,0:T(8,128)(2,1)S(1)}, bf16[16,128,128]{2,1,0:T(8,128)(2,1)S(1)}, u32[]{:S(2)}, u32[]{:S(2)}) collective-permute-start(bf16[16,128,128]{2,1,0:T(8,128)(2,1)S(1)} %collective-permute-done.4.refs_4_), channel_id=1, source_target_pairs={{0,448},{64,0},{128,64},{192,128},{256,192},{320,256},{384,320},{4... | collective-permute-start | bytes 1572872 | tf_op jit(solution)/shard_map/ppermute | solution.py:75
  64.3 1.9 %collective-permute-start.11 = (bf16[16,64,384]{2,1,0:T(8,128)(2,1)S(1)}, bf16[16,64,384]{2,1,0:T(8,128)(2,1)S(1)}, u32[]{:S(2)}, u32[]{:S(2)}) collective-permute-start(bf16[16,64,384]{2,1,0:T(8,128)(2,1)S(1)} %collective-permute-done.10.refs_11_), channel_id=1, source_target_pairs={{0,4},{4,8},{8,12},{12,16},{16,20},{20,24},{24,28},{28,0},{1,5},{5... | collective-permute-start | bytes 2359304 | tf_op jit(solution)/shard_map/ppermute | solution.py:74
  66.2 5.1 %collective-permute-start.14 = (bf16[16,64,384]{2,1,0:T(8,128)(2,1)S(1)}, bf16[16,64,384]{2,1,0:T(8,128)(2,1)S(1)}, u32[]{:S(2)}, u32[]{:S(2)}) collective-permute-start(bf16[16,64,384]{2,1,0:T(8,128)(2,1)S(1)} %collective-permute-done.13.refs_14_), channel_id=1, source_target_pairs={{0,28},{4,0},{8,4},{12,8},{16,12},{20,16},{24,20},{28,24},{1,29},{... | collective-permute-start | bytes 2359304 | tf_op jit(solution)/shard_map/ppermute | solution.py:75
  71.4 0.3 collective-permute-done.2.refs_2_
  71.7 5.6 %collective-permute-start.3 = (bf16[16,128,128]{2,1,0:T(8,128)(2,1)S(1)}, bf16[16,128,128]{2,1,0:T(8,128)(2,1)S(1)}, u32[]{:S(2)}, u32[]{:S(2)}) collective-permute-start(bf16[16,128,128]{2,1,0:T(8,128)(2,1)S(1)} %collective-permute-done.2.refs_2_), channel_id=1, source_target_pairs={{0,64},{64,128},{128,192},{192,256},{256,320},{320,384},{384,448},... | collective-permute-start | bytes 1572872 | tf_op jit(solution)/shard_map/ppermute | solution.py:74
  77.3 1.9 %collective-permute-start.6 = (bf16[16,128,128]{2,1,0:T(8,128)(2,1)S(1)}, bf16[16,128,128]{2,1,0:T(8,128)(2,1)S(1)}, u32[]{:S(2)}, u32[]{:S(2)}) collective-permute-start(bf16[16,128,128]{2,1,0:T(8,128)(2,1)S(1)} %collective-permute-done.5.refs_5_), channel_id=1, source_target_pairs={{0,448},{64,0},{128,64},{192,128},{256,192},{320,256},{384,320},{4... | collective-permute-start | bytes 1572872 | tf_op jit(solution)/shard_map/ppermute | solution.py:75
  79.2 5.4 %collective-permute-done.11.refs_12_ = bf16[16,64,384]{2,1,0:T(8,128)(2,1)S(1)} collective-permute-done((bf16[16,64,384]{2,1,0:T(8,128)(2,1)S(1)}, bf16[16,64,384]{2,1,0:T(8,128)(2,1)S(1)}, u32[]{:S(2)}, u32[]{:S(2)}) %collective-permute-start.11) | collective-permute-done | bytes 786464 | tf_op jit(solution)/shard_map/ppermute | solution.py:74
  84.6 1.9 %collective-permute-start.15 = (bf16[8,64,384]{2,1,0:T(8,128)(2,1)S(1)}, bf16[8,64,384]{2,1,0:T(8,128)(2,1)S(1)}, u32[]{:S(2)}, u32[]{:S(2)}) collective-permute-start(bf16[8,64,384]{2,1,0:T(8,128)(2,1)S(1)} %slice.18), channel_id=1, source_target_pairs={{0,4},{4,8},{8,12},{12,16},{16,20},{20,24},{24,28},{28,0},{1,5},{5... | collective-permute-start | bytes 1179656 | tf_op jit(solution)/shard_map/ppermute | solution.py:76
  86.6 5.1 %collective-permute-start.16 = (bf16[8,64,384]{2,1,0:T(8,128)(2,1)S(1)}, bf16[8,64,384]{2,1,0:T(8,128)(2,1)S(1)}, u32[]{:S(2)}, u32[]{:S(2)}) collective-permute-start(bf16[8,64,384]{2,1,0:T(8,128)(2,1)S(1)} %slice.19), channel_id=1, source_target_pairs={{0,28},{4,0},{8,4},{12,8},{16,12},{20,16},{24,20},{28,24},{1,29},{... | collective-permute-start | bytes 1179656 | tf_op jit(solution)/shard_map/ppermute | solution.py:76
  91.8 4.9 %collective-permute-start.7 = (bf16[8,128,128]{2,1,0:T(8,128)(2,1)S(1)}, bf16[8,128,128]{2,1,0:T(8,128)(2,1)S(1)}, u32[]{:S(2)}, u32[]{:S(2)}) collective-permute-start(bf16[8,128,128]{2,1,0:T(8,128)(2,1)S(1)} %slice.16), channel_id=1, source_target_pairs={{0,64},{64,128},{128,192},{192,256},{256,320},{320,384},{384,448},... | collective-permute-start | bytes 786440 | tf_op jit(solution)/shard_map/ppermute | solution.py:76
  96.7 1.9 %collective-permute-start.8 = (bf16[8,128,128]{2,1,0:T(8,128)(2,1)S(1)}, bf16[8,128,128]{2,1,0:T(8,128)(2,1)S(1)}, u32[]{:S(2)}, u32[]{:S(2)}) collective-permute-start(bf16[8,128,128]{2,1,0:T(8,128)(2,1)S(1)} %slice.17), channel_id=1, source_target_pairs={{0,448},{64,0},{128,64},{192,128},{256,192},{320,256},{384,320},{4... | collective-permute-start | bytes 786440 | tf_op jit(solution)/shard_map/ppermute | solution.py:76
  98.6 1.9 %collective-permute-done.7.refs_7_ = bf16[8,128,128]{2,1,0:T(8,128)(2,1)S(1)} collective-permute-done((bf16[8,128,128]{2,1,0:T(8,128)(2,1)S(1)}, bf16[8,128,128]{2,1,0:T(8,128)(2,1)S(1)}, u32[]{:S(2)}, u32[]{:S(2)}) %collective-permute-start.7) | collective-permute-done | bytes 262176 | tf_op jit(solution)/shard_map/ppermute | solution.py:76
  100.5 5.6 %collective-permute-done.8.refs_8_ = bf16[8,128,128]{2,1,0:T(8,128)(2,1)S(1)} collective-permute-done((bf16[8,128,128]{2,1,0:T(8,128)(2,1)S(1)}, bf16[8,128,128]{2,1,0:T(8,128)(2,1)S(1)}, u32[]{:S(2)}, u32[]{:S(2)}) %collective-permute-start.8) | collective-permute-done | bytes 262176 | tf_op jit(solution)/shard_map/ppermute | solution.py:76
  106.2 1.1 copy-done
  107.3 4.7 %shard_map.55 = (bf16[8,16,128,128]{3,2,1,0:T(8,128)(2,1)S(1)}, f32[256,384]{1,0:T(8,128)S(1)}) custom-call(s32[3]{0:T(128)S(1)} %pad_add_fusion.place, bf16[16,128,128]{2,1,0:T(8,128)(2,1)S(1)} %collective-permute-done.refs_0_, bf16[16,128,128]{2,1,0:T(8,128)(2,1)S(1)} %collective-permute-done.1.refs_1_, ...), custom_call_target="tpu_custom_call" | custom-call | flops 1073741824 | bytes 16777216 | tf_op jit(solution)/shard_map/pallas_call | solution.py:85
  112.0 0.0 copy-start.1
  112.0 0.0 copy-start.2
  112.0 0.0 copy-start.3
  112.0 1.1 shard_map.56
  113.2 12.7 %all_to_all.5 = f32[8,96,128]{2,1,0:T(8,128)S(1)} all-to-all(f32[8,96,128]{2,1,0:T(8,128)S(1)} %bitcast.4), channel_id=1, replica_groups=mesh['y'=8,'xl'=2,'z'=8,'xh'=2,'core'=2] {'xl','xh','core'}, dimensions={0} | all-to-all | bytes 786432 | tf_op jit(solution)/shard_map/all_to_all | solution.py:107
  126.0 0.7 add_divide_fusion
  (20 shorter events, 0.2 us)
Async XLA Ops:
  0.1 28.7 %collective-permute-start.9 = (bf16[16,64,384]{2,1,0:T(8,128)(2,1)}, bf16[16,64,384]{2,1,0:T(8,128)(2,1)S(1)}, u32[]{:S(2)}, u32[]{:S(2)}) collective-permute-start(bf16[16,64,384]{2,1,0:T(8,128)(2,1)} %refs_9_), channel_id=1, source_target_pairs={{0,4},{4,8},{8,12},{12,16},{16,20},{20,24},{24,28},{28,0},{1,5},{5... | collective-permute-start | bytes 2359304 | tf_op jit(solution)/shard_map/ppermute | solution.py:74
  4.4 26.3 %collective-permute-start.12 = (bf16[16,64,384]{2,1,0:T(8,128)(2,1)}, bf16[16,64,384]{2,1,0:T(8,128)(2,1)S(1)}, u32[]{:S(2)}, u32[]{:S(2)}) collective-permute-start(bf16[16,64,384]{2,1,0:T(8,128)(2,1)} %refs_9_), channel_id=1, source_target_pairs={{0,28},{4,0},{8,4},{12,8},{16,12},{20,16},{24,20},{28,24},{1,29},{... | collective-permute-start | bytes 2359304 | tf_op jit(solution)/shard_map/ppermute | solution.py:75
  13.0 22.9 %collective-permute-start = (bf16[16,128,128]{2,1,0:T(8,128)(2,1)}, bf16[16,128,128]{2,1,0:T(8,128)(2,1)S(1)}, u32[]{:S(2)}, u32[]{:S(2)}) collective-permute-start(bf16[16,128,128]{2,1,0:T(8,128)(2,1)} %param.6), channel_id=1, source_target_pairs={{0,0},{32,448},{64,64},{96,384},{128,128},{160,320},{192,192},{224... | collective-permute-start | bytes 1572872 | tf_op jit(solution)/shard_map/ppermute | solution.py:84
  28.8 35.5 %collective-permute-start.10 = (bf16[16,64,384]{2,1,0:T(8,128)(2,1)S(1)}, bf16[16,64,384]{2,1,0:T(8,128)(2,1)S(1)}, u32[]{:S(2)}, u32[]{:S(2)}) collective-permute-start(bf16[16,64,384]{2,1,0:T(8,128)(2,1)S(1)} %collective-permute-done.9.refs_10_), channel_id=1, source_target_pairs={{0,4},{4,8},{8,12},{12,16},{16,20},{20,24},{24,28},{28,0},{1,5},{5... | collective-permute-start | bytes 2359304 | tf_op jit(solution)/shard_map/ppermute | solution.py:74
  30.7 35.5 %collective-permute-start.13 = (bf16[16,64,384]{2,1,0:T(8,128)(2,1)S(1)}, bf16[16,64,384]{2,1,0:T(8,128)(2,1)S(1)}, u32[]{:S(2)}, u32[]{:S(2)}) collective-permute-start(bf16[16,64,384]{2,1,0:T(8,128)(2,1)S(1)} %collective-permute-done.12.refs_13_), channel_id=1, source_target_pairs={{0,28},{4,0},{8,4},{12,8},{16,12},{20,16},{24,20},{28,24},{1,29},{... | collective-permute-start | bytes 2359304 | tf_op jit(solution)/shard_map/ppermute | solution.py:75
  35.8 20.9 %collective-permute-start.1 = (bf16[16,128,128]{2,1,0:T(8,128)(2,1)S(1)}, bf16[16,128,128]{2,1,0:T(8,128)(2,1)S(1)}, u32[]{:S(2)}, u32[]{:S(2)}) collective-permute-start(bf16[16,128,128]{2,1,0:T(8,128)(2,1)S(1)} %collective-permute-done.refs_0_), channel_id=1, source_target_pairs={{0,64},{64,128},{128,192},{192,256},{256,320},{320,384},{384,448},... | collective-permute-start | bytes 1572872 | tf_op jit(solution)/shard_map/ppermute | solution.py:74
  46.5 15.9 %collective-permute-start.4 = (bf16[16,128,128]{2,1,0:T(8,128)(2,1)S(1)}, bf16[16,128,128]{2,1,0:T(8,128)(2,1)S(1)}, u32[]{:S(2)}, u32[]{:S(2)}) collective-permute-start(bf16[16,128,128]{2,1,0:T(8,128)(2,1)S(1)} %collective-permute-done.refs_0_), channel_id=1, source_target_pairs={{0,448},{64,0},{128,64},{192,128},{256,192},{320,256},{384,320},{4... | collective-permute-start | bytes 1572872 | tf_op jit(solution)/shard_map/ppermute | solution.py:75
  56.8 14.9 %collective-permute-start.2 = (bf16[16,128,128]{2,1,0:T(8,128)(2,1)S(1)}, bf16[16,128,128]{2,1,0:T(8,128)(2,1)S(1)}, u32[]{:S(2)}, u32[]{:S(2)}) collective-permute-start(bf16[16,128,128]{2,1,0:T(8,128)(2,1)S(1)} %collective-permute-done.1.refs_1_), channel_id=1, source_target_pairs={{0,64},{64,128},{128,192},{192,256},{256,320},{320,384},{384,448},... | collective-permute-start | bytes 1572872 | tf_op jit(solution)/shard_map/ppermute | solution.py:74
  62.4 14.9 %collective-permute-start.5 = (bf16[16,128,128]{2,1,0:T(8,128)(2,1)S(1)}, bf16[16,128,128]{2,1,0:T(8,128)(2,1)S(1)}, u32[]{:S(2)}, u32[]{:S(2)}) collective-permute-start(bf16[16,128,128]{2,1,0:T(8,128)(2,1)S(1)} %collective-permute-done.4.refs_4_), channel_id=1, source_target_pairs={{0,448},{64,0},{128,64},{192,128},{256,192},{320,256},{384,320},{4... | collective-permute-start | bytes 1572872 | tf_op jit(solution)/shard_map/ppermute | solution.py:75
  64.3 20.3 %collective-permute-start.11 = (bf16[16,64,384]{2,1,0:T(8,128)(2,1)S(1)}, bf16[16,64,384]{2,1,0:T(8,128)(2,1)S(1)}, u32[]{:S(2)}, u32[]{:S(2)}) collective-permute-start(bf16[16,64,384]{2,1,0:T(8,128)(2,1)S(1)} %collective-permute-done.10.refs_11_), channel_id=1, source_target_pairs={{0,4},{4,8},{8,12},{12,16},{16,20},{20,24},{24,28},{28,0},{1,5},{5... | collective-permute-start | bytes 2359304 | tf_op jit(solution)/shard_map/ppermute | solution.py:74
  66.2 20.3 %collective-permute-start.14 = (bf16[16,64,384]{2,1,0:T(8,128)(2,1)S(1)}, bf16[16,64,384]{2,1,0:T(8,128)(2,1)S(1)}, u32[]{:S(2)}, u32[]{:S(2)}) collective-permute-start(bf16[16,64,384]{2,1,0:T(8,128)(2,1)S(1)} %collective-permute-done.13.refs_14_), channel_id=1, source_target_pairs={{0,28},{4,0},{8,4},{12,8},{16,12},{20,16},{24,20},{28,24},{1,29},{... | collective-permute-start | bytes 2359304 | tf_op jit(solution)/shard_map/ppermute | solution.py:75
  71.7 20.1 %collective-permute-start.3 = (bf16[16,128,128]{2,1,0:T(8,128)(2,1)S(1)}, bf16[16,128,128]{2,1,0:T(8,128)(2,1)S(1)}, u32[]{:S(2)}, u32[]{:S(2)}) collective-permute-start(bf16[16,128,128]{2,1,0:T(8,128)(2,1)S(1)} %collective-permute-done.2.refs_2_), channel_id=1, source_target_pairs={{0,64},{64,128},{128,192},{192,256},{256,320},{320,384},{384,448},... | collective-permute-start | bytes 1572872 | tf_op jit(solution)/shard_map/ppermute | solution.py:74
  77.3 19.4 %collective-permute-start.6 = (bf16[16,128,128]{2,1,0:T(8,128)(2,1)S(1)}, bf16[16,128,128]{2,1,0:T(8,128)(2,1)S(1)}, u32[]{:S(2)}, u32[]{:S(2)}) collective-permute-start(bf16[16,128,128]{2,1,0:T(8,128)(2,1)S(1)} %collective-permute-done.5.refs_5_), channel_id=1, source_target_pairs={{0,448},{64,0},{128,64},{192,128},{256,192},{320,256},{384,320},{4... | collective-permute-start | bytes 1572872 | tf_op jit(solution)/shard_map/ppermute | solution.py:75
  84.6 27.4 %collective-permute-start.15 = (bf16[8,64,384]{2,1,0:T(8,128)(2,1)S(1)}, bf16[8,64,384]{2,1,0:T(8,128)(2,1)S(1)}, u32[]{:S(2)}, u32[]{:S(2)}) collective-permute-start(bf16[8,64,384]{2,1,0:T(8,128)(2,1)S(1)} %slice.18), channel_id=1, source_target_pairs={{0,4},{4,8},{8,12},{12,16},{16,20},{20,24},{24,28},{28,0},{1,5},{5... | collective-permute-start | bytes 1179656 | tf_op jit(solution)/shard_map/ppermute | solution.py:76
  86.6 25.4 %collective-permute-start.16 = (bf16[8,64,384]{2,1,0:T(8,128)(2,1)S(1)}, bf16[8,64,384]{2,1,0:T(8,128)(2,1)S(1)}, u32[]{:S(2)}, u32[]{:S(2)}) collective-permute-start(bf16[8,64,384]{2,1,0:T(8,128)(2,1)S(1)} %slice.19), channel_id=1, source_target_pairs={{0,28},{4,0},{8,4},{12,8},{16,12},{20,16},{24,20},{28,24},{1,29},{... | collective-permute-start | bytes 1179656 | tf_op jit(solution)/shard_map/ppermute | solution.py:76
  91.8 8.7 %collective-permute-start.7 = (bf16[8,128,128]{2,1,0:T(8,128)(2,1)S(1)}, bf16[8,128,128]{2,1,0:T(8,128)(2,1)S(1)}, u32[]{:S(2)}, u32[]{:S(2)}) collective-permute-start(bf16[8,128,128]{2,1,0:T(8,128)(2,1)S(1)} %slice.16), channel_id=1, source_target_pairs={{0,64},{64,128},{128,192},{192,256},{256,320},{320,384},{384,448},... | collective-permute-start | bytes 786440 | tf_op jit(solution)/shard_map/ppermute | solution.py:76
  96.7 9.5 %collective-permute-start.8 = (bf16[8,128,128]{2,1,0:T(8,128)(2,1)S(1)}, bf16[8,128,128]{2,1,0:T(8,128)(2,1)S(1)}, u32[]{:S(2)}, u32[]{:S(2)}) collective-permute-start(bf16[8,128,128]{2,1,0:T(8,128)(2,1)S(1)} %slice.17), channel_id=1, source_target_pairs={{0,448},{64,0},{128,64},{192,128},{256,192},{320,256},{384,320},{4... | collective-permute-start | bytes 786440 | tf_op jit(solution)/shard_map/ppermute | solution.py:76
  106.2 1.1 copy-start
  112.0 14.0 %copy-start.1 = (bf16[96,128]{1,0:T(8,128)(2,1)S(1)}, bf16[96,128]{1,0:T(8,128)(2,1)}, u32[]{:S(2)}) copy-start(bf16[96,128]{1,0:T(8,128)(2,1)} %param.7) | copy-start | bytes 73732
  112.0 14.0 %copy-start.2 = (f32[128]{0:T(128)S(1)}, f32[128]{0:T(128)}, u32[]{:S(2)}) copy-start(f32[128]{0:T(128)} %param.9) | copy-start | bytes 1540
  112.0 14.0 %copy-start.3 = (f32[96]{0:T(128)S(1)}, f32[96]{0:T(128)}, u32[]{:S(2)}) copy-start(f32[96]{0:T(128)} %param.8) | copy-start | bytes 1156

commit v5 on v4

v5 whole, which is shorter than its diff:
```python
import jax
import jax.numpy as jnp
from jax import lax
from jax.experimental import pallas as pl
from jax.experimental.pallas import tpu as pltpu
from jax.sharding import Mesh, PartitionSpec as P

UP = [(i, (i + 1) % 8) for i in range(8)]
DOWN = [(i, (i - 1) % 8) for i in range(8)]
TRADE = [
    (2 * y + x, 2 * y + x if y // 4 == x else 2 * (7 - y) + 1 - x) for y in range(8) for x in range(2)
]
SHIFTS = (0, -1, -2, -3, 1, 2, 3)
ANY = pl.BlockSpec(memory_space=pl.ANY)
SMEM = pl.BlockSpec(memory_space=pltpu.SMEM)
VMEM = pl.BlockSpec(memory_space=pltpu.VMEM)
FLOAT = jnp.float32


def columns(amp_ref, slot, source):
    rows = pl.ds(pl.multiple_of(lax.rem(source, 2) * 64, 64), 64)
    return amp_ref[slot, :, rows, :].reshape(1024, 128)


def times(amp, block):
    return lax.dot_general(
        amp, block.reshape(1024, 384), (((0,), (0,)), ((), ())), preferred_element_type=FLOAT
    )


def piece(x, amp_ref, source, block):
    y = x * 4 + source // 2
    return times(
        jnp.concatenate([columns(amp_ref, slot, source) for slot in (y, 7 - y)], axis=1), block
    )


def early_kernel(place, *refs):
    (amps, blocks), (amp, held, out, sems) = (refs[:7], refs[7:14]), refs[14:]
    x, y, z = place[0], place[1], place[2]
    turns = [lax.rem(shift + 8, 8) for shift in SHIFTS]
    copies = [
        pltpu.make_async_copy(ref, amp.at[lax.rem(y + turn, 8)], sems.at[j])
        for j, (ref, turn) in enumerate(zip(amps, turns))
    ] + [
        pltpu.make_async_copy(ref, held.at[lax.rem(z + turn, 8)], sems.at[7 + j])
        for j, (ref, turn) in enumerate(zip(blocks, turns))
    ]
    for copy in copies:
        copy.start()
    amp[lax.rem(y + 4, 8)] = jnp.zeros((16, 128, 128), jnp.bfloat16)
    for copy in copies[:7]:
        copy.wait()
    total = None
    for j, turn in enumerate(turns):
        copies[7 + j].wait()
        source = lax.rem(z + turn, 8)
        part = piece(x, amp, source, held[source])
        total = part if total is None else total + part
    out[...] = total


def late_kernel(place, early, amp_in, held, amp_far, block_far, out, total):
    x, y, z = place[0], place[1], place[2]
    slot, opposite = lax.rem(y + 4, 8), lax.rem(z + 4, 8)
    mine = x * 4 + opposite // 2
    pair = jnp.concatenate(
        [
            jnp.where(at == slot, columns(amp_far, 0, opposite), columns(amp_in, at, opposite))
            for at in (mine, 7 - mine)
        ],
        axis=1,
    )
    total[...] = early[...] + times(pair, block_far[...])
    other = jnp.where(slot // 4 == x, 0, 1)
    first = lax.rem(jnp.where(other == 0, slot, 7 - slot), 4) * 2
    for source in (first, first + 1):

        @pl.when(source != opposite)
        def _():
            at = pl.ds(pl.multiple_of(other * 128, 128), 128)
            total[at, :] += times(columns(amp_far, 0, source), held[source])

    for n in range(2):
        out[lax.rem(x + n, 2)] = total[n * 128 : (n + 1) * 128].T


def after(block, *arrived):
    return lax.optimization_barrier((block,) + arrived)[0]


def local(integrals, amplitudes, coulomb, row_gap, col_gap):
    place = jnp.stack([lax.axis_index(a) for a in ("xl", "y", "z")])
    place, integrals, amplitudes = lax.optimization_barrier((place, integrals, amplitudes))

    def up(block, axis, *arrived):
        return lax.ppermute(after(block, *arrived), axis, UP)

    def down(block, axis, *arrived):
        return lax.ppermute(after(block, *arrived), axis, DOWN)

    a0 = lax.ppermute(amplitudes, ("y", "xl"), TRADE)
    i0 = integrals
    iu1, id1 = up(i0, "z"), down(i0, "z")
    iu2 = up(iu1, "z")
    au1, ad1 = up(a0, "y", iu1), down(a0, "y", iu1)
    id2 = down(id1, "z", a0)
    au2 = up(au1, "y", id1)
    iu3 = up(iu2, "z", au1)
    ad2 = down(ad1, "y", iu2)
    au3 = up(au2, "y", ad1)
    id3 = down(id2, "z", au2)
    iu4 = up(iu3, "z", id2)
    ad3 = down(ad2, "y", iu3)
    au4 = up(au3, "y", ad2)
    held_shape = jax.ShapeDtypeStruct((8, 16, 64, 384), jnp.bfloat16)
    amp_shape = jax.ShapeDtypeStruct((8, 16, 128, 128), jnp.bfloat16)
    amp, held, early = pl.pallas_call(
        early_kernel,
        out_shape=(amp_shape, held_shape, jax.ShapeDtypeStruct((256, 384), FLOAT)),
        in_specs=[SMEM] + [ANY] * 14,
        out_specs=(VMEM, VMEM, VMEM),
        scratch_shapes=[pltpu.SemaphoreType.DMA((14,))],
        compiler_params=pltpu.CompilerParams(vmem_limit_bytes=24 << 20),
        cost_estimate=pl.CostEstimate(flops=1 << 30, bytes_accessed=16 << 20, transcendentals=0),
    )(place, a0, au1, au2, au3, ad1, ad2, ad3, i0, iu1, iu2, iu3, id1, id2, id3)
    shares = pl.pallas_call(
        late_kernel,
        out_shape=jax.ShapeDtypeStruct((2, 384, 128), FLOAT),
        in_specs=[SMEM] + [VMEM] * 5,
        out_specs=VMEM,
        scratch_shapes=[pltpu.VMEM((256, 384), FLOAT)],
        compiler_params=pltpu.CompilerParams(vmem_limit_bytes=8 << 20),
    )(place, early, amp, held, au4[None], iu4)
    shares = lax.all_to_all(
        shares.reshape(8, 96, 128), ("xl", "xh", "core"), 0, 0, tiled=True
    )
    own = jnp.sum(shares, axis=0)
    gap_sum = row_gap[:, None] + col_gap[None, :]
    return (coulomb.astype(FLOAT) + own) / gap_sum


def solution(mesh):
    fine = Mesh(mesh.devices.reshape(8, 2, 8, 2, 2), ("y", "xl", "z", "xh", "core"))
    layer, col = ("xh", "core"), ("xl", "z")
    placed = (
        P(layer, col, "y"),
        P(layer, "y", col),
        P(("y",) + layer, col),
        P(("y",) + layer),
        P(col),
    )
    return jax.shard_map(
        local, mesh=fine, in_specs=placed, out_specs=P(("y",) + layer, col), check_vma=False
    )
```

time: 127 us -> 116 us (0.913)
  the two profiles are of different devices: /device:TPU:24 before, /device:TPU:1 now
where the time goes in v5:
time: 116 us; the launch traced here: 114 us
  starting transfers between devices  63.4 us (55%)
  waiting for transfers between devices  25.8 us (22%)
  blocking collectives  15.8 us (14%)
  Pallas kernels  6.51 us (6%)
    ppermute x6, starting transfers between devices, down(): return lax.ppermute(after(block, *arrived), axis, DOWN)  40.6 us
    ppermute x8, starting transfers between devices, up(): return lax.ppermute(after(block, *arrived), axis, UP)  21.1 us
    ppermute x8, waiting for transfers between devices, up(): return lax.ppermute(after(block, *arrived), axis, UP)  19.6 us
    all_to_all x1, blocking collectives, local(): lax.all_to_all(shares.reshape(8, 96, 128), ('xl', 'xh', 'core'), 0, 0, ti...  15.8 us
    ppermute x6, waiting for transfers between devices, down(): return lax.ppermute(after(block, *arrived), axis, DOWN)  6.25 us
    pallas_call x1, Pallas kernels, local(): pl.pallas_call(early_kernel, out_shape=(amp_shape, held_shape, jax.ShapeD...  4.65 us
  transfers between devices with their start and end apart: 15, of which 5 were waited for; matrix products, arithmetic and copies ran while one was open for 0% of the time, Pallas kernels for 4%

profile of v5, /device:TPU:1, one launch (start us, length us, event | category | flops | bytes accessed | tf_op | source)
XLA Modules:
  0.0 113.8 jit_solution(5753691970976571242)
XLA Ops:
  0.0 0.1 pad_add_fusion.place
  0.1 4.8 %collective-permute-start.1 = (bf16[16,64,384]{2,1,0:T(8,128)(2,1)}, bf16[16,64,384]{2,1,0:T(8,128)(2,1)S(1)}, u32[]{:S(2)}, u32[]{:S(2)}) collective-permute-start(bf16[16,64,384]{2,1,0:T(8,128)(2,1)} %refs_7_), channel_id=1, source_target_pairs={{0,4},{4,8},{8,12},{12,16},{16,20},{20,24},{24,28},{28,0},{1,5},{5... | collective-permute-start | bytes 2359304 | tf_op jit(solution)/shard_map/ppermute | solution.py:97
  4.9 1.7 %collective-permute-start = (bf16[16,128,128]{2,1,0:T(8,128)(2,1)}, bf16[16,128,128]{2,1,0:T(8,128)(2,1)S(1)}, u32[]{:S(2)}, u32[]{:S(2)}) collective-permute-start(bf16[16,128,128]{2,1,0:T(8,128)(2,1)} %param.6), channel_id=1, source_target_pairs={{0,0},{32,448},{64,64},{96,384},{128,128},{160,320},{192,192},{224... | collective-permute-start | bytes 1572872 | tf_op jit(solution)/shard_map/ppermute | solution.py:102
  6.6 8.6 %collective-permute-start.3 = (bf16[16,64,384]{2,1,0:T(8,128)(2,1)}, bf16[16,64,384]{2,1,0:T(8,128)(2,1)S(1)}, u32[]{:S(2)}, u32[]{:S(2)}) collective-permute-start(bf16[16,64,384]{2,1,0:T(8,128)(2,1)} %refs_7_), channel_id=1, source_target_pairs={{0,28},{4,0},{8,4},{12,8},{16,12},{20,16},{24,20},{28,24},{1,29},{... | collective-permute-start | bytes 2359304 | tf_op jit(solution)/shard_map/ppermute | solution.py:100
  15.2 13.8 %collective-permute-done.1.refs_8_ = bf16[16,64,384]{2,1,0:T(8,128)(2,1)S(1)} collective-permute-done((bf16[16,64,384]{2,1,0:T(8,128)(2,1)}, bf16[16,64,384]{2,1,0:T(8,128)(2,1)S(1)}, u32[]{:S(2)}, u32[]{:S(2)}) %collective-permute-start.1) | collective-permute-done | bytes 786464 | tf_op jit(solution)/shard_map/ppermute | solution.py:97
  29.0 1.9 %collective-permute-start.7 = (bf16[16,64,384]{2,1,0:T(8,128)(2,1)S(1)}, bf16[16,64,384]{2,1,0:T(8,128)(2,1)S(1)}, u32[]{:S(2)}, u32[]{:S(2)}) collective-permute-start(bf16[16,64,384]{2,1,0:T(8,128)(2,1)S(1)} %collective-permute-done.1.refs_8_), channel_id=1, source_target_pairs={{0,4},{4,8},{8,12},{12,16},{16,20},{20,24},{24,28},{28,0},{1,5},{5... | collective-permute-start | bytes 2359304 | tf_op jit(solution)/shard_map/ppermute | solution.py:97
  31.0 3.2 %collective-permute-start.2 = (bf16[16,128,128]{2,1,0:T(8,128)(2,1)S(1)}, bf16[16,128,128]{2,1,0:T(8,128)(2,1)S(1)}, u32[]{:S(2)}, u32[]{:S(2)}) collective-permute-start(bf16[16,128,128]{2,1,0:T(8,128)(2,1)S(1)} %collective-permute-done.refs_0_), channel_id=1, source_target_pairs={{0,64},{64,128},{128,192},{192,256},{256,320},{320,384},{384,448},... | collective-permute-start | bytes 1572872 | tf_op jit(solution)/shard_map/ppermute | solution.py:97
  34.2 5.7 %collective-permute-start.5 = (bf16[16,128,128]{2,1,0:T(8,128)(2,1)S(1)}, bf16[16,128,128]{2,1,0:T(8,128)(2,1)S(1)}, u32[]{:S(2)}, u32[]{:S(2)}) collective-permute-start(bf16[16,128,128]{2,1,0:T(8,128)(2,1)S(1)} %collective-permute-done.refs_0_), channel_id=1, source_target_pairs={{0,448},{64,0},{128,64},{192,128},{256,192},{320,256},{384,320},{4... | collective-permute-start | bytes 1572872 | tf_op jit(solution)/shard_map/ppermute | solution.py:100
  39.9 0.0 collective-permute-done.3.refs_11_
  39.9 8.9 %collective-permute-start.11 = (bf16[16,64,384]{2,1,0:T(8,128)(2,1)S(1)}, bf16[16,64,384]{2,1,0:T(8,128)(2,1)S(1)}, u32[]{:S(2)}, u32[]{:S(2)}) collective-permute-start(bf16[16,64,384]{2,1,0:T(8,128)(2,1)S(1)} %collective-permute-done.3.refs_11_), channel_id=1, source_target_pairs={{0,28},{4,0},{8,4},{12,8},{16,12},{20,16},{24,20},{28,24},{1,29},{... | collective-permute-start | bytes 2359304 | tf_op jit(solution)/shard_map/ppermute | solution.py:100
  48.8 1.9 %collective-permute-start.4 = (bf16[16,128,128]{2,1,0:T(8,128)(2,1)S(1)}, bf16[16,128,128]{2,1,0:T(8,128)(2,1)S(1)}, u32[]{:S(2)}, u32[]{:S(2)}) collective-permute-start(bf16[16,128,128]{2,1,0:T(8,128)(2,1)S(1)} %collective-permute-done.2.refs_1_), channel_id=1, source_target_pairs={{0,64},{64,128},{128,192},{192,256},{256,320},{320,384},{384,448},... | collective-permute-start | bytes 1572872 | tf_op jit(solution)/shard_map/ppermute | solution.py:97
  50.7 0.0 collective-permute-done.7.refs_9_
  50.7 3.5 %collective-permute-start.9 = (bf16[16,64,384]{2,1,0:T(8,128)(2,1)S(1)}, bf16[16,64,384]{2,1,0:T(8,128)(2,1)S(1)}, u32[]{:S(2)}, u32[]{:S(2)}) collective-permute-start(bf16[16,64,384]{2,1,0:T(8,128)(2,1)S(1)} %collective-permute-done.7.refs_9_), channel_id=1, source_target_pairs={{0,4},{4,8},{8,12},{12,16},{16,20},{20,24},{24,28},{28,0},{1,5},{5... | collective-permute-start | bytes 2359304 | tf_op jit(solution)/shard_map/ppermute | solution.py:97
  54.2 0.0 collective-permute-done.5.refs_4_
  54.2 4.6 %collective-permute-start.8 = (bf16[16,128,128]{2,1,0:T(8,128)(2,1)S(1)}, bf16[16,128,128]{2,1,0:T(8,128)(2,1)S(1)}, u32[]{:S(2)}, u32[]{:S(2)}) collective-permute-start(bf16[16,128,128]{2,1,0:T(8,128)(2,1)S(1)} %collective-permute-done.5.refs_4_), channel_id=1, source_target_pairs={{0,448},{64,0},{128,64},{192,128},{256,192},{320,256},{384,320},{4... | collective-permute-start | bytes 1572872 | tf_op jit(solution)/shard_map/ppermute | solution.py:100
  58.8 4.4 %collective-permute-done.4.refs_2_ = bf16[16,128,128]{2,1,0:T(8,128)(2,1)S(1)} collective-permute-done((bf16[16,128,128]{2,1,0:T(8,128)(2,1)S(1)}, bf16[16,128,128]{2,1,0:T(8,128)(2,1)S(1)}, u32[]{:S(2)}, u32[]{:S(2)}) %collective-permute-start.4) | collective-permute-done | bytes 524320 | tf_op jit(solution)/shard_map/ppermute | solution.py:97
  63.2 1.9 %collective-permute-start.6 = (bf16[16,128,128]{2,1,0:T(8,128)(2,1)S(1)}, bf16[16,128,128]{2,1,0:T(8,128)(2,1)S(1)}, u32[]{:S(2)}, u32[]{:S(2)}) collective-permute-start(bf16[16,128,128]{2,1,0:T(8,128)(2,1)S(1)} %collective-permute-done.4.refs_2_), channel_id=1, source_target_pairs={{0,64},{64,128},{128,192},{192,256},{256,320},{320,384},{384,448},... | collective-permute-start | bytes 1572872 | tf_op jit(solution)/shard_map/ppermute | solution.py:97
  65.1 8.6 %collective-permute-start.12 = (bf16[16,64,384]{2,1,0:T(8,128)(2,1)S(1)}, bf16[16,64,384]{2,1,0:T(8,128)(2,1)S(1)}, u32[]{:S(2)}, u32[]{:S(2)}) collective-permute-start(bf16[16,64,384]{2,1,0:T(8,128)(2,1)S(1)} %collective-permute-done.11.refs_12_), channel_id=1, source_target_pairs={{0,28},{4,0},{8,4},{12,8},{16,12},{20,16},{24,20},{28,24},{1,29},{... | collective-permute-start | bytes 2359304 | tf_op jit(solution)/shard_map/ppermute | solution.py:100
  73.8 1.3 %collective-permute-done.9.refs_10_ = bf16[16,64,384]{2,1,0:T(8,128)(2,1)S(1)} collective-permute-done((bf16[16,64,384]{2,1,0:T(8,128)(2,1)S(1)}, bf16[16,64,384]{2,1,0:T(8,128)(2,1)S(1)}, u32[]{:S(2)}, u32[]{:S(2)}) %collective-permute-start.9) | collective-permute-done | bytes 786464 | tf_op jit(solution)/shard_map/ppermute | solution.py:97
  75.1 1.9 %collective-permute-start.14 = (bf16[16,64,384]{2,1,0:T(8,128)(2,1)S(1)}, bf16[16,64,384]{2,1,0:T(8,128)(2,1)S(1)}, u32[]{:S(2)}, u32[]{:S(2)}) collective-permute-start(bf16[16,64,384]{2,1,0:T(8,128)(2,1)S(1)} %collective-permute-done.9.refs_10_), channel_id=1, source_target_pairs={{0,4},{4,8},{8,12},{12,16},{16,20},{20,24},{24,28},{28,0},{1,5},{5... | collective-permute-start | bytes 2359304 | tf_op jit(solution)/shard_map/ppermute | solution.py:97
  77.0 4.3 %collective-permute-start.10 = (bf16[16,128,128]{2,1,0:T(8,128)(2,1)S(1)}, bf16[16,128,128]{2,1,0:T(8,128)(2,1)S(1)}, u32[]{:S(2)}, u32[]{:S(2)}) collective-permute-start(bf16[16,128,128]{2,1,0:T(8,128)(2,1)S(1)} %collective-permute-done.8.refs_5_), channel_id=1, source_target_pairs={{0,448},{64,0},{128,64},{192,128},{256,192},{320,256},{384,320},{4... | collective-permute-start | bytes 1572872 | tf_op jit(solution)/shard_map/ppermute | solution.py:100
  81.3 1.9 %collective-permute-start.13 = (bf16[16,128,128]{2,1,0:T(8,128)(2,1)S(1)}, bf16[16,128,128]{2,1,0:T(8,128)(2,1)S(1)}, u32[]{:S(2)}, u32[]{:S(2)}) collective-permute-start(bf16[16,128,128]{2,1,0:T(8,128)(2,1)S(1)} %collective-permute-done.6.refs_3_), channel_id=1, source_target_pairs={{0,64},{64,128},{128,192},{192,256},{256,320},{320,384},{384,448},... | collective-permute-start | bytes 1572872 | tf_op jit(solution)/shard_map/ppermute | solution.py:97
  83.3 4.2 %collective-permute-done.12.refs_13_ = bf16[16,64,384]{2,1,0:T(8,128)(2,1)S(1)} collective-permute-done((bf16[16,64,384]{2,1,0:T(8,128)(2,1)S(1)}, bf16[16,64,384]{2,1,0:T(8,128)(2,1)S(1)}, u32[]{:S(2)}, u32[]{:S(2)}) %collective-permute-start.12) | collective-permute-done | bytes 786464 | tf_op jit(solution)/shard_map/ppermute | solution.py:100
  87.5 2.0 %collective-permute-done.10.refs_6_ = bf16[16,128,128]{2,1,0:T(8,128)(2,1)S(1)} collective-permute-done((bf16[16,128,128]{2,1,0:T(8,128)(2,1)S(1)}, bf16[16,128,128]{2,1,0:T(8,128)(2,1)S(1)}, u32[]{:S(2)}, u32[]{:S(2)}) %collective-permute-start.10) | collective-permute-done | bytes 524320 | tf_op jit(solution)/shard_map/ppermute | solution.py:100
  89.5 1.1 copy-done
  90.6 4.7 %shard_map.55 = (bf16[8,16,128,128]{3,2,1,0:T(8,128)(2,1)S(1)}, bf16[8,16,64,384]{3,2,1,0:T(8,128)(2,1)S(1)}, f32[256,384]{1,0:T(8,128)S(1)}) custom-call(s32[3]{0:T(128)S(1)} %pad_add_fusion.place, bf16[16,128,128]{2,1,0:T(8,128)(2,1)S(1)} %collective-permute-done.refs_0_, bf16[16,128,128]{2,1,0:T(8,128)(2,1)S(1)} %collective-permute-done.2.refs_1_, ...), custom_call_target="tpu_custom_call" | custom-call | flops 1073741824 | bytes 16777216 | tf_op jit(solution)/shard_map/pallas_call | solution.py:118
  95.3 0.0 copy-start.1
  95.3 0.0 copy-start.2
  95.3 0.0 copy-start.3
  95.3 1.9 %shard_map.56 = f32[2,384,128]{2,1,0:T(8,128)S(1)} custom-call(s32[3]{0:T(128)S(1)} %pad_add_fusion.place, f32[256,384]{1,0:T(8,128)S(1)} %get-tuple-element.32.early, bf16[8,16,128,128]{3,2,1,0:T(8,128)(2,1)S(1)} %get-tuple-element.33.amp_in, bf16[8,16,64,384]{3,2,1,0:T(8,128)(2,1)S(1)} %get-tuple-element.34.held, bf16[1,16,128,128]{3,2,1,0:T(8,128)(2,1)S(1)} %bitcast.6, ...), custom_call_target="tpu_custom_call" | custom-call | tf_op jit(solution)/shard_map/pallas_call | solution.py:127
  97.2 15.8 %all_to_all.5 = f32[8,96,128]{2,1,0:T(8,128)S(1)} all-to-all(f32[8,96,128]{2,1,0:T(8,128)S(1)} %bitcast.5), channel_id=1, replica_groups=mesh['y'=8,'xl'=2,'z'=8,'xh'=2,'core'=2] {'xl','xh','core'}, dimensions={0} | all-to-all | bytes 786432 | tf_op jit(solution)/shard_map/all_to_all | solution.py:135
  113.1 0.7 add_divide_fusion
  (12 shorter events, 0.1 us)
Async XLA Ops:
  0.1 29.0 %collective-permute-start.1 = (bf16[16,64,384]{2,1,0:T(8,128)(2,1)}, bf16[16,64,384]{2,1,0:T(8,128)(2,1)S(1)}, u32[]{:S(2)}, u32[]{:S(2)}) collective-permute-start(bf16[16,64,384]{2,1,0:T(8,128)(2,1)} %refs_7_), channel_id=1, source_target_pairs={{0,4},{4,8},{8,12},{12,16},{16,20},{20,24},{24,28},{28,0},{1,5},{5... | collective-permute-start | bytes 2359304 | tf_op jit(solution)/shard_map/ppermute | solution.py:97
  4.9 26.0 %collective-permute-start = (bf16[16,128,128]{2,1,0:T(8,128)(2,1)}, bf16[16,128,128]{2,1,0:T(8,128)(2,1)S(1)}, u32[]{:S(2)}, u32[]{:S(2)}) collective-permute-start(bf16[16,128,128]{2,1,0:T(8,128)(2,1)} %param.6), channel_id=1, source_target_pairs={{0,0},{32,448},{64,64},{96,384},{128,128},{160,320},{192,192},{224... | collective-permute-start | bytes 1572872 | tf_op jit(solution)/shard_map/ppermute | solution.py:102
  6.6 33.2 %collective-permute-start.3 = (bf16[16,64,384]{2,1,0:T(8,128)(2,1)}, bf16[16,64,384]{2,1,0:T(8,128)(2,1)S(1)}, u32[]{:S(2)}, u32[]{:S(2)}) collective-permute-start(bf16[16,64,384]{2,1,0:T(8,128)(2,1)} %refs_7_), channel_id=1, source_target_pairs={{0,28},{4,0},{8,4},{12,8},{16,12},{20,16},{24,20},{28,24},{1,29},{... | collective-permute-start | bytes 2359304 | tf_op jit(solution)/shard_map/ppermute | solution.py:100
  29.0 21.7 %collective-permute-start.7 = (bf16[16,64,384]{2,1,0:T(8,128)(2,1)S(1)}, bf16[16,64,384]{2,1,0:T(8,128)(2,1)S(1)}, u32[]{:S(2)}, u32[]{:S(2)}) collective-permute-start(bf16[16,64,384]{2,1,0:T(8,128)(2,1)S(1)} %collective-permute-done.1.refs_8_), channel_id=1, source_target_pairs={{0,4},{4,8},{8,12},{12,16},{16,20},{20,24},{24,28},{28,0},{1,5},{5... | collective-permute-start | bytes 2359304 | tf_op jit(solution)/shard_map/ppermute | solution.py:97
  31.0 17.8 %collective-permute-start.2 = (bf16[16,128,128]{2,1,0:T(8,128)(2,1)S(1)}, bf16[16,128,128]{2,1,0:T(8,128)(2,1)S(1)}, u32[]{:S(2)}, u32[]{:S(2)}) collective-permute-start(bf16[16,128,128]{2,1,0:T(8,128)(2,1)S(1)} %collective-permute-done.refs_0_), channel_id=1, source_target_pairs={{0,64},{64,128},{128,192},{192,256},{256,320},{320,384},{384,448},... | collective-permute-start | bytes 1572872 | tf_op jit(solution)/shard_map/ppermute | solution.py:97
  34.2 20.0 %collective-permute-start.5 = (bf16[16,128,128]{2,1,0:T(8,128)(2,1)S(1)}, bf16[16,128,128]{2,1,0:T(8,128)(2,1)S(1)}, u32[]{:S(2)}, u32[]{:S(2)}) collective-permute-start(bf16[16,128,128]{2,1,0:T(8,128)(2,1)S(1)} %collective-permute-done.refs_0_), channel_id=1, source_target_pairs={{0,448},{64,0},{128,64},{192,128},{256,192},{320,256},{384,320},{4... | collective-permute-start | bytes 1572872 | tf_op jit(solution)/shard_map/ppermute | solution.py:100
  39.9 25.3 %collective-permute-start.11 = (bf16[16,64,384]{2,1,0:T(8,128)(2,1)S(1)}, bf16[16,64,384]{2,1,0:T(8,128)(2,1)S(1)}, u32[]{:S(2)}, u32[]{:S(2)}) collective-permute-start(bf16[16,64,384]{2,1,0:T(8,128)(2,1)S(1)} %collective-permute-done.3.refs_11_), channel_id=1, source_target_pairs={{0,28},{4,0},{8,4},{12,8},{16,12},{20,16},{24,20},{28,24},{1,29},{... | collective-permute-start | bytes 2359304 | tf_op jit(solution)/shard_map/ppermute | solution.py:100
  48.8 14.4 %collective-permute-start.4 = (bf16[16,128,128]{2,1,0:T(8,128)(2,1)S(1)}, bf16[16,128,128]{2,1,0:T(8,128)(2,1)S(1)}, u32[]{:S(2)}, u32[]{:S(2)}) collective-permute-start(bf16[16,128,128]{2,1,0:T(8,128)(2,1)S(1)} %collective-permute-done.2.refs_1_), channel_id=1, source_target_pairs={{0,64},{64,128},{128,192},{192,256},{256,320},{320,384},{384,448},... | collective-permute-start | bytes 1572872 | tf_op jit(solution)/shard_map/ppermute | solution.py:97
  50.7 24.4 %collective-permute-start.9 = (bf16[16,64,384]{2,1,0:T(8,128)(2,1)S(1)}, bf16[16,64,384]{2,1,0:T(8,128)(2,1)S(1)}, u32[]{:S(2)}, u32[]{:S(2)}) collective-permute-start(bf16[16,64,384]{2,1,0:T(8,128)(2,1)S(1)} %collective-permute-done.7.refs_9_), channel_id=1, source_target_pairs={{0,4},{4,8},{8,12},{12,16},{16,20},{20,24},{24,28},{28,0},{1,5},{5... | collective-permute-start | bytes 2359304 | tf_op jit(solution)/shard_map/ppermute | solution.py:97
  54.2 22.8 %collective-permute-start.8 = (bf16[16,128,128]{2,1,0:T(8,128)(2,1)S(1)}, bf16[16,128,128]{2,1,0:T(8,128)(2,1)S(1)}, u32[]{:S(2)}, u32[]{:S(2)}) collective-permute-start(bf16[16,128,128]{2,1,0:T(8,128)(2,1)S(1)} %collective-permute-done.5.refs_4_), channel_id=1, source_target_pairs={{0,448},{64,0},{128,64},{192,128},{256,192},{320,256},{384,320},{4... | collective-permute-start | bytes 1572872 | tf_op jit(solution)/shard_map/ppermute | solution.py:100
  63.2 18.1 %collective-permute-start.6 = (bf16[16,128,128]{2,1,0:T(8,128)(2,1)S(1)}, bf16[16,128,128]{2,1,0:T(8,128)(2,1)S(1)}, u32[]{:S(2)}, u32[]{:S(2)}) collective-permute-start(bf16[16,128,128]{2,1,0:T(8,128)(2,1)S(1)} %collective-permute-done.4.refs_2_), channel_id=1, source_target_pairs={{0,64},{64,128},{128,192},{192,256},{256,320},{320,384},{384,448},... | collective-permute-start | bytes 1572872 | tf_op jit(solution)/shard_map/ppermute | solution.py:97
  65.1 22.3 %collective-permute-start.12 = (bf16[16,64,384]{2,1,0:T(8,128)(2,1)S(1)}, bf16[16,64,384]{2,1,0:T(8,128)(2,1)S(1)}, u32[]{:S(2)}, u32[]{:S(2)}) collective-permute-start(bf16[16,64,384]{2,1,0:T(8,128)(2,1)S(1)} %collective-permute-done.11.refs_12_), channel_id=1, source_target_pairs={{0,28},{4,0},{8,4},{12,8},{16,12},{20,16},{24,20},{28,24},{1,29},{... | collective-permute-start | bytes 2359304 | tf_op jit(solution)/shard_map/ppermute | solution.py:100
  75.1 20.2 %collective-permute-start.14 = (bf16[16,64,384]{2,1,0:T(8,128)(2,1)S(1)}, bf16[16,64,384]{2,1,0:T(8,128)(2,1)S(1)}, u32[]{:S(2)}, u32[]{:S(2)}) collective-permute-start(bf16[16,64,384]{2,1,0:T(8,128)(2,1)S(1)} %collective-permute-done.9.refs_10_), channel_id=1, source_target_pairs={{0,4},{4,8},{8,12},{12,16},{16,20},{20,24},{24,28},{28,0},{1,5},{5... | collective-permute-start | bytes 2359304 | tf_op jit(solution)/shard_map/ppermute | solution.py:97
  77.0 12.5 %collective-permute-start.10 = (bf16[16,128,128]{2,1,0:T(8,128)(2,1)S(1)}, bf16[16,128,128]{2,1,0:T(8,128)(2,1)S(1)}, u32[]{:S(2)}, u32[]{:S(2)}) collective-permute-start(bf16[16,128,128]{2,1,0:T(8,128)(2,1)S(1)} %collective-permute-done.8.refs_5_), channel_id=1, source_target_pairs={{0,448},{64,0},{128,64},{192,128},{256,192},{320,256},{384,320},{4... | collective-permute-start | bytes 1572872 | tf_op jit(solution)/shard_map/ppermute | solution.py:100
  81.3 14.0 %collective-permute-start.13 = (bf16[16,128,128]{2,1,0:T(8,128)(2,1)S(1)}, bf16[16,128,128]{2,1,0:T(8,128)(2,1)S(1)}, u32[]{:S(2)}, u32[]{:S(2)}) collective-permute-start(bf16[16,128,128]{2,1,0:T(8,128)(2,1)S(1)} %collective-permute-done.6.refs_3_), channel_id=1, source_target_pairs={{0,64},{64,128},{128,192},{192,256},{256,320},{320,384},{384,448},... | collective-permute-start | bytes 1572872 | tf_op jit(solution)/shard_map/ppermute | solution.py:97
  89.5 1.1 copy-start
  95.3 17.8 %copy-start.1 = (bf16[96,128]{1,0:T(8,128)(2,1)S(1)}, bf16[96,128]{1,0:T(8,128)(2,1)}, u32[]{:S(2)}) copy-start(bf16[96,128]{1,0:T(8,128)(2,1)} %param.7) | copy-start | bytes 73732
  95.3 17.8 %copy-start.2 = (f32[128]{0:T(128)S(1)}, f32[128]{0:T(128)}, u32[]{:S(2)}) copy-start(f32[128]{0:T(128)} %param.9) | copy-start | bytes 1540
  95.3 17.8 %copy-start.3 = (f32[96]{0:T(128)S(1)}, f32[96]{0:T(128)}, u32[]{:S(2)}) copy-start(f32[96]{0:T(128)} %param.8) | copy-start | bytes 1156

commit v6 on v5

v6 whole, which is shorter than its diff:
```python
import jax
import jax.numpy as jnp
from jax import lax
from jax.experimental import pallas as pl
from jax.experimental.pallas import tpu as pltpu
from jax.sharding import Mesh, PartitionSpec as P

UP = [(i, (i + 1) % 8) for i in range(8)]
DOWN = [(i, (i - 1) % 8) for i in range(8)]
TRADE = [
    (2 * y + x, 2 * y + x if y // 4 == x else 2 * (7 - y) + 1 - x) for y in range(8) for x in range(2)
]
SHIFTS = (0, -1, -2, -3, 1, 2)
LATE = (3, 4)
ANY = pl.BlockSpec(memory_space=pl.ANY)
SMEM = pl.BlockSpec(memory_space=pltpu.SMEM)
VMEM = pl.BlockSpec(memory_space=pltpu.VMEM)
FLOAT = jnp.float32


def columns(amp_ref, slot, source):
    rows = pl.ds(pl.multiple_of(lax.rem(source, 2) * 64, 64), 64)
    return amp_ref[slot, :, rows, :].reshape(1024, 128)


def times(amp, block):
    return lax.dot_general(
        amp, block.reshape(1024, 384), (((0,), (0,)), ((), ())), preferred_element_type=FLOAT
    )


def piece(x, amp_ref, source, block):
    y = x * 4 + source // 2
    return times(
        jnp.concatenate([columns(amp_ref, slot, source) for slot in (y, 7 - y)], axis=1), block
    )


def early_kernel(place, *refs):
    count = len(SHIFTS)
    amps, blocks, (amp, held, out, sems) = refs[:count], refs[count : 2 * count], refs[2 * count :]
    x, y, z = place[0], place[1], place[2]
    turns = [lax.rem(shift + 8, 8) for shift in SHIFTS]
    copies = [
        pltpu.make_async_copy(ref, amp.at[lax.rem(y + turn, 8)], sems.at[j])
        for j, (ref, turn) in enumerate(zip(amps, turns))
    ] + [
        pltpu.make_async_copy(ref, held.at[lax.rem(z + turn, 8)], sems.at[count + j])
        for j, (ref, turn) in enumerate(zip(blocks, turns))
    ]
    for copy in copies:
        copy.start()
    for turn in LATE:
        amp[lax.rem(y + turn, 8)] = jnp.zeros((16, 128, 128), jnp.bfloat16)
    for copy in copies[:count]:
        copy.wait()
    total = None
    for j, turn in enumerate(turns):
        copies[count + j].wait()
        source = lax.rem(z + turn, 8)
        part = piece(x, amp, source, held[source])
        total = part if total is None else total + part
    out[...] = total


def late_kernel(place, early, amp_in, held, *refs):
    count = len(LATE)
    amps, blocks, (out, total) = refs[:count], refs[count : 2 * count], refs[2 * count :]
    x, y, z = place[0], place[1], place[2]
    slots = [lax.rem(y + turn, 8) for turn in LATE]
    sources = [lax.rem(z + turn, 8) for turn in LATE]

    def either(at, source):
        amp = columns(amp_in, at, source)
        for slot, ref in zip(slots, amps):
            amp = jnp.where(at == slot, columns(ref, 0, source), amp)
        return amp

    new = early[...]
    for source, ref in zip(sources, blocks):
        at = x * 4 + source // 2
        pair = jnp.concatenate([either(at, source), either(7 - at, source)], axis=1)
        new = new + times(pair, ref[...])
    total[...] = new
    for slot, ref in zip(slots, amps):
        other = jnp.where(slot // 4 == x, 0, 1)
        first = lax.rem(jnp.where(other == 0, slot, 7 - slot), 4) * 2
        for source in (first, first + 1):
            fresh = source != sources[0]
            for late in sources[1:]:
                fresh &= source != late

            @pl.when(fresh)
            def _():
                at = pl.ds(pl.multiple_of(other * 128, 128), 128)
                total[at, :] += times(columns(ref, 0, source), held[source])

    for n in range(2):
        out[lax.rem(x + n, 2)] = total[n * 128 : (n + 1) * 128].T


def after(block, *arrived):
    return lax.optimization_barrier((block,) + arrived)[0]


def local(integrals, amplitudes, coulomb, row_gap, col_gap):
    place = jnp.stack([lax.axis_index(a) for a in ("xl", "y", "z")])
    place, integrals, amplitudes = lax.optimization_barrier((place, integrals, amplitudes))

    def up(block, axis, *arrived):
        return lax.ppermute(after(block, *arrived), axis, UP)

    def down(block, axis, *arrived):
        return lax.ppermute(after(block, *arrived), axis, DOWN)

    i0 = integrals
    iu1 = up(i0, "z")
    a0 = lax.ppermute(amplitudes, ("y", "xl"), TRADE)
    id1 = down(i0, "z")
    iu2 = up(iu1, "z")
    au1 = up(a0, "y")
    id2 = down(id1, "z")
    ad1 = down(a0, "y", id1)
    au2 = up(au1, "y")
    iu3 = up(iu2, "z")
    ad2 = down(ad1, "y")
    id3 = down(id2, "z")
    au3 = up(au2, "y")
    iu4 = up(iu3, "z")
    ad3 = down(ad2, "y")
    au4 = up(au3, "y")
    held_shape = jax.ShapeDtypeStruct((8, 16, 64, 384), jnp.bfloat16)
    amp_shape = jax.ShapeDtypeStruct((8, 16, 128, 128), jnp.bfloat16)
    amp, held, early = pl.pallas_call(
        early_kernel,
        out_shape=(amp_shape, held_shape, jax.ShapeDtypeStruct((256, 384), FLOAT)),
        in_specs=[SMEM] + [ANY] * 12,
        out_specs=(VMEM, VMEM, VMEM),
        scratch_shapes=[pltpu.SemaphoreType.DMA((12,))],
        compiler_params=pltpu.CompilerParams(vmem_limit_bytes=24 << 20),
        cost_estimate=pl.CostEstimate(flops=1 << 30, bytes_accessed=16 << 20, transcendentals=0),
    )(place, a0, au1, au2, au3, ad1, ad2, i0, iu1, iu2, iu3, id1, id2)
    shares = pl.pallas_call(
        late_kernel,
        out_shape=jax.ShapeDtypeStruct((2, 384, 128), FLOAT),
        in_specs=[SMEM] + [VMEM] * 7,
        out_specs=VMEM,
        scratch_shapes=[pltpu.VMEM((256, 384), FLOAT)],
        compiler_params=pltpu.CompilerParams(vmem_limit_bytes=8 << 20),
    )(place, early, amp, held, ad3[None], au4[None], id3, iu4)
    shares = lax.all_to_all(
        shares.reshape(8, 96, 128), ("xl", "xh", "core"), 0, 0, tiled=True
    )
    own = jnp.sum(shares, axis=0)
    gap_sum = row_gap[:, None] + col_gap[None, :]
    return (coulomb.astype(FLOAT) + own) / gap_sum


def solution(mesh):
    fine = Mesh(mesh.devices.reshape(8, 2, 8, 2, 2), ("y", "xl", "z", "xh", "core"))
    layer, col = ("xh", "core"), ("xl", "z")
    placed = (
        P(layer, col, "y"),
        P(layer, "y", col),
        P(("y",) + layer, col),
        P(("y",) + layer),
        P(col),
    )
    return jax.shard_map(
        local, mesh=fine, in_specs=placed, out_specs=P(("y",) + layer, col), check_vma=False
    )
```

time: 116 us -> 115 us (level); the launches traced: 114 us -> 114 us
    ppermute x6, waiting for transfers between devices: 6.25 us -> 0.99 us  [down(): return lax.ppermute(after(block, *arrived), axis, DOWN)]
    ppermute x8, waiting for transfers between devices: 19.6 us -> 24.5 us  [up(): return lax.ppermute(after(block, *arrived), axis, UP)]
where the time goes in v6:
time: 115 us; the launch traced here: 114 us
  starting transfers between devices  63.4 us (55%)
  waiting for transfers between devices  25.5 us (22%)
  blocking collectives  16.2 us (14%)
  Pallas kernels  6.98 us (6%)
    ppermute x6, starting transfers between devices, down(): return lax.ppermute(after(block, *arrived), axis, DOWN)  40.6 us
    ppermute x8, waiting for transfers between devices, up(): return lax.ppermute(after(block, *arrived), axis, UP)  24.5 us
    ppermute x8, starting transfers between devices, up(): return lax.ppermute(after(block, *arrived), axis, UP)  21.1 us
    all_to_all x1, blocking collectives, local(): lax.all_to_all(shares.reshape(8, 96, 128), ('xl', 'xh', 'core'), 0, 0, ti...  16.2 us
    pallas_call x1, Pallas kernels, local(): pl.pallas_call(early_kernel, out_shape=(amp_shape, held_shape, jax.ShapeD...  4.12 us
    pallas_call x1, Pallas kernels, local(): pl.pallas_call(late_kernel, out_shape=jax.ShapeDtypeStruct((2, 384, 128),...  2.85 us
  transfers between devices with their start and end apart: 15, of which 5 were waited for; matrix products, arithmetic and copies ran while one was open for 0% of the time, Pallas kernels for 4%

profile of v6, /device:TPU:1, one launch (start us, length us, event | category | flops | bytes accessed | tf_op | source)
XLA Modules:
  0.0 114.3 jit_solution(4993946239576672987)
XLA Ops:
  0.0 0.1 pad_add_fusion.place
  0.1 4.8 %collective-permute-start.7 = (bf16[16,64,384]{2,1,0:T(8,128)(2,1)}, bf16[16,64,384]{2,1,0:T(8,128)(2,1)S(1)}, u32[]{:S(2)}, u32[]{:S(2)}) collective-permute-start(bf16[16,64,384]{2,1,0:T(8,128)(2,1)} %refs_6_), channel_id=1, source_target_pairs={{0,4},{4,8},{8,12},{12,16},{16,20},{20,24},{24,28},{28,0},{1,5},{5... | collective-permute-start | bytes 2359304 | tf_op jit(solution)/shard_map/ppermute | solution.py:111
  4.9 1.7 %collective-permute-start = (bf16[16,128,128]{2,1,0:T(8,128)(2,1)}, bf16[16,128,128]{2,1,0:T(8,128)(2,1)S(1)}, u32[]{:S(2)}, u32[]{:S(2)}) collective-permute-start(bf16[16,128,128]{2,1,0:T(8,128)(2,1)} %param.6), channel_id=1, source_target_pairs={{0,0},{32,448},{64,64},{96,384},{128,128},{160,320},{192,192},{224... | collective-permute-start | bytes 1572872 | tf_op jit(solution)/shard_map/ppermute | solution.py:118
  6.6 8.6 %collective-permute-start.4 = (bf16[16,64,384]{2,1,0:T(8,128)(2,1)}, bf16[16,64,384]{2,1,0:T(8,128)(2,1)S(1)}, u32[]{:S(2)}, u32[]{:S(2)}) collective-permute-start(bf16[16,64,384]{2,1,0:T(8,128)(2,1)} %refs_6_), channel_id=1, source_target_pairs={{0,28},{4,0},{8,4},{12,8},{16,12},{20,16},{24,20},{28,24},{1,29},{... | collective-permute-start | bytes 2359304 | tf_op jit(solution)/shard_map/ppermute | solution.py:114
  15.2 13.8 %collective-permute-done.7.refs_7_ = bf16[16,64,384]{2,1,0:T(8,128)(2,1)S(1)} collective-permute-done((bf16[16,64,384]{2,1,0:T(8,128)(2,1)}, bf16[16,64,384]{2,1,0:T(8,128)(2,1)S(1)}, u32[]{:S(2)}, u32[]{:S(2)}) %collective-permute-start.7) | collective-permute-done | bytes 786464 | tf_op jit(solution)/shard_map/ppermute | solution.py:111
  29.0 1.9 %collective-permute-start.8 = (bf16[16,64,384]{2,1,0:T(8,128)(2,1)S(1)}, bf16[16,64,384]{2,1,0:T(8,128)(2,1)S(1)}, u32[]{:S(2)}, u32[]{:S(2)}) collective-permute-start(bf16[16,64,384]{2,1,0:T(8,128)(2,1)S(1)} %collective-permute-done.7.refs_7_), channel_id=1, source_target_pairs={{0,4},{4,8},{8,12},{12,16},{16,20},{20,24},{24,28},{28,0},{1,5},{5... | collective-permute-start | bytes 2359304 | tf_op jit(solution)/shard_map/ppermute | solution.py:111
  31.0 0.0 collective-permute-done.refs_0_
  31.0 3.2 %collective-permute-start.1 = (bf16[16,128,128]{2,1,0:T(8,128)(2,1)S(1)}, bf16[16,128,128]{2,1,0:T(8,128)(2,1)S(1)}, u32[]{:S(2)}, u32[]{:S(2)}) collective-permute-start(bf16[16,128,128]{2,1,0:T(8,128)(2,1)S(1)} %collective-permute-done.refs_0_), channel_id=1, source_target_pairs={{0,64},{64,128},{128,192},{192,256},{256,320},{320,384},{384,448},... | collective-permute-start | bytes 1572872 | tf_op jit(solution)/shard_map/ppermute | solution.py:111
  34.2 0.0 collective-permute-done.4.refs_10_
  34.2 5.7 %collective-permute-start.5 = (bf16[16,128,128]{2,1,0:T(8,128)(2,1)S(1)}, bf16[16,128,128]{2,1,0:T(8,128)(2,1)S(1)}, u32[]{:S(2)}, u32[]{:S(2)}) collective-permute-start(bf16[16,128,128]{2,1,0:T(8,128)(2,1)S(1)} %collective-permute-done.refs_0_), channel_id=1, source_target_pairs={{0,448},{64,0},{128,64},{192,128},{256,192},{320,256},{384,320},{4... | collective-permute-start | bytes 1572872 | tf_op jit(solution)/shard_map/ppermute | solution.py:114
  39.9 8.9 %collective-permute-start.10 = (bf16[16,64,384]{2,1,0:T(8,128)(2,1)S(1)}, bf16[16,64,384]{2,1,0:T(8,128)(2,1)S(1)}, u32[]{:S(2)}, u32[]{:S(2)}) collective-permute-start(bf16[16,64,384]{2,1,0:T(8,128)(2,1)S(1)} %collective-permute-done.4.refs_10_), channel_id=1, source_target_pairs={{0,28},{4,0},{8,4},{12,8},{16,12},{20,16},{24,20},{28,24},{1,29},{... | collective-permute-start | bytes 2359304 | tf_op jit(solution)/shard_map/ppermute | solution.py:114
  48.8 1.9 %collective-permute-start.2 = (bf16[16,128,128]{2,1,0:T(8,128)(2,1)S(1)}, bf16[16,128,128]{2,1,0:T(8,128)(2,1)S(1)}, u32[]{:S(2)}, u32[]{:S(2)}) collective-permute-start(bf16[16,128,128]{2,1,0:T(8,128)(2,1)S(1)} %collective-permute-done.1.refs_1_), channel_id=1, source_target_pairs={{0,64},{64,128},{128,192},{192,256},{256,320},{320,384},{384,448},... | collective-permute-start | bytes 1572872 | tf_op jit(solution)/shard_map/ppermute | solution.py:111
  50.7 0.0 collective-permute-done.8.refs_8_
  50.7 3.5 %collective-permute-start.9 = (bf16[16,64,384]{2,1,0:T(8,128)(2,1)S(1)}, bf16[16,64,384]{2,1,0:T(8,128)(2,1)S(1)}, u32[]{:S(2)}, u32[]{:S(2)}) collective-permute-start(bf16[16,64,384]{2,1,0:T(8,128)(2,1)S(1)} %collective-permute-done.8.refs_8_), channel_id=1, source_target_pairs={{0,4},{4,8},{8,12},{12,16},{16,20},{20,24},{24,28},{28,0},{1,5},{5... | collective-permute-start | bytes 2359304 | tf_op jit(solution)/shard_map/ppermute | solution.py:111
  54.2 0.0 collective-permute-done.5.refs_4_
  54.2 4.6 %collective-permute-start.6 = (bf16[16,128,128]{2,1,0:T(8,128)(2,1)S(1)}, bf16[16,128,128]{2,1,0:T(8,128)(2,1)S(1)}, u32[]{:S(2)}, u32[]{:S(2)}) collective-permute-start(bf16[16,128,128]{2,1,0:T(8,128)(2,1)S(1)} %collective-permute-done.5.refs_4_), channel_id=1, source_target_pairs={{0,448},{64,0},{128,64},{192,128},{256,192},{320,256},{384,320},{4... | collective-permute-start | bytes 1572872 | tf_op jit(solution)/shard_map/ppermute | solution.py:114
  58.8 4.4 %collective-permute-done.2.refs_2_ = bf16[16,128,128]{2,1,0:T(8,128)(2,1)S(1)} collective-permute-done((bf16[16,128,128]{2,1,0:T(8,128)(2,1)S(1)}, bf16[16,128,128]{2,1,0:T(8,128)(2,1)S(1)}, u32[]{:S(2)}, u32[]{:S(2)}) %collective-permute-start.2) | collective-permute-done | bytes 524320 | tf_op jit(solution)/shard_map/ppermute | solution.py:111
  63.2 1.9 %collective-permute-start.3 = (bf16[16,128,128]{2,1,0:T(8,128)(2,1)S(1)}, bf16[16,128,128]{2,1,0:T(8,128)(2,1)S(1)}, u32[]{:S(2)}, u32[]{:S(2)}) collective-permute-start(bf16[16,128,128]{2,1,0:T(8,128)(2,1)S(1)} %collective-permute-done.2.refs_2_), channel_id=1, source_target_pairs={{0,64},{64,128},{128,192},{192,256},{256,320},{320,384},{384,448},... | collective-permute-start | bytes 1572872 | tf_op jit(solution)/shard_map/ppermute | solution.py:111
  65.1 0.0 collective-permute-done.10.refs_11_
  65.1 8.6 %collective-permute-start.13 = (bf16[16,64,384]{2,1,0:T(8,128)(2,1)S(1)}, bf16[16,64,384]{2,1,0:T(8,128)(2,1)S(1)}, u32[]{:S(2)}, u32[]{:S(2)}) collective-permute-start(bf16[16,64,384]{2,1,0:T(8,128)(2,1)S(1)} %collective-permute-done.10.refs_11_), channel_id=1, source_target_pairs={{0,28},{4,0},{8,4},{12,8},{16,12},{20,16},{24,20},{28,24},{1,29},{... | collective-permute-start | bytes 2359304 | tf_op jit(solution)/shard_map/ppermute | solution.py:114
  73.8 1.3 %collective-permute-done.9.refs_9_ = bf16[16,64,384]{2,1,0:T(8,128)(2,1)S(1)} collective-permute-done((bf16[16,64,384]{2,1,0:T(8,128)(2,1)S(1)}, bf16[16,64,384]{2,1,0:T(8,128)(2,1)S(1)}, u32[]{:S(2)}, u32[]{:S(2)}) %collective-permute-start.9) | collective-permute-done | bytes 786464 | tf_op jit(solution)/shard_map/ppermute | solution.py:111
  75.1 1.9 %collective-permute-start.14 = (bf16[16,64,384]{2,1,0:T(8,128)(2,1)S(1)}, bf16[16,64,384]{2,1,0:T(8,128)(2,1)S(1)}, u32[]{:S(2)}, u32[]{:S(2)}) collective-permute-start(bf16[16,64,384]{2,1,0:T(8,128)(2,1)S(1)} %collective-permute-done.9.refs_9_), channel_id=1, source_target_pairs={{0,4},{4,8},{8,12},{12,16},{16,20},{20,24},{24,28},{28,0},{1,5},{5... | collective-permute-start | bytes 2359304 | tf_op jit(solution)/shard_map/ppermute | solution.py:111
  77.0 4.3 %collective-permute-start.11 = (bf16[16,128,128]{2,1,0:T(8,128)(2,1)S(1)}, bf16[16,128,128]{2,1,0:T(8,128)(2,1)S(1)}, u32[]{:S(2)}, u32[]{:S(2)}) collective-permute-start(bf16[16,128,128]{2,1,0:T(8,128)(2,1)S(1)} %collective-permute-done.6.refs_5_), channel_id=1, source_target_pairs={{0,448},{64,0},{128,64},{192,128},{256,192},{320,256},{384,320},{4... | collective-permute-start | bytes 1572872 | tf_op jit(solution)/shard_map/ppermute | solution.py:114
  81.3 1.9 %collective-permute-start.12 = (bf16[16,128,128]{2,1,0:T(8,128)(2,1)S(1)}, bf16[16,128,128]{2,1,0:T(8,128)(2,1)S(1)}, u32[]{:S(2)}, u32[]{:S(2)}) collective-permute-start(bf16[16,128,128]{2,1,0:T(8,128)(2,1)S(1)} %collective-permute-done.3.refs_3_), channel_id=1, source_target_pairs={{0,64},{64,128},{128,192},{192,256},{256,320},{320,384},{384,448},... | collective-permute-start | bytes 1572872 | tf_op jit(solution)/shard_map/ppermute | solution.py:111
  83.3 0.0 copy-start
  83.3 1.1 copy-done
  84.4 4.1 %shard_map.55 = (bf16[8,16,128,128]{3,2,1,0:T(8,128)(2,1)S(1)}, bf16[8,16,64,384]{3,2,1,0:T(8,128)(2,1)S(1)}, f32[256,384]{1,0:T(8,128)S(1)}) custom-call(s32[3]{0:T(128)S(1)} %pad_add_fusion.place, bf16[16,128,128]{2,1,0:T(8,128)(2,1)S(1)} %collective-permute-done.refs_0_, bf16[16,128,128]{2,1,0:T(8,128)(2,1)S(1)} %collective-permute-done.1.refs_1_, ...), custom_call_target="tpu_custom_call" | custom-call | flops 1073741824 | bytes 16777216 | tf_op jit(solution)/shard_map/pallas_call | solution.py:134
  88.5 1.0 collective-permute-done.11
  89.5 5.0 %collective-permute-done.12 = bf16[16,128,128]{2,1,0:T(8,128)(2,1)S(1)} collective-permute-done((bf16[16,128,128]{2,1,0:T(8,128)(2,1)S(1)}, bf16[16,128,128]{2,1,0:T(8,128)(2,1)S(1)}, u32[]{:S(2)}, u32[]{:S(2)}) %collective-permute-start.12) | collective-permute-done | bytes 524320 | tf_op jit(solution)/shard_map/ppermute | solution.py:111
  94.5 2.9 %shard_map.56 = f32[2,384,128]{2,1,0:T(8,128)S(1)} custom-call(s32[3]{0:T(128)S(1)} %pad_add_fusion.place, f32[256,384]{1,0:T(8,128)S(1)} %get-tuple-element.16.early, bf16[8,16,128,128]{3,2,1,0:T(8,128)(2,1)S(1)} %get-tuple-element.17.amp_in, bf16[8,16,64,384]{3,2,1,0:T(8,128)(2,1)S(1)} %get-tuple-element.18.held, bf16[1,16,128,128]{3,2,1,0:T(8,128)(2,1)S(1)} %bitcast.7, ...), custom_call_target="tpu_custom_call" | custom-call | tf_op jit(solution)/shard_map/pallas_call | solution.py:143
  97.3 16.2 %all_to_all.5 = f32[8,96,128]{2,1,0:T(8,128)S(1)} all-to-all(f32[8,96,128]{2,1,0:T(8,128)S(1)} %bitcast.6), channel_id=1, replica_groups=mesh['y'=8,'xl'=2,'z'=8,'xh'=2,'core'=2] {'xl','xh','core'}, dimensions={0} | all-to-all | bytes 786432 | tf_op jit(solution)/shard_map/all_to_all | solution.py:151
  113.6 0.7 add_divide_fusion
  (12 shorter events, 0.0 us)
Async XLA Ops:
  0.1 29.0 %collective-permute-start.7 = (bf16[16,64,384]{2,1,0:T(8,128)(2,1)}, bf16[16,64,384]{2,1,0:T(8,128)(2,1)S(1)}, u32[]{:S(2)}, u32[]{:S(2)}) collective-permute-start(bf16[16,64,384]{2,1,0:T(8,128)(2,1)} %refs_6_), channel_id=1, source_target_pairs={{0,4},{4,8},{8,12},{12,16},{16,20},{20,24},{24,28},{28,0},{1,5},{5... | collective-permute-start | bytes 2359304 | tf_op jit(solution)/shard_map/ppermute | solution.py:111
  4.9 26.0 %collective-permute-start = (bf16[16,128,128]{2,1,0:T(8,128)(2,1)}, bf16[16,128,128]{2,1,0:T(8,128)(2,1)S(1)}, u32[]{:S(2)}, u32[]{:S(2)}) collective-permute-start(bf16[16,128,128]{2,1,0:T(8,128)(2,1)} %param.6), channel_id=1, source_target_pairs={{0,0},{32,448},{64,64},{96,384},{128,128},{160,320},{192,192},{224... | collective-permute-start | bytes 1572872 | tf_op jit(solution)/shard_map/ppermute | solution.py:118
  6.6 27.6 %collective-permute-start.4 = (bf16[16,64,384]{2,1,0:T(8,128)(2,1)}, bf16[16,64,384]{2,1,0:T(8,128)(2,1)S(1)}, u32[]{:S(2)}, u32[]{:S(2)}) collective-permute-start(bf16[16,64,384]{2,1,0:T(8,128)(2,1)} %refs_6_), channel_id=1, source_target_pairs={{0,28},{4,0},{8,4},{12,8},{16,12},{20,16},{24,20},{28,24},{1,29},{... | collective-permute-start | bytes 2359304 | tf_op jit(solution)/shard_map/ppermute | solution.py:114
  29.0 21.7 %collective-permute-start.8 = (bf16[16,64,384]{2,1,0:T(8,128)(2,1)S(1)}, bf16[16,64,384]{2,1,0:T(8,128)(2,1)S(1)}, u32[]{:S(2)}, u32[]{:S(2)}) collective-permute-start(bf16[16,64,384]{2,1,0:T(8,128)(2,1)S(1)} %collective-permute-done.7.refs_7_), channel_id=1, source_target_pairs={{0,4},{4,8},{8,12},{12,16},{16,20},{20,24},{24,28},{28,0},{1,5},{5... | collective-permute-start | bytes 2359304 | tf_op jit(solution)/shard_map/ppermute | solution.py:111
  31.0 17.8 %collective-permute-start.1 = (bf16[16,128,128]{2,1,0:T(8,128)(2,1)S(1)}, bf16[16,128,128]{2,1,0:T(8,128)(2,1)S(1)}, u32[]{:S(2)}, u32[]{:S(2)}) collective-permute-start(bf16[16,128,128]{2,1,0:T(8,128)(2,1)S(1)} %collective-permute-done.refs_0_), channel_id=1, source_target_pairs={{0,64},{64,128},{128,192},{192,256},{256,320},{320,384},{384,448},... | collective-permute-start | bytes 1572872 | tf_op jit(solution)/shard_map/ppermute | solution.py:111
  34.2 20.0 %collective-permute-start.5 = (bf16[16,128,128]{2,1,0:T(8,128)(2,1)S(1)}, bf16[16,128,128]{2,1,0:T(8,128)(2,1)S(1)}, u32[]{:S(2)}, u32[]{:S(2)}) collective-permute-start(bf16[16,128,128]{2,1,0:T(8,128)(2,1)S(1)} %collective-permute-done.refs_0_), channel_id=1, source_target_pairs={{0,448},{64,0},{128,64},{192,128},{256,192},{320,256},{384,320},{4... | collective-permute-start | bytes 1572872 | tf_op jit(solution)/shard_map/ppermute | solution.py:114
  39.9 25.3 %collective-permute-start.10 = (bf16[16,64,384]{2,1,0:T(8,128)(2,1)S(1)}, bf16[16,64,384]{2,1,0:T(8,128)(2,1)S(1)}, u32[]{:S(2)}, u32[]{:S(2)}) collective-permute-start(bf16[16,64,384]{2,1,0:T(8,128)(2,1)S(1)} %collective-permute-done.4.refs_10_), channel_id=1, source_target_pairs={{0,28},{4,0},{8,4},{12,8},{16,12},{20,16},{24,20},{28,24},{1,29},{... | collective-permute-start | bytes 2359304 | tf_op jit(solution)/shard_map/ppermute | solution.py:114
  48.8 14.4 %collective-permute-start.2 = (bf16[16,128,128]{2,1,0:T(8,128)(2,1)S(1)}, bf16[16,128,128]{2,1,0:T(8,128)(2,1)S(1)}, u32[]{:S(2)}, u32[]{:S(2)}) collective-permute-start(bf16[16,128,128]{2,1,0:T(8,128)(2,1)S(1)} %collective-permute-done.1.refs_1_), channel_id=1, source_target_pairs={{0,64},{64,128},{128,192},{192,256},{256,320},{320,384},{384,448},... | collective-permute-start | bytes 1572872 | tf_op jit(solution)/shard_map/ppermute | solution.py:111
  50.7 24.4 %collective-permute-start.9 = (bf16[16,64,384]{2,1,0:T(8,128)(2,1)S(1)}, bf16[16,64,384]{2,1,0:T(8,128)(2,1)S(1)}, u32[]{:S(2)}, u32[]{:S(2)}) collective-permute-start(bf16[16,64,384]{2,1,0:T(8,128)(2,1)S(1)} %collective-permute-done.8.refs_8_), channel_id=1, source_target_pairs={{0,4},{4,8},{8,12},{12,16},{16,20},{20,24},{24,28},{28,0},{1,5},{5... | collective-permute-start | bytes 2359304 | tf_op jit(solution)/shard_map/ppermute | solution.py:111
  54.2 22.8 %collective-permute-start.6 = (bf16[16,128,128]{2,1,0:T(8,128)(2,1)S(1)}, bf16[16,128,128]{2,1,0:T(8,128)(2,1)S(1)}, u32[]{:S(2)}, u32[]{:S(2)}) collective-permute-start(bf16[16,128,128]{2,1,0:T(8,128)(2,1)S(1)} %collective-permute-done.5.refs_4_), channel_id=1, source_target_pairs={{0,448},{64,0},{128,64},{192,128},{256,192},{320,256},{384,320},{4... | collective-permute-start | bytes 1572872 | tf_op jit(solution)/shard_map/ppermute | solution.py:114
  63.2 18.1 %collective-permute-start.3 = (bf16[16,128,128]{2,1,0:T(8,128)(2,1)S(1)}, bf16[16,128,128]{2,1,0:T(8,128)(2,1)S(1)}, u32[]{:S(2)}, u32[]{:S(2)}) collective-permute-start(bf16[16,128,128]{2,1,0:T(8,128)(2,1)S(1)} %collective-permute-done.2.refs_2_), channel_id=1, source_target_pairs={{0,64},{64,128},{128,192},{192,256},{256,320},{320,384},{384,448},... | collective-permute-start | bytes 1572872 | tf_op jit(solution)/shard_map/ppermute | solution.py:111
  65.1 24.4 %collective-permute-start.13 = (bf16[16,64,384]{2,1,0:T(8,128)(2,1)S(1)}, bf16[16,64,384]{2,1,0:T(8,128)(2,1)S(1)}, u32[]{:S(2)}, u32[]{:S(2)}) collective-permute-start(bf16[16,64,384]{2,1,0:T(8,128)(2,1)S(1)} %collective-permute-done.10.refs_11_), channel_id=1, source_target_pairs={{0,28},{4,0},{8,4},{12,8},{16,12},{20,16},{24,20},{28,24},{1,29},{... | collective-permute-start | bytes 2359304 | tf_op jit(solution)/shard_map/ppermute | solution.py:114
  75.1 19.4 %collective-permute-start.14 = (bf16[16,64,384]{2,1,0:T(8,128)(2,1)S(1)}, bf16[16,64,384]{2,1,0:T(8,128)(2,1)S(1)}, u32[]{:S(2)}, u32[]{:S(2)}) collective-permute-start(bf16[16,64,384]{2,1,0:T(8,128)(2,1)S(1)} %collective-permute-done.9.refs_9_), channel_id=1, source_target_pairs={{0,4},{4,8},{8,12},{12,16},{16,20},{20,24},{24,28},{28,0},{1,5},{5... | collective-permute-start | bytes 2359304 | tf_op jit(solution)/shard_map/ppermute | solution.py:111
  77.0 12.5 %collective-permute-start.11 = (bf16[16,128,128]{2,1,0:T(8,128)(2,1)S(1)}, bf16[16,128,128]{2,1,0:T(8,128)(2,1)S(1)}, u32[]{:S(2)}, u32[]{:S(2)}) collective-permute-start(bf16[16,128,128]{2,1,0:T(8,128)(2,1)S(1)} %collective-permute-done.6.refs_5_), channel_id=1, source_target_pairs={{0,448},{64,0},{128,64},{192,128},{256,192},{320,256},{384,320},{4... | collective-permute-start | bytes 1572872 | tf_op jit(solution)/shard_map/ppermute | solution.py:114
  81.3 13.1 %collective-permute-start.12 = (bf16[16,128,128]{2,1,0:T(8,128)(2,1)S(1)}, bf16[16,128,128]{2,1,0:T(8,128)(2,1)S(1)}, u32[]{:S(2)}, u32[]{:S(2)}) collective-permute-start(bf16[16,128,128]{2,1,0:T(8,128)(2,1)S(1)} %collective-permute-done.3.refs_3_), channel_id=1, source_target_pairs={{0,64},{64,128},{128,192},{192,256},{256,320},{320,384},{384,448},... | collective-permute-start | bytes 1572872 | tf_op jit(solution)/shard_map/ppermute | solution.py:111
  83.3 1.1 copy-start
  94.5 19.1 %copy-start.1 = (bf16[96,128]{1,0:T(8,128)(2,1)S(1)}, bf16[96,128]{1,0:T(8,128)(2,1)}, u32[]{:S(2)}) copy-start(bf16[96,128]{1,0:T(8,128)(2,1)} %param.7) | copy-start | bytes 73732
  94.5 19.1 %copy-start.2 = (f32[128]{0:T(128)S(1)}, f32[128]{0:T(128)}, u32[]{:S(2)}) copy-start(f32[128]{0:T(128)} %param.9) | copy-start | bytes 1540
  94.5 19.1 %copy-start.3 = (f32[96]{0:T(128)S(1)}, f32[96]{0:T(128)}, u32[]{:S(2)}) copy-start(f32[96]{0:T(128)} %param.8) | copy-start | bytes 1156

commit v7 on v6

--- a/solution.py
+++ b/solution.py
@@ -5,8 +5,8 @@
 from jax.experimental.pallas import tpu as pltpu
 from jax.sharding import Mesh, PartitionSpec as P
 
-UP = [(i, (i + 1) % 8) for i in range(8)]
-DOWN = [(i, (i - 1) % 8) for i in range(8)]
+FORTH = [(2 * i + c, 2 * ((i + 1 - 2 * c) % 8) + c) for i in range(8) for c in range(2)]
+BACK = [(j, i) for i, j in FORTH]
 TRADE = [
     (2 * y + x, 2 * y + x if y // 4 == x else 2 * (7 - y) + 1 - x) for y in range(8) for x in range(2)
 ]
@@ -39,8 +39,8 @@
 def early_kernel(place, *refs):
     count = len(SHIFTS)
     amps, blocks, (amp, held, out, sems) = refs[:count], refs[count : 2 * count], refs[2 * count :]
-    x, y, z = place[0], place[1], place[2]
-    turns = [lax.rem(shift + 8, 8) for shift in SHIFTS]
+    x, y, z, way = place[0], place[1], place[2], 1 - 2 * place[3]
+    turns = [lax.rem(way * shift + 8, 8) for shift in SHIFTS]
     copies = [
         pltpu.make_async_copy(ref, amp.at[lax.rem(y + turn, 8)], sems.at[j])
         for j, (ref, turn) in enumerate(zip(amps, turns))
@@ -51,7 +51,7 @@
     for copy in copies:
         copy.start()
     for turn in LATE:
-        amp[lax.rem(y + turn, 8)] = jnp.zeros((16, 128, 128), jnp.bfloat16)
+        amp[lax.rem(y + way * turn + 8, 8)] = jnp.zeros((16, 128, 128), jnp.bfloat16)
     for copy in copies[:count]:
         copy.wait()
     total = None
@@ -66,9 +66,9 @@
 def late_kernel(place, early, amp_in, held, *refs):
     count = len(LATE)
     amps, blocks, (out, total) = refs[:count], refs[count : 2 * count], refs[2 * count :]
-    x, y, z = place[0], place[1], place[2]
-    slots = [lax.rem(y + turn, 8) for turn in LATE]
-    sources = [lax.rem(z + turn, 8) for turn in LATE]
+    x, y, z, way = place[0], place[1], place[2], 1 - 2 * place[3]
+    slots = [lax.rem(y + way * turn + 8, 8) for turn in LATE]
+    sources = [lax.rem(z + way * turn + 8, 8) for turn in LATE]
 
     def either(at, source):
         amp = columns(amp_in, at, source)
@@ -104,31 +104,31 @@
 
 
 def local(integrals, amplitudes, coulomb, row_gap, col_gap):
-    place = jnp.stack([lax.axis_index(a) for a in ("xl", "y", "z")])
+    place = jnp.stack([lax.axis_index(a) for a in ("xl", "y", "z", "core")])
     place, integrals, amplitudes = lax.optimization_barrier((place, integrals, amplitudes))
 
-    def up(block, axis, *arrived):
-        return lax.ppermute(after(block, *arrived), axis, UP)
+    def forth(block, axis, *arrived):
+        return lax.ppermute(after(block, *arrived), (axis, "core"), FORTH)
 
-    def down(block, axis, *arrived):
-        return lax.ppermute(after(block, *arrived), axis, DOWN)
+    def back(block, axis, *arrived):
+        return lax.ppermute(after(block, *arrived), (axis, "core"), BACK)
 
     i0 = integrals
-    iu1 = up(i0, "z")
+    iu1 = forth(i0, "z")
     a0 = lax.ppermute(amplitudes, ("y", "xl"), TRADE)
-    id1 = down(i0, "z")
-    iu2 = up(iu1, "z")
-    au1 = up(a0, "y")
-    id2 = down(id1, "z")
-    ad1 = down(a0, "y", id1)
-    au2 = up(au1, "y")
-    iu3 = up(iu2, "z")
-    ad2 = down(ad1, "y")
-    id3 = down(id2, "z")
-    au3 = up(au2, "y")
-    iu4 = up(iu3, "z")
-    ad3 = down(ad2, "y")
-    au4 = up(au3, "y")
+    id1 = back(i0, "z")
+    iu2 = forth(iu1, "z")
+    au1 = forth(a0, "y", iu1)
+    ad1 = back(a0, "y", iu1)
+    id2 = back(id1, "z", a0)
+    au2 = forth(au1, "y", id1)
+    iu3 = forth(iu2, "z", au1)
+    id3 = back(id2, "z", iu2)
+    au3 = forth(au2, "y", id2)
+    ad2 = back(ad1, "y", au2)
+    iu4 = forth(iu3, "z", ad1)
+    au4 = forth(au3, "y", iu3)
+    ad3 = back(ad2, "y", au3)
     held_shape = jax.ShapeDtypeStruct((8, 16, 64, 384), jnp.bfloat16)
     amp_shape = jax.ShapeDtypeStruct((8, 16, 128, 128), jnp.bfloat16)
     amp, held, early = pl.pallas_call(

time: 115 us -> 115 us (level)
  starting transfers between devices: 63.4 us -> 67.9 us
  blocking collectives: 16.2 us -> 13.5 us
  waiting for transfers between devices: 25.5 us -> 24.1 us
    ppermute x14, starting transfers between devices: 61.7 us -> 66.2 us  [the longest x8 54.7 us: forth(): return lax.ppermute(after(block, *arrived), (axis, 'core'), FORTH)]
    all_to_all x1, blocking collectives: 16.2 us -> 13.5 us  [local(): lax.all_to_all(shares.reshape(8, 96, 128), ('xl', 'xh', 'core'), 0, 0, ti...]
    ppermute x14, waiting for transfers between devices: 25.5 us -> 24.1 us  [the longest x8 23.5 us: forth(): return lax.ppermute(after(block, *arrived), (axis, 'core'), FORTH)]
  transfers between devices with their start and end apart: 15 -> 15, of which waited for: 5 -> 6; matrix products, arithmetic and copies ran while one was open for 0% -> 0% of each run, Pallas kernels for 4% -> 4%
where the time goes in v7:
time: 115 us; the launch traced here: 114 us
  starting transfers between devices  67.9 us (59%)
  waiting for transfers between devices  24.1 us (21%)
  blocking collectives  13.5 us (12%)
  Pallas kernels  6.34 us (6%)
    ppermute x8, starting transfers between devices, forth(): return lax.ppermute(after(block, *arrived), (axis, 'core'), FORTH)  54.7 us
    ppermute x8, waiting for transfers between devices, forth(): return lax.ppermute(after(block, *arrived), (axis, 'core'), FORTH)  23.5 us
    all_to_all x1, blocking collectives, local(): lax.all_to_all(shares.reshape(8, 96, 128), ('xl', 'xh', 'core'), 0, 0, ti...  13.5 us
    ppermute x6, starting transfers between devices, back(): return lax.ppermute(after(block, *arrived), (axis, 'core'), BACK)  11.5 us
    pallas_call x1, Pallas kernels, local(): pl.pallas_call(early_kernel, out_shape=(amp_shape, held_shape, jax.ShapeD...  4.13 us
  transfers between devices with their start and end apart: 15, of which 6 were waited for; matrix products, arithmetic and copies ran while one was open for 0% of the time, Pallas kernels for 4%

profile of v7, /device:TPU:1, one launch (start us, length us, event | category | flops | bytes accessed | tf_op | source)
XLA Modules:
  0.0 114.0 jit_solution(17454654004439360081)
XLA Ops:
  0.0 0.1 pad_add_fusion.place
  0.1 11.5 %collective-permute-start.1 = (bf16[16,64,384]{2,1,0:T(8,128)(2,1)}, bf16[16,64,384]{2,1,0:T(8,128)(2,1)S(1)}, u32[]{:S(2)}, u32[]{:S(2)}) collective-permute-start(bf16[16,64,384]{2,1,0:T(8,128)(2,1)} %refs_6_), channel_id=1, source_target_pairs={{0,4},{1,29},{4,8},{5,1},{8,12},{9,5},{12,16},{13,9},{16,20},{17,1... | collective-permute-start | bytes 2359304 | tf_op jit(solution)/shard_map/ppermute | solution.py:111
  11.6 1.7 %collective-permute-start = (bf16[16,128,128]{2,1,0:T(8,128)(2,1)}, bf16[16,128,128]{2,1,0:T(8,128)(2,1)S(1)}, u32[]{:S(2)}, u32[]{:S(2)}) collective-permute-start(bf16[16,128,128]{2,1,0:T(8,128)(2,1)} %param.6), channel_id=1, source_target_pairs={{0,0},{32,448},{64,64},{96,384},{128,128},{160,320},{192,192},{224... | collective-permute-start | bytes 1572872 | tf_op jit(solution)/shard_map/ppermute | solution.py:118
  13.3 1.9 %collective-permute-start.3 = (bf16[16,64,384]{2,1,0:T(8,128)(2,1)}, bf16[16,64,384]{2,1,0:T(8,128)(2,1)S(1)}, u32[]{:S(2)}, u32[]{:S(2)}) collective-permute-start(bf16[16,64,384]{2,1,0:T(8,128)(2,1)} %refs_6_), channel_id=1, source_target_pairs={{4,0},{29,1},{8,4},{1,5},{12,8},{5,9},{16,12},{9,13},{20,16},{13,1... | collective-permute-start | bytes 2359304 | tf_op jit(solution)/shard_map/ppermute | solution.py:114
  15.2 9.2 %collective-permute-done.1.refs_7_ = bf16[16,64,384]{2,1,0:T(8,128)(2,1)S(1)} collective-permute-done((bf16[16,64,384]{2,1,0:T(8,128)(2,1)}, bf16[16,64,384]{2,1,0:T(8,128)(2,1)S(1)}, u32[]{:S(2)}, u32[]{:S(2)}) %collective-permute-start.1) | collective-permute-done | bytes 786464 | tf_op jit(solution)/shard_map/ppermute | solution.py:111
  24.4 5.2 %collective-permute-start.9 = (bf16[16,64,384]{2,1,0:T(8,128)(2,1)S(1)}, bf16[16,64,384]{2,1,0:T(8,128)(2,1)S(1)}, u32[]{:S(2)}, u32[]{:S(2)}) collective-permute-start(bf16[16,64,384]{2,1,0:T(8,128)(2,1)S(1)} %collective-permute-done.1.refs_7_), channel_id=1, source_target_pairs={{0,4},{1,29},{4,8},{5,1},{8,12},{9,5},{12,16},{13,9},{16,20},{17,1... | collective-permute-start | bytes 2359304 | tf_op jit(solution)/shard_map/ppermute | solution.py:111
  29.6 10.9 %collective-permute-start.2 = (bf16[16,128,128]{2,1,0:T(8,128)(2,1)S(1)}, bf16[16,128,128]{2,1,0:T(8,128)(2,1)S(1)}, u32[]{:S(2)}, u32[]{:S(2)}) collective-permute-start(bf16[16,128,128]{2,1,0:T(8,128)(2,1)S(1)} %collective-permute-done.refs_0_), channel_id=1, source_target_pairs={{0,64},{1,449},{64,128},{65,1},{128,192},{129,65},{192,256},{193,1... | collective-permute-start | bytes 1572872 | tf_op jit(solution)/shard_map/ppermute | solution.py:111
  40.5 0.0 collective-permute-done.3.refs_10_
  40.5 1.9 %collective-permute-start.5 = (bf16[16,64,384]{2,1,0:T(8,128)(2,1)S(1)}, bf16[16,64,384]{2,1,0:T(8,128)(2,1)S(1)}, u32[]{:S(2)}, u32[]{:S(2)}) collective-permute-start(bf16[16,64,384]{2,1,0:T(8,128)(2,1)S(1)} %collective-permute-done.3.refs_10_), channel_id=1, source_target_pairs={{4,0},{29,1},{8,4},{1,5},{12,8},{5,9},{16,12},{9,13},{20,16},{13,1... | collective-permute-start | bytes 2359304 | tf_op jit(solution)/shard_map/ppermute | solution.py:114
  42.5 1.9 %collective-permute-start.7 = (bf16[16,128,128]{2,1,0:T(8,128)(2,1)S(1)}, bf16[16,128,128]{2,1,0:T(8,128)(2,1)S(1)}, u32[]{:S(2)}, u32[]{:S(2)}) collective-permute-start(bf16[16,128,128]{2,1,0:T(8,128)(2,1)S(1)} %collective-permute-done.refs_0_), channel_id=1, source_target_pairs={{64,0},{449,1},{128,64},{1,65},{192,128},{65,129},{256,192},{129,1... | collective-permute-start | bytes 1572872 | tf_op jit(solution)/shard_map/ppermute | solution.py:114
  44.4 2.2 %collective-permute-done.2.refs_1_ = bf16[16,128,128]{2,1,0:T(8,128)(2,1)S(1)} collective-permute-done((bf16[16,128,128]{2,1,0:T(8,128)(2,1)S(1)}, bf16[16,128,128]{2,1,0:T(8,128)(2,1)S(1)}, u32[]{:S(2)}, u32[]{:S(2)}) %collective-permute-start.2) | collective-permute-done | bytes 524320 | tf_op jit(solution)/shard_map/ppermute | solution.py:111
  46.6 5.0 %collective-permute-start.4 = (bf16[16,128,128]{2,1,0:T(8,128)(2,1)S(1)}, bf16[16,128,128]{2,1,0:T(8,128)(2,1)S(1)}, u32[]{:S(2)}, u32[]{:S(2)}) collective-permute-start(bf16[16,128,128]{2,1,0:T(8,128)(2,1)S(1)} %collective-permute-done.2.refs_1_), channel_id=1, source_target_pairs={{0,64},{1,449},{64,128},{65,1},{128,192},{129,65},{192,256},{193,1... | collective-permute-start | bytes 1572872 | tf_op jit(solution)/shard_map/ppermute | solution.py:111
  51.6 0.0 collective-permute-done.9.refs_8_
  51.7 7.2 %collective-permute-start.10 = (bf16[16,64,384]{2,1,0:T(8,128)(2,1)S(1)}, bf16[16,64,384]{2,1,0:T(8,128)(2,1)S(1)}, u32[]{:S(2)}, u32[]{:S(2)}) collective-permute-start(bf16[16,64,384]{2,1,0:T(8,128)(2,1)S(1)} %collective-permute-done.9.refs_8_), channel_id=1, source_target_pairs={{0,4},{1,29},{4,8},{5,1},{8,12},{9,5},{12,16},{13,9},{16,20},{17,1... | collective-permute-start | bytes 2359304 | tf_op jit(solution)/shard_map/ppermute | solution.py:111
  58.8 0.0 collective-permute-done.7.refs_4_
  58.8 4.2 %collective-permute-done.4.refs_2_ = bf16[16,128,128]{2,1,0:T(8,128)(2,1)S(1)} collective-permute-done((bf16[16,128,128]{2,1,0:T(8,128)(2,1)S(1)}, bf16[16,128,128]{2,1,0:T(8,128)(2,1)S(1)}, u32[]{:S(2)}, u32[]{:S(2)}) %collective-permute-start.4) | collective-permute-done | bytes 524320 | tf_op jit(solution)/shard_map/ppermute | solution.py:111
  63.0 1.9 %collective-permute-start.8 = (bf16[16,128,128]{2,1,0:T(8,128)(2,1)S(1)}, bf16[16,128,128]{2,1,0:T(8,128)(2,1)S(1)}, u32[]{:S(2)}, u32[]{:S(2)}) collective-permute-start(bf16[16,128,128]{2,1,0:T(8,128)(2,1)S(1)} %collective-permute-done.7.refs_4_), channel_id=1, source_target_pairs={{64,0},{449,1},{128,64},{1,65},{192,128},{65,129},{256,192},{129,1... | collective-permute-start | bytes 1572872 | tf_op jit(solution)/shard_map/ppermute | solution.py:114
  65.0 0.0 collective-permute-done.5.refs_11_
  65.0 5.3 %collective-permute-start.6 = (bf16[16,128,128]{2,1,0:T(8,128)(2,1)S(1)}, bf16[16,128,128]{2,1,0:T(8,128)(2,1)S(1)}, u32[]{:S(2)}, u32[]{:S(2)}) collective-permute-start(bf16[16,128,128]{2,1,0:T(8,128)(2,1)S(1)} %collective-permute-done.4.refs_2_), channel_id=1, source_target_pairs={{0,64},{1,449},{64,128},{65,1},{128,192},{129,65},{192,256},{193,1... | collective-permute-start | bytes 1572872 | tf_op jit(solution)/shard_map/ppermute | solution.py:111
  70.3 1.9 %collective-permute-start.13 = (bf16[16,64,384]{2,1,0:T(8,128)(2,1)S(1)}, bf16[16,64,384]{2,1,0:T(8,128)(2,1)S(1)}, u32[]{:S(2)}, u32[]{:S(2)}) collective-permute-start(bf16[16,64,384]{2,1,0:T(8,128)(2,1)S(1)} %collective-permute-done.5.refs_11_), channel_id=1, source_target_pairs={{4,0},{29,1},{8,4},{1,5},{12,8},{5,9},{16,12},{9,13},{20,16},{13,1... | collective-permute-start | bytes 2359304 | tf_op jit(solution)/shard_map/ppermute | solution.py:114
  72.2 4.6 %collective-permute-start.14 = (bf16[16,64,384]{2,1,0:T(8,128)(2,1)S(1)}, bf16[16,64,384]{2,1,0:T(8,128)(2,1)S(1)}, u32[]{:S(2)}, u32[]{:S(2)}) collective-permute-start(bf16[16,64,384]{2,1,0:T(8,128)(2,1)S(1)} %collective-permute-done.10.refs_9_), channel_id=1, source_target_pairs={{0,4},{1,29},{4,8},{5,1},{8,12},{9,5},{12,16},{13,9},{16,20},{17,1... | collective-permute-start | bytes 2359304 | tf_op jit(solution)/shard_map/ppermute | solution.py:111
  76.8 3.8 %collective-permute-done.6.refs_3_ = bf16[16,128,128]{2,1,0:T(8,128)(2,1)S(1)} collective-permute-done((bf16[16,128,128]{2,1,0:T(8,128)(2,1)S(1)}, bf16[16,128,128]{2,1,0:T(8,128)(2,1)S(1)}, u32[]{:S(2)}, u32[]{:S(2)}) %collective-permute-start.6) | collective-permute-done | bytes 524320 | tf_op jit(solution)/shard_map/ppermute | solution.py:111
  80.6 1.9 %collective-permute-start.11 = (bf16[16,128,128]{2,1,0:T(8,128)(2,1)S(1)}, bf16[16,128,128]{2,1,0:T(8,128)(2,1)S(1)}, u32[]{:S(2)}, u32[]{:S(2)}) collective-permute-start(bf16[16,128,128]{2,1,0:T(8,128)(2,1)S(1)} %collective-permute-done.8.refs_5_), channel_id=1, source_target_pairs={{64,0},{449,1},{128,64},{1,65},{192,128},{65,129},{256,192},{129,1... | collective-permute-start | bytes 1572872 | tf_op jit(solution)/shard_map/ppermute | solution.py:114
  82.5 5.0 %collective-permute-start.12 = (bf16[16,128,128]{2,1,0:T(8,128)(2,1)S(1)}, bf16[16,128,128]{2,1,0:T(8,128)(2,1)S(1)}, u32[]{:S(2)}, u32[]{:S(2)}) collective-permute-start(bf16[16,128,128]{2,1,0:T(8,128)(2,1)S(1)} %collective-permute-done.6.refs_3_), channel_id=1, source_target_pairs={{0,64},{1,449},{64,128},{65,1},{128,192},{129,65},{192,256},{193,1... | collective-permute-start | bytes 1572872 | tf_op jit(solution)/shard_map/ppermute | solution.py:111
  87.6 0.0 copy-start
  87.6 1.1 copy-done
  88.7 4.1 %shard_map.55 = (bf16[8,16,128,128]{3,2,1,0:T(8,128)(2,1)S(1)}, bf16[8,16,64,384]{3,2,1,0:T(8,128)(2,1)S(1)}, f32[256,384]{1,0:T(8,128)S(1)}) custom-call(s32[4]{0:T(128)S(1)} %pad_add_fusion.place, bf16[16,128,128]{2,1,0:T(8,128)(2,1)S(1)} %collective-permute-done.refs_0_, bf16[16,128,128]{2,1,0:T(8,128)(2,1)S(1)} %collective-permute-done.2.refs_1_, ...), custom_call_target="tpu_custom_call" | custom-call | flops 1073741824 | bytes 16777216 | tf_op jit(solution)/shard_map/pallas_call | solution.py:134
  92.9 0.6 collective-permute-done.11
  93.5 4.0 %collective-permute-done.12 = bf16[16,128,128]{2,1,0:T(8,128)(2,1)S(1)} collective-permute-done((bf16[16,128,128]{2,1,0:T(8,128)(2,1)S(1)}, bf16[16,128,128]{2,1,0:T(8,128)(2,1)S(1)}, u32[]{:S(2)}, u32[]{:S(2)}) %collective-permute-start.12) | collective-permute-done | bytes 524320 | tf_op jit(solution)/shard_map/ppermute | solution.py:111
  97.5 2.2 %shard_map.56 = f32[2,384,128]{2,1,0:T(8,128)S(1)} custom-call(s32[4]{0:T(128)S(1)} %pad_add_fusion.place, f32[256,384]{1,0:T(8,128)S(1)} %get-tuple-element.30.early, bf16[8,16,128,128]{3,2,1,0:T(8,128)(2,1)S(1)} %get-tuple-element.31.amp_in, bf16[8,16,64,384]{3,2,1,0:T(8,128)(2,1)S(1)} %get-tuple-element.32.held, bf16[1,16,128,128]{3,2,1,0:T(8,128)(2,1)S(1)} %bitcast.8, ...), custom_call_target="tpu_custom_call" | custom-call | tf_op jit(solution)/shard_map/pallas_call | solution.py:143
  99.7 13.5 %all_to_all.5 = f32[8,96,128]{2,1,0:T(8,128)S(1)} all-to-all(f32[8,96,128]{2,1,0:T(8,128)S(1)} %bitcast.7), channel_id=1, replica_groups=mesh['y'=8,'xl'=2,'z'=8,'xh'=2,'core'=2] {'xl','xh','core'}, dimensions={0} | all-to-all | bytes 786432 | tf_op jit(solution)/shard_map/all_to_all | solution.py:151
  113.3 0.7 add_divide_fusion
  (12 shorter events, 0.0 us)
Async XLA Ops:
  0.1 24.3 %collective-permute-start.1 = (bf16[16,64,384]{2,1,0:T(8,128)(2,1)}, bf16[16,64,384]{2,1,0:T(8,128)(2,1)S(1)}, u32[]{:S(2)}, u32[]{:S(2)}) collective-permute-start(bf16[16,64,384]{2,1,0:T(8,128)(2,1)} %refs_6_), channel_id=1, source_target_pairs={{0,4},{1,29},{4,8},{5,1},{8,12},{9,5},{12,16},{13,9},{16,20},{17,1... | collective-permute-start | bytes 2359304 | tf_op jit(solution)/shard_map/ppermute | solution.py:111
  11.6 18.0 %collective-permute-start = (bf16[16,128,128]{2,1,0:T(8,128)(2,1)}, bf16[16,128,128]{2,1,0:T(8,128)(2,1)S(1)}, u32[]{:S(2)}, u32[]{:S(2)}) collective-permute-start(bf16[16,128,128]{2,1,0:T(8,128)(2,1)} %param.6), channel_id=1, source_target_pairs={{0,0},{32,448},{64,64},{96,384},{128,128},{160,320},{192,192},{224... | collective-permute-start | bytes 1572872 | tf_op jit(solution)/shard_map/ppermute | solution.py:118
  13.3 27.2 %collective-permute-start.3 = (bf16[16,64,384]{2,1,0:T(8,128)(2,1)}, bf16[16,64,384]{2,1,0:T(8,128)(2,1)S(1)}, u32[]{:S(2)}, u32[]{:S(2)}) collective-permute-start(bf16[16,64,384]{2,1,0:T(8,128)(2,1)} %refs_6_), channel_id=1, source_target_pairs={{4,0},{29,1},{8,4},{1,5},{12,8},{5,9},{16,12},{9,13},{20,16},{13,1... | collective-permute-start | bytes 2359304 | tf_op jit(solution)/shard_map/ppermute | solution.py:114
  24.4 27.2 %collective-permute-start.9 = (bf16[16,64,384]{2,1,0:T(8,128)(2,1)S(1)}, bf16[16,64,384]{2,1,0:T(8,128)(2,1)S(1)}, u32[]{:S(2)}, u32[]{:S(2)}) collective-permute-start(bf16[16,64,384]{2,1,0:T(8,128)(2,1)S(1)} %collective-permute-done.1.refs_7_), channel_id=1, source_target_pairs={{0,4},{1,29},{4,8},{5,1},{8,12},{9,5},{12,16},{13,9},{16,20},{17,1... | collective-permute-start | bytes 2359304 | tf_op jit(solution)/shard_map/ppermute | solution.py:111
  29.6 17.0 %collective-permute-start.2 = (bf16[16,128,128]{2,1,0:T(8,128)(2,1)S(1)}, bf16[16,128,128]{2,1,0:T(8,128)(2,1)S(1)}, u32[]{:S(2)}, u32[]{:S(2)}) collective-permute-start(bf16[16,128,128]{2,1,0:T(8,128)(2,1)S(1)} %collective-permute-done.refs_0_), channel_id=1, source_target_pairs={{0,64},{1,449},{64,128},{65,1},{128,192},{129,65},{192,256},{193,1... | collective-permute-start | bytes 1572872 | tf_op jit(solution)/shard_map/ppermute | solution.py:111
  40.5 24.4 %collective-permute-start.5 = (bf16[16,64,384]{2,1,0:T(8,128)(2,1)S(1)}, bf16[16,64,384]{2,1,0:T(8,128)(2,1)S(1)}, u32[]{:S(2)}, u32[]{:S(2)}) collective-permute-start(bf16[16,64,384]{2,1,0:T(8,128)(2,1)S(1)} %collective-permute-done.3.refs_10_), channel_id=1, source_target_pairs={{4,0},{29,1},{8,4},{1,5},{12,8},{5,9},{16,12},{9,13},{20,16},{13,1... | collective-permute-start | bytes 2359304 | tf_op jit(solution)/shard_map/ppermute | solution.py:114
  42.5 16.4 %collective-permute-start.7 = (bf16[16,128,128]{2,1,0:T(8,128)(2,1)S(1)}, bf16[16,128,128]{2,1,0:T(8,128)(2,1)S(1)}, u32[]{:S(2)}, u32[]{:S(2)}) collective-permute-start(bf16[16,128,128]{2,1,0:T(8,128)(2,1)S(1)} %collective-permute-done.refs_0_), channel_id=1, source_target_pairs={{64,0},{449,1},{128,64},{1,65},{192,128},{65,129},{256,192},{129,1... | collective-permute-start | bytes 1572872 | tf_op jit(solution)/shard_map/ppermute | solution.py:114
  46.6 16.4 %collective-permute-start.4 = (bf16[16,128,128]{2,1,0:T(8,128)(2,1)S(1)}, bf16[16,128,128]{2,1,0:T(8,128)(2,1)S(1)}, u32[]{:S(2)}, u32[]{:S(2)}) collective-permute-start(bf16[16,128,128]{2,1,0:T(8,128)(2,1)S(1)} %collective-permute-done.2.refs_1_), channel_id=1, source_target_pairs={{0,64},{1,449},{64,128},{65,1},{128,192},{129,65},{192,256},{193,1... | collective-permute-start | bytes 1572872 | tf_op jit(solution)/shard_map/ppermute | solution.py:111
  51.7 20.6 %collective-permute-start.10 = (bf16[16,64,384]{2,1,0:T(8,128)(2,1)S(1)}, bf16[16,64,384]{2,1,0:T(8,128)(2,1)S(1)}, u32[]{:S(2)}, u32[]{:S(2)}) collective-permute-start(bf16[16,64,384]{2,1,0:T(8,128)(2,1)S(1)} %collective-permute-done.9.refs_8_), channel_id=1, source_target_pairs={{0,4},{1,29},{4,8},{5,1},{8,12},{9,5},{12,16},{13,9},{16,20},{17,1... | collective-permute-start | bytes 2359304 | tf_op jit(solution)/shard_map/ppermute | solution.py:111
  63.0 13.8 %collective-permute-start.8 = (bf16[16,128,128]{2,1,0:T(8,128)(2,1)S(1)}, bf16[16,128,128]{2,1,0:T(8,128)(2,1)S(1)}, u32[]{:S(2)}, u32[]{:S(2)}) collective-permute-start(bf16[16,128,128]{2,1,0:T(8,128)(2,1)S(1)} %collective-permute-done.7.refs_4_), channel_id=1, source_target_pairs={{64,0},{449,1},{128,64},{1,65},{192,128},{65,129},{256,192},{129,1... | collective-permute-start | bytes 1572872 | tf_op jit(solution)/shard_map/ppermute | solution.py:114
  65.0 15.7 %collective-permute-start.6 = (bf16[16,128,128]{2,1,0:T(8,128)(2,1)S(1)}, bf16[16,128,128]{2,1,0:T(8,128)(2,1)S(1)}, u32[]{:S(2)}, u32[]{:S(2)}) collective-permute-start(bf16[16,128,128]{2,1,0:T(8,128)(2,1)S(1)} %collective-permute-done.4.refs_2_), channel_id=1, source_target_pairs={{0,64},{1,449},{64,128},{65,1},{128,192},{129,65},{192,256},{193,1... | collective-permute-start | bytes 1572872 | tf_op jit(solution)/shard_map/ppermute | solution.py:111
  70.3 22.6 %collective-permute-start.13 = (bf16[16,64,384]{2,1,0:T(8,128)(2,1)S(1)}, bf16[16,64,384]{2,1,0:T(8,128)(2,1)S(1)}, u32[]{:S(2)}, u32[]{:S(2)}) collective-permute-start(bf16[16,64,384]{2,1,0:T(8,128)(2,1)S(1)} %collective-permute-done.5.refs_11_), channel_id=1, source_target_pairs={{4,0},{29,1},{8,4},{1,5},{12,8},{5,9},{16,12},{9,13},{20,16},{13,1... | collective-permute-start | bytes 2359304 | tf_op jit(solution)/shard_map/ppermute | solution.py:114
  72.2 25.3 %collective-permute-start.14 = (bf16[16,64,384]{2,1,0:T(8,128)(2,1)S(1)}, bf16[16,64,384]{2,1,0:T(8,128)(2,1)S(1)}, u32[]{:S(2)}, u32[]{:S(2)}) collective-permute-start(bf16[16,64,384]{2,1,0:T(8,128)(2,1)S(1)} %collective-permute-done.10.refs_9_), channel_id=1, source_target_pairs={{0,4},{1,29},{4,8},{5,1},{8,12},{9,5},{12,16},{13,9},{16,20},{17,1... | collective-permute-start | bytes 2359304 | tf_op jit(solution)/shard_map/ppermute | solution.py:111
  80.6 12.9 %collective-permute-start.11 = (bf16[16,128,128]{2,1,0:T(8,128)(2,1)S(1)}, bf16[16,128,128]{2,1,0:T(8,128)(2,1)S(1)}, u32[]{:S(2)}, u32[]{:S(2)}) collective-permute-start(bf16[16,128,128]{2,1,0:T(8,128)(2,1)S(1)} %collective-permute-done.8.refs_5_), channel_id=1, source_target_pairs={{64,0},{449,1},{128,64},{1,65},{192,128},{65,129},{256,192},{129,1... | collective-permute-start | bytes 1572872 | tf_op jit(solution)/shard_map/ppermute | solution.py:114
  82.5 15.0 %collective-permute-start.12 = (bf16[16,128,128]{2,1,0:T(8,128)(2,1)S(1)}, bf16[16,128,128]{2,1,0:T(8,128)(2,1)S(1)}, u32[]{:S(2)}, u32[]{:S(2)}) collective-permute-start(bf16[16,128,128]{2,1,0:T(8,128)(2,1)S(1)} %collective-permute-done.6.refs_3_), channel_id=1, source_target_pairs={{0,64},{1,449},{64,128},{65,1},{128,192},{129,65},{192,256},{193,1... | collective-permute-start | bytes 1572872 | tf_op jit(solution)/shard_map/ppermute | solution.py:111
  87.6 1.1 copy-start
  97.5 15.8 %copy-start.1 = (bf16[96,128]{1,0:T(8,128)(2,1)S(1)}, bf16[96,128]{1,0:T(8,128)(2,1)}, u32[]{:S(2)}) copy-start(bf16[96,128]{1,0:T(8,128)(2,1)} %param.7) | copy-start | bytes 73732
  97.5 15.8 %copy-start.2 = (f32[128]{0:T(128)S(1)}, f32[128]{0:T(128)}, u32[]{:S(2)}) copy-start(f32[128]{0:T(128)} %param.9) | copy-start | bytes 1540
  97.5 15.8 %copy-start.3 = (f32[96]{0:T(128)S(1)}, f32[96]{0:T(128)}, u32[]{:S(2)}) copy-start(f32[96]{0:T(128)} %param.8) | copy-start | bytes 1156

commit v8 on v7

--- a/solution.py
+++ b/solution.py
@@ -32,7 +32,7 @@
 def piece(x, amp_ref, source, block):
     y = x * 4 + source // 2
     return times(
-        jnp.concatenate([columns(amp_ref, slot, source) for slot in (y, 7 - y)], axis=1), block
+        jnp.concatenate([columns(amp_ref, slot, source) for slot in (y, 7 - y)], axis=1), block[...]
     )
 
 
@@ -63,27 +63,29 @@
     out[...] = total
 
 
-def late_kernel(place, early, amp_in, held, *refs):
+def late_sources(place):
+    z, way = place[2], 1 - 2 * place[3]
+    return [lax.rem(z + way * turn + 8, 8) for turn in LATE]
+
+
+def middle_kernel(place, early, amp, *refs):
+    blocks, out = refs[:-1], refs[-1]
+    new = early[...]
+    for source, ref in zip(late_sources(place), blocks):
+        new = new + piece(place[0], amp, source, ref)
+    out[...] = new
+
+
+def late_kernel(place, middle, held, *refs):
     count = len(LATE)
     amps, blocks, (out, total) = refs[:count], refs[count : 2 * count], refs[2 * count :]
-    x, y, z, way = place[0], place[1], place[2], 1 - 2 * place[3]
-    slots = [lax.rem(y + way * turn + 8, 8) for turn in LATE]
-    sources = [lax.rem(z + way * turn + 8, 8) for turn in LATE]
-
-    def either(at, source):
-        amp = columns(amp_in, at, source)
-        for slot, ref in zip(slots, amps):
-            amp = jnp.where(at == slot, columns(ref, 0, source), amp)
-        return amp
-
-    new = early[...]
-    for source, ref in zip(sources, blocks):
-        at = x * 4 + source // 2
-        pair = jnp.concatenate([either(at, source), either(7 - at, source)], axis=1)
-        new = new + times(pair, ref[...])
-    total[...] = new
-    for slot, ref in zip(slots, amps):
+    x, y, way = place[0], place[1], 1 - 2 * place[3]
+    sources = late_sources(place)
+    total[...] = middle[...]
+    for turn, ref in zip(LATE, amps):
+        slot = lax.rem(y + way * turn + 8, 8)
         other = jnp.where(slot // 4 == x, 0, 1)
+        at = pl.ds(pl.multiple_of(other * 128, 128), 128)
         first = lax.rem(jnp.where(other == 0, slot, 7 - slot), 4) * 2
         for source in (first, first + 1):
             fresh = source != sources[0]
@@ -92,8 +94,13 @@
 
             @pl.when(fresh)
             def _():
-                at = pl.ds(pl.multiple_of(other * 128, 128), 128)
                 total[at, :] += times(columns(ref, 0, source), held[source])
+
+            for late, block in zip(sources, blocks):
+
+                @pl.when(source == late)
+                def _():
+                    total[at, :] += times(columns(ref, 0, source), block[...])
 
     for n in range(2):
         out[lax.rem(x + n, 2)] = total[n * 128 : (n + 1) * 128].T
@@ -140,14 +147,21 @@
         compiler_params=pltpu.CompilerParams(vmem_limit_bytes=24 << 20),
         cost_estimate=pl.CostEstimate(flops=1 << 30, bytes_accessed=16 << 20, transcendentals=0),
     )(place, a0, au1, au2, au3, ad1, ad2, i0, iu1, iu2, iu3, id1, id2)
+    middle = pl.pallas_call(
+        middle_kernel,
+        out_shape=jax.ShapeDtypeStruct((256, 384), FLOAT),
+        in_specs=[SMEM] + [VMEM] * 4,
+        out_specs=VMEM,
+        compiler_params=pltpu.CompilerParams(vmem_limit_bytes=8 << 20),
+    )(place, early, amp, id3, iu4)
     shares = pl.pallas_call(
         late_kernel,
         out_shape=jax.ShapeDtypeStruct((2, 384, 128), FLOAT),
-        in_specs=[SMEM] + [VMEM] * 7,
+        in_specs=[SMEM] + [VMEM] * 6,
         out_specs=VMEM,
         scratch_shapes=[pltpu.VMEM((256, 384), FLOAT)],
         compiler_params=pltpu.CompilerParams(vmem_limit_bytes=8 << 20),
-    )(place, early, amp, held, ad3[None], au4[None], id3, iu4)
+    )(place, middle, held, ad3[None], au4[None], id3, iu4)
     shares = lax.all_to_all(
         shares.reshape(8, 96, 128), ("xl", "xh", "core"), 0, 0, tiled=True
     )

time: 115 us -> 114 us (level)
  waiting for transfers between devices: 24.1 us -> 22.8 us
  Pallas kernels: 6.34 us -> 7.55 us
    pallas_call x0 -> x1, Pallas kernels: none -> 1.3 us  [local(): pl.pallas_call(middle_kernel, out_shape=jax.ShapeDtypeStruct((256, 384),...]
  transfers between devices with their start and end apart: 15 -> 15, of which waited for: 6 -> 6; matrix products, arithmetic and copies ran while one was open for 0% -> 0% of each run, Pallas kernels for 4% -> 5%
where the time goes in v8:
time: 114 us; the launch traced here: 113 us
  starting transfers between devices  67.9 us (60%)
  waiting for transfers between devices  22.8 us (20%)
  blocking collectives  12.9 us (11%)
  Pallas kernels  7.55 us (7%)
  local copies, waits for them, and re-layouts  1.15 us (1%)
    ppermute x8, starting transfers between devices, forth(): return lax.ppermute(after(block, *arrived), (axis, 'core'), FORTH)  54.7 us
    ppermute x8, waiting for transfers between devices, forth(): return lax.ppermute(after(block, *arrived), (axis, 'core'), FORTH)  22.8 us
    all_to_all x1, blocking collectives, local(): lax.all_to_all(shares.reshape(8, 96, 128), ('xl', 'xh', 'core'), 0, 0, ti...  12.9 us
    ppermute x6, starting transfers between devices, back(): return lax.ppermute(after(block, *arrived), (axis, 'core'), BACK)  11.5 us
    pallas_call x1, Pallas kernels, local(): pl.pallas_call(early_kernel, out_shape=(amp_shape, held_shape, jax.ShapeD...  4.13 us
  transfers between devices with their start and end apart: 15, of which 6 were waited for; matrix products, arithmetic and copies ran while one was open for 0% of the time, Pallas kernels for 5%

profile of v8, /device:TPU:1, one launch (start us, length us, event | category | flops | bytes accessed | tf_op | source)
XLA Modules:
  0.0 113.3 jit_solution(15508402841085380469)
XLA Ops:
  0.0 0.1 pad_add_fusion.place
  0.1 11.5 %collective-permute-start.1 = (bf16[16,64,384]{2,1,0:T(8,128)(2,1)}, bf16[16,64,384]{2,1,0:T(8,128)(2,1)S(1)}, u32[]{:S(2)}, u32[]{:S(2)}) collective-permute-start(bf16[16,64,384]{2,1,0:T(8,128)(2,1)} %refs_6_), channel_id=1, source_target_pairs={{0,4},{1,29},{4,8},{5,1},{8,12},{9,5},{12,16},{13,9},{16,20},{17,1... | collective-permute-start | bytes 2359304 | tf_op jit(solution)/shard_map/ppermute | solution.py:118
  11.6 1.7 %collective-permute-start = (bf16[16,128,128]{2,1,0:T(8,128)(2,1)}, bf16[16,128,128]{2,1,0:T(8,128)(2,1)S(1)}, u32[]{:S(2)}, u32[]{:S(2)}) collective-permute-start(bf16[16,128,128]{2,1,0:T(8,128)(2,1)} %param.6), channel_id=1, source_target_pairs={{0,0},{32,448},{64,64},{96,384},{128,128},{160,320},{192,192},{224... | collective-permute-start | bytes 1572872 | tf_op jit(solution)/shard_map/ppermute | solution.py:125
  13.3 1.9 %collective-permute-start.3 = (bf16[16,64,384]{2,1,0:T(8,128)(2,1)}, bf16[16,64,384]{2,1,0:T(8,128)(2,1)S(1)}, u32[]{:S(2)}, u32[]{:S(2)}) collective-permute-start(bf16[16,64,384]{2,1,0:T(8,128)(2,1)} %refs_6_), channel_id=1, source_target_pairs={{4,0},{29,1},{8,4},{1,5},{12,8},{5,9},{16,12},{9,13},{20,16},{13,1... | collective-permute-start | bytes 2359304 | tf_op jit(solution)/shard_map/ppermute | solution.py:121
  15.2 9.2 %collective-permute-done.1.refs_7_ = bf16[16,64,384]{2,1,0:T(8,128)(2,1)S(1)} collective-permute-done((bf16[16,64,384]{2,1,0:T(8,128)(2,1)}, bf16[16,64,384]{2,1,0:T(8,128)(2,1)S(1)}, u32[]{:S(2)}, u32[]{:S(2)}) %collective-permute-start.1) | collective-permute-done | bytes 786464 | tf_op jit(solution)/shard_map/ppermute | solution.py:118
  24.4 5.2 %collective-permute-start.9 = (bf16[16,64,384]{2,1,0:T(8,128)(2,1)S(1)}, bf16[16,64,384]{2,1,0:T(8,128)(2,1)S(1)}, u32[]{:S(2)}, u32[]{:S(2)}) collective-permute-start(bf16[16,64,384]{2,1,0:T(8,128)(2,1)S(1)} %collective-permute-done.1.refs_7_), channel_id=1, source_target_pairs={{0,4},{1,29},{4,8},{5,1},{8,12},{9,5},{12,16},{13,9},{16,20},{17,1... | collective-permute-start | bytes 2359304 | tf_op jit(solution)/shard_map/ppermute | solution.py:118
  29.6 10.9 %collective-permute-start.2 = (bf16[16,128,128]{2,1,0:T(8,128)(2,1)S(1)}, bf16[16,128,128]{2,1,0:T(8,128)(2,1)S(1)}, u32[]{:S(2)}, u32[]{:S(2)}) collective-permute-start(bf16[16,128,128]{2,1,0:T(8,128)(2,1)S(1)} %collective-permute-done.refs_0_), channel_id=1, source_target_pairs={{0,64},{1,449},{64,128},{65,1},{128,192},{129,65},{192,256},{193,1... | collective-permute-start | bytes 1572872 | tf_op jit(solution)/shard_map/ppermute | solution.py:118
  40.5 1.9 %collective-permute-start.5 = (bf16[16,64,384]{2,1,0:T(8,128)(2,1)S(1)}, bf16[16,64,384]{2,1,0:T(8,128)(2,1)S(1)}, u32[]{:S(2)}, u32[]{:S(2)}) collective-permute-start(bf16[16,64,384]{2,1,0:T(8,128)(2,1)S(1)} %collective-permute-done.3.refs_10_), channel_id=1, source_target_pairs={{4,0},{29,1},{8,4},{1,5},{12,8},{5,9},{16,12},{9,13},{20,16},{13,1... | collective-permute-start | bytes 2359304 | tf_op jit(solution)/shard_map/ppermute | solution.py:121
  42.5 1.9 %collective-permute-start.7 = (bf16[16,128,128]{2,1,0:T(8,128)(2,1)S(1)}, bf16[16,128,128]{2,1,0:T(8,128)(2,1)S(1)}, u32[]{:S(2)}, u32[]{:S(2)}) collective-permute-start(bf16[16,128,128]{2,1,0:T(8,128)(2,1)S(1)} %collective-permute-done.refs_0_), channel_id=1, source_target_pairs={{64,0},{449,1},{128,64},{1,65},{192,128},{65,129},{256,192},{129,1... | collective-permute-start | bytes 1572872 | tf_op jit(solution)/shard_map/ppermute | solution.py:121
  44.4 2.2 %collective-permute-done.2.refs_1_ = bf16[16,128,128]{2,1,0:T(8,128)(2,1)S(1)} collective-permute-done((bf16[16,128,128]{2,1,0:T(8,128)(2,1)S(1)}, bf16[16,128,128]{2,1,0:T(8,128)(2,1)S(1)}, u32[]{:S(2)}, u32[]{:S(2)}) %collective-permute-start.2) | collective-permute-done | bytes 524320 | tf_op jit(solution)/shard_map/ppermute | solution.py:118
  46.6 5.0 %collective-permute-start.4 = (bf16[16,128,128]{2,1,0:T(8,128)(2,1)S(1)}, bf16[16,128,128]{2,1,0:T(8,128)(2,1)S(1)}, u32[]{:S(2)}, u32[]{:S(2)}) collective-permute-start(bf16[16,128,128]{2,1,0:T(8,128)(2,1)S(1)} %collective-permute-done.2.refs_1_), channel_id=1, source_target_pairs={{0,64},{1,449},{64,128},{65,1},{128,192},{129,65},{192,256},{193,1... | collective-permute-start | bytes 1572872 | tf_op jit(solution)/shard_map/ppermute | solution.py:118
  51.7 7.2 %collective-permute-start.10 = (bf16[16,64,384]{2,1,0:T(8,128)(2,1)S(1)}, bf16[16,64,384]{2,1,0:T(8,128)(2,1)S(1)}, u32[]{:S(2)}, u32[]{:S(2)}) collective-permute-start(bf16[16,64,384]{2,1,0:T(8,128)(2,1)S(1)} %collective-permute-done.9.refs_8_), channel_id=1, source_target_pairs={{0,4},{1,29},{4,8},{5,1},{8,12},{9,5},{12,16},{13,9},{16,20},{17,1... | collective-permute-start | bytes 2359304 | tf_op jit(solution)/shard_map/ppermute | solution.py:118
  58.8 4.2 %collective-permute-done.4.refs_2_ = bf16[16,128,128]{2,1,0:T(8,128)(2,1)S(1)} collective-permute-done((bf16[16,128,128]{2,1,0:T(8,128)(2,1)S(1)}, bf16[16,128,128]{2,1,0:T(8,128)(2,1)S(1)}, u32[]{:S(2)}, u32[]{:S(2)}) %collective-permute-start.4) | collective-permute-done | bytes 524320 | tf_op jit(solution)/shard_map/ppermute | solution.py:118
  63.0 1.9 %collective-permute-start.8 = (bf16[16,128,128]{2,1,0:T(8,128)(2,1)S(1)}, bf16[16,128,128]{2,1,0:T(8,128)(2,1)S(1)}, u32[]{:S(2)}, u32[]{:S(2)}) collective-permute-start(bf16[16,128,128]{2,1,0:T(8,128)(2,1)S(1)} %collective-permute-done.7.refs_4_), channel_id=1, source_target_pairs={{64,0},{449,1},{128,64},{1,65},{192,128},{65,129},{256,192},{129,1... | collective-permute-start | bytes 1572872 | tf_op jit(solution)/shard_map/ppermute | solution.py:121
  65.0 5.3 %collective-permute-start.6 = (bf16[16,128,128]{2,1,0:T(8,128)(2,1)S(1)}, bf16[16,128,128]{2,1,0:T(8,128)(2,1)S(1)}, u32[]{:S(2)}, u32[]{:S(2)}) collective-permute-start(bf16[16,128,128]{2,1,0:T(8,128)(2,1)S(1)} %collective-permute-done.4.refs_2_), channel_id=1, source_target_pairs={{0,64},{1,449},{64,128},{65,1},{128,192},{129,65},{192,256},{193,1... | collective-permute-start | bytes 1572872 | tf_op jit(solution)/shard_map/ppermute | solution.py:118
  70.3 1.9 %collective-permute-start.11 = (bf16[16,64,384]{2,1,0:T(8,128)(2,1)S(1)}, bf16[16,64,384]{2,1,0:T(8,128)(2,1)S(1)}, u32[]{:S(2)}, u32[]{:S(2)}) collective-permute-start(bf16[16,64,384]{2,1,0:T(8,128)(2,1)S(1)} %collective-permute-done.5.refs_11_), channel_id=1, source_target_pairs={{4,0},{29,1},{8,4},{1,5},{12,8},{5,9},{16,12},{9,13},{20,16},{13,1... | collective-permute-start | bytes 2359304 | tf_op jit(solution)/shard_map/ppermute | solution.py:121
  72.2 4.6 %collective-permute-start.12 = (bf16[16,64,384]{2,1,0:T(8,128)(2,1)S(1)}, bf16[16,64,384]{2,1,0:T(8,128)(2,1)S(1)}, u32[]{:S(2)}, u32[]{:S(2)}) collective-permute-start(bf16[16,64,384]{2,1,0:T(8,128)(2,1)S(1)} %collective-permute-done.10.refs_9_), channel_id=1, source_target_pairs={{0,4},{1,29},{4,8},{5,1},{8,12},{9,5},{12,16},{13,9},{16,20},{17,1... | collective-permute-start | bytes 2359304 | tf_op jit(solution)/shard_map/ppermute | solution.py:118
  76.8 3.8 %collective-permute-done.6.refs_3_ = bf16[16,128,128]{2,1,0:T(8,128)(2,1)S(1)} collective-permute-done((bf16[16,128,128]{2,1,0:T(8,128)(2,1)S(1)}, bf16[16,128,128]{2,1,0:T(8,128)(2,1)S(1)}, u32[]{:S(2)}, u32[]{:S(2)}) %collective-permute-start.6) | collective-permute-done | bytes 524320 | tf_op jit(solution)/shard_map/ppermute | solution.py:118
  80.6 1.9 %collective-permute-start.13 = (bf16[16,128,128]{2,1,0:T(8,128)(2,1)S(1)}, bf16[16,128,128]{2,1,0:T(8,128)(2,1)S(1)}, u32[]{:S(2)}, u32[]{:S(2)}) collective-permute-start(bf16[16,128,128]{2,1,0:T(8,128)(2,1)S(1)} %collective-permute-done.8.refs_5_), channel_id=1, source_target_pairs={{64,0},{449,1},{128,64},{1,65},{192,128},{65,129},{256,192},{129,1... | collective-permute-start | bytes 1572872 | tf_op jit(solution)/shard_map/ppermute | solution.py:121
  82.5 5.0 %collective-permute-start.14 = (bf16[16,128,128]{2,1,0:T(8,128)(2,1)S(1)}, bf16[16,128,128]{2,1,0:T(8,128)(2,1)S(1)}, u32[]{:S(2)}, u32[]{:S(2)}) collective-permute-start(bf16[16,128,128]{2,1,0:T(8,128)(2,1)S(1)} %collective-permute-done.6.refs_3_), channel_id=1, source_target_pairs={{0,64},{1,449},{64,128},{65,1},{128,192},{129,65},{192,256},{193,1... | collective-permute-start | bytes 1572872 | tf_op jit(solution)/shard_map/ppermute | solution.py:118
  87.6 0.0 copy-start
  87.6 1.1 copy-done
  88.7 4.1 %shard_map.55 = (bf16[8,16,128,128]{3,2,1,0:T(8,128)(2,1)S(1)}, bf16[8,16,64,384]{3,2,1,0:T(8,128)(2,1)S(1)}, f32[256,384]{1,0:T(8,128)S(1)}) custom-call(s32[4]{0:T(128)S(1)} %pad_add_fusion.place, bf16[16,128,128]{2,1,0:T(8,128)(2,1)S(1)} %collective-permute-done.refs_0_, bf16[16,128,128]{2,1,0:T(8,128)(2,1)S(1)} %collective-permute-done.2.refs_1_, ...), custom_call_target="tpu_custom_call" | custom-call | flops 1073741824 | bytes 16777216 | tf_op jit(solution)/shard_map/pallas_call | solution.py:141
  92.9 1.3 %collective-permute-done.12.refs_1_.refs_3_ = bf16[16,64,384]{2,1,0:T(8,128)(2,1)S(1)} collective-permute-done((bf16[16,64,384]{2,1,0:T(8,128)(2,1)S(1)}, bf16[16,64,384]{2,1,0:T(8,128)(2,1)S(1)}, u32[]{:S(2)}, u32[]{:S(2)}) %collective-permute-start.12) | collective-permute-done | bytes 786464 | tf_op jit(solution)/shard_map/ppermute | solution.py:118
  94.1 1.3 %shard_map.56.middle = f32[256,384]{1,0:T(8,128)S(1)} custom-call(s32[4]{0:T(128)S(1)} %pad_add_fusion.place, f32[256,384]{1,0:T(8,128)S(1)} %get-tuple-element.30.early, bf16[8,16,128,128]{3,2,1,0:T(8,128)(2,1)S(1)} %get-tuple-element.31.amp, bf16[16,64,384]{2,1,0:T(8,128)(2,1)S(1)} %collective-permute-done.11.refs_0_.refs_2_, ...), custom_call_target="tpu_custom_call" | custom-call | tf_op jit(solution)/shard_map/pallas_call | solution.py:150
  95.4 0.0 copy-start.1
  95.5 0.0 copy-start.2
  95.5 0.0 copy-start.3
  95.5 2.0 %collective-permute-done.14 = bf16[16,128,128]{2,1,0:T(8,128)(2,1)S(1)} collective-permute-done((bf16[16,128,128]{2,1,0:T(8,128)(2,1)S(1)}, bf16[16,128,128]{2,1,0:T(8,128)(2,1)S(1)}, u32[]{:S(2)}, u32[]{:S(2)}) %collective-permute-start.14) | collective-permute-done | bytes 524320 | tf_op jit(solution)/shard_map/ppermute | solution.py:118
  97.5 2.1 %shard_map.57 = f32[2,384,128]{2,1,0:T(8,128)S(1)} custom-call(s32[4]{0:T(128)S(1)} %pad_add_fusion.place, f32[256,384]{1,0:T(8,128)S(1)} %shard_map.56.middle, bf16[8,16,64,384]{3,2,1,0:T(8,128)(2,1)S(1)} %get-tuple-element.34.held, bf16[1,16,128,128]{3,2,1,0:T(8,128)(2,1)S(1)} %bitcast.8, bf16[1,16,128,128]{3,2,1,0:T(8,128)(2,1)S(1)} %bitcast.9, ...), custom_call_target="tpu_custom_call" | custom-call | tf_op jit(solution)/shard_map/pallas_call | solution.py:157
  99.6 12.9 %all_to_all.5 = f32[8,96,128]{2,1,0:T(8,128)S(1)} all-to-all(f32[8,96,128]{2,1,0:T(8,128)S(1)} %bitcast.7), channel_id=1, replica_groups=mesh['y'=8,'xl'=2,'z'=8,'xh'=2,'core'=2] {'xl','xh','core'}, dimensions={0} | all-to-all | bytes 786432 | tf_op jit(solution)/shard_map/all_to_all | solution.py:165
  112.6 0.7 add_divide_fusion
  (13 shorter events, 0.1 us)
Async XLA Ops:
  0.1 24.3 %collective-permute-start.1 = (bf16[16,64,384]{2,1,0:T(8,128)(2,1)}, bf16[16,64,384]{2,1,0:T(8,128)(2,1)S(1)}, u32[]{:S(2)}, u32[]{:S(2)}) collective-permute-start(bf16[16,64,384]{2,1,0:T(8,128)(2,1)} %refs_6_), channel_id=1, source_target_pairs={{0,4},{1,29},{4,8},{5,1},{8,12},{9,5},{12,16},{13,9},{16,20},{17,1... | collective-permute-start | bytes 2359304 | tf_op jit(solution)/shard_map/ppermute | solution.py:118
  11.6 18.0 %collective-permute-start = (bf16[16,128,128]{2,1,0:T(8,128)(2,1)}, bf16[16,128,128]{2,1,0:T(8,128)(2,1)S(1)}, u32[]{:S(2)}, u32[]{:S(2)}) collective-permute-start(bf16[16,128,128]{2,1,0:T(8,128)(2,1)} %param.6), channel_id=1, source_target_pairs={{0,0},{32,448},{64,64},{96,384},{128,128},{160,320},{192,192},{224... | collective-permute-start | bytes 1572872 | tf_op jit(solution)/shard_map/ppermute | solution.py:125
  13.3 27.2 %collective-permute-start.3 = (bf16[16,64,384]{2,1,0:T(8,128)(2,1)}, bf16[16,64,384]{2,1,0:T(8,128)(2,1)S(1)}, u32[]{:S(2)}, u32[]{:S(2)}) collective-permute-start(bf16[16,64,384]{2,1,0:T(8,128)(2,1)} %refs_6_), channel_id=1, source_target_pairs={{4,0},{29,1},{8,4},{1,5},{12,8},{5,9},{16,12},{9,13},{20,16},{13,1... | collective-permute-start | bytes 2359304 | tf_op jit(solution)/shard_map/ppermute | solution.py:121
  24.4 27.2 %collective-permute-start.9 = (bf16[16,64,384]{2,1,0:T(8,128)(2,1)S(1)}, bf16[16,64,384]{2,1,0:T(8,128)(2,1)S(1)}, u32[]{:S(2)}, u32[]{:S(2)}) collective-permute-start(bf16[16,64,384]{2,1,0:T(8,128)(2,1)S(1)} %collective-permute-done.1.refs_7_), channel_id=1, source_target_pairs={{0,4},{1,29},{4,8},{5,1},{8,12},{9,5},{12,16},{13,9},{16,20},{17,1... | collective-permute-start | bytes 2359304 | tf_op jit(solution)/shard_map/ppermute | solution.py:118
  29.6 17.0 %collective-permute-start.2 = (bf16[16,128,128]{2,1,0:T(8,128)(2,1)S(1)}, bf16[16,128,128]{2,1,0:T(8,128)(2,1)S(1)}, u32[]{:S(2)}, u32[]{:S(2)}) collective-permute-start(bf16[16,128,128]{2,1,0:T(8,128)(2,1)S(1)} %collective-permute-done.refs_0_), channel_id=1, source_target_pairs={{0,64},{1,449},{64,128},{65,1},{128,192},{129,65},{192,256},{193,1... | collective-permute-start | bytes 1572872 | tf_op jit(solution)/shard_map/ppermute | solution.py:118
  40.5 24.4 %collective-permute-start.5 = (bf16[16,64,384]{2,1,0:T(8,128)(2,1)S(1)}, bf16[16,64,384]{2,1,0:T(8,128)(2,1)S(1)}, u32[]{:S(2)}, u32[]{:S(2)}) collective-permute-start(bf16[16,64,384]{2,1,0:T(8,128)(2,1)S(1)} %collective-permute-done.3.refs_10_), channel_id=1, source_target_pairs={{4,0},{29,1},{8,4},{1,5},{12,8},{5,9},{16,12},{9,13},{20,16},{13,1... | collective-permute-start | bytes 2359304 | tf_op jit(solution)/shard_map/ppermute | solution.py:121
  42.5 16.4 %collective-permute-start.7 = (bf16[16,128,128]{2,1,0:T(8,128)(2,1)S(1)}, bf16[16,128,128]{2,1,0:T(8,128)(2,1)S(1)}, u32[]{:S(2)}, u32[]{:S(2)}) collective-permute-start(bf16[16,128,128]{2,1,0:T(8,128)(2,1)S(1)} %collective-permute-done.refs_0_), channel_id=1, source_target_pairs={{64,0},{449,1},{128,64},{1,65},{192,128},{65,129},{256,192},{129,1... | collective-permute-start | bytes 1572872 | tf_op jit(solution)/shard_map/ppermute | solution.py:121
  46.6 16.4 %collective-permute-start.4 = (bf16[16,128,128]{2,1,0:T(8,128)(2,1)S(1)}, bf16[16,128,128]{2,1,0:T(8,128)(2,1)S(1)}, u32[]{:S(2)}, u32[]{:S(2)}) collective-permute-start(bf16[16,128,128]{2,1,0:T(8,128)(2,1)S(1)} %collective-permute-done.2.refs_1_), channel_id=1, source_target_pairs={{0,64},{1,449},{64,128},{65,1},{128,192},{129,65},{192,256},{193,1... | collective-permute-start | bytes 1572872 | tf_op jit(solution)/shard_map/ppermute | solution.py:118
  51.7 20.6 %collective-permute-start.10 = (bf16[16,64,384]{2,1,0:T(8,128)(2,1)S(1)}, bf16[16,64,384]{2,1,0:T(8,128)(2,1)S(1)}, u32[]{:S(2)}, u32[]{:S(2)}) collective-permute-start(bf16[16,64,384]{2,1,0:T(8,128)(2,1)S(1)} %collective-permute-done.9.refs_8_), channel_id=1, source_target_pairs={{0,4},{1,29},{4,8},{5,1},{8,12},{9,5},{12,16},{13,9},{16,20},{17,1... | collective-permute-start | bytes 2359304 | tf_op jit(solution)/shard_map/ppermute | solution.py:118
  63.0 13.8 %collective-permute-start.8 = (bf16[16,128,128]{2,1,0:T(8,128)(2,1)S(1)}, bf16[16,128,128]{2,1,0:T(8,128)(2,1)S(1)}, u32[]{:S(2)}, u32[]{:S(2)}) collective-permute-start(bf16[16,128,128]{2,1,0:T(8,128)(2,1)S(1)} %collective-permute-done.7.refs_4_), channel_id=1, source_target_pairs={{64,0},{449,1},{128,64},{1,65},{192,128},{65,129},{256,192},{129,1... | collective-permute-start | bytes 1572872 | tf_op jit(solution)/shard_map/ppermute | solution.py:121
  65.0 15.7 %collective-permute-start.6 = (bf16[16,128,128]{2,1,0:T(8,128)(2,1)S(1)}, bf16[16,128,128]{2,1,0:T(8,128)(2,1)S(1)}, u32[]{:S(2)}, u32[]{:S(2)}) collective-permute-start(bf16[16,128,128]{2,1,0:T(8,128)(2,1)S(1)} %collective-permute-done.4.refs_2_), channel_id=1, source_target_pairs={{0,64},{1,449},{64,128},{65,1},{128,192},{129,65},{192,256},{193,1... | collective-permute-start | bytes 1572872 | tf_op jit(solution)/shard_map/ppermute | solution.py:118
  70.3 22.6 %collective-permute-start.11 = (bf16[16,64,384]{2,1,0:T(8,128)(2,1)S(1)}, bf16[16,64,384]{2,1,0:T(8,128)(2,1)S(1)}, u32[]{:S(2)}, u32[]{:S(2)}) collective-permute-start(bf16[16,64,384]{2,1,0:T(8,128)(2,1)S(1)} %collective-permute-done.5.refs_11_), channel_id=1, source_target_pairs={{4,0},{29,1},{8,4},{1,5},{12,8},{5,9},{16,12},{9,13},{20,16},{13,1... | collective-permute-start | bytes 2359304 | tf_op jit(solution)/shard_map/ppermute | solution.py:121
  72.2 21.9 %collective-permute-start.12 = (bf16[16,64,384]{2,1,0:T(8,128)(2,1)S(1)}, bf16[16,64,384]{2,1,0:T(8,128)(2,1)S(1)}, u32[]{:S(2)}, u32[]{:S(2)}) collective-permute-start(bf16[16,64,384]{2,1,0:T(8,128)(2,1)S(1)} %collective-permute-done.10.refs_9_), channel_id=1, source_target_pairs={{0,4},{1,29},{4,8},{5,1},{8,12},{9,5},{12,16},{13,9},{16,20},{17,1... | collective-permute-start | bytes 2359304 | tf_op jit(solution)/shard_map/ppermute | solution.py:118
  80.6 14.9 %collective-permute-start.13 = (bf16[16,128,128]{2,1,0:T(8,128)(2,1)S(1)}, bf16[16,128,128]{2,1,0:T(8,128)(2,1)S(1)}, u32[]{:S(2)}, u32[]{:S(2)}) collective-permute-start(bf16[16,128,128]{2,1,0:T(8,128)(2,1)S(1)} %collective-permute-done.8.refs_5_), channel_id=1, source_target_pairs={{64,0},{449,1},{128,64},{1,65},{192,128},{65,129},{256,192},{129,1... | collective-permute-start | bytes 1572872 | tf_op jit(solution)/shard_map/ppermute | solution.py:121
  82.5 15.0 %collective-permute-start.14 = (bf16[16,128,128]{2,1,0:T(8,128)(2,1)S(1)}, bf16[16,128,128]{2,1,0:T(8,128)(2,1)S(1)}, u32[]{:S(2)}, u32[]{:S(2)}) collective-permute-start(bf16[16,128,128]{2,1,0:T(8,128)(2,1)S(1)} %collective-permute-done.6.refs_3_), channel_id=1, source_target_pairs={{0,64},{1,449},{64,128},{65,1},{128,192},{129,65},{192,256},{193,1... | collective-permute-start | bytes 1572872 | tf_op jit(solution)/shard_map/ppermute | solution.py:118
  87.6 1.1 %copy-start = (bf16[16,64,384]{2,1,0:T(8,128)(2,1)S(1)}, bf16[16,64,384]{2,1,0:T(8,128)(2,1)}, u32[]{:S(2)}) copy-start(bf16[16,64,384]{2,1,0:T(8,128)(2,1)} %refs_6_) | copy-start | bytes 2359300
  95.4 17.1 %copy-start.1 = (bf16[96,128]{1,0:T(8,128)(2,1)S(1)}, bf16[96,128]{1,0:T(8,128)(2,1)}, u32[]{:S(2)}) copy-start(bf16[96,128]{1,0:T(8,128)(2,1)} %param.7) | copy-start | bytes 73732
  95.5 17.1 %copy-start.2 = (f32[128]{0:T(128)S(1)}, f32[128]{0:T(128)}, u32[]{:S(2)}) copy-start(f32[128]{0:T(128)} %param.9) | copy-start | bytes 1540
  95.5 17.1 %copy-start.3 = (f32[96]{0:T(128)S(1)}, f32[96]{0:T(128)}, u32[]{:S(2)}) copy-start(f32[96]{0:T(128)} %param.8) | copy-start | bytes 1156

commit v9 on v8

--- a/solution.py
+++ b/solution.py
@@ -76,34 +76,39 @@
     out[...] = new
 
 
-def late_kernel(place, middle, held, *refs):
-    count = len(LATE)
-    amps, blocks, (out, total) = refs[:count], refs[count : 2 * count], refs[2 * count :]
+def add_late(turn, place, total, amp, held, blocks):
     x, y, way = place[0], place[1], 1 - 2 * place[3]
     sources = late_sources(place)
+    slot = lax.rem(y + way * turn + 8, 8)
+    other = jnp.where(slot // 4 == x, 0, 1)
+    at = pl.ds(pl.multiple_of(other * 128, 128), 128)
+    first = lax.rem(jnp.where(other == 0, slot, 7 - slot), 4) * 2
+    for source in (first, first + 1):
+        fresh = source != sources[0]
+        for late in sources[1:]:
+            fresh &= source != late
+
+        @pl.when(fresh)
+        def _():
+            total[at, :] += times(columns(amp, 0, source), held[source])
+
+        for late, block in zip(sources, blocks):
+
+            @pl.when(source == late)
+            def _():
+                total[at, :] += times(columns(amp, 0, source), block[...])
+
+
+def third_kernel(place, middle, held, amp, low, high, total):
     total[...] = middle[...]
-    for turn, ref in zip(LATE, amps):
-        slot = lax.rem(y + way * turn + 8, 8)
-        other = jnp.where(slot // 4 == x, 0, 1)
-        at = pl.ds(pl.multiple_of(other * 128, 128), 128)
-        first = lax.rem(jnp.where(other == 0, slot, 7 - slot), 4) * 2
-        for source in (first, first + 1):
-            fresh = source != sources[0]
-            for late in sources[1:]:
-                fresh &= source != late
+    add_late(LATE[0], place, total, amp, held, (low, high))
 
-            @pl.when(fresh)
-            def _():
-                total[at, :] += times(columns(ref, 0, source), held[source])
 
-            for late, block in zip(sources, blocks):
-
-                @pl.when(source == late)
-                def _():
-                    total[at, :] += times(columns(ref, 0, source), block[...])
-
+def late_kernel(place, third, held, amp, low, high, out, total):
+    total[...] = third[...]
+    add_late(LATE[1], place, total, amp, held, (low, high))
     for n in range(2):
-        out[lax.rem(x + n, 2)] = total[n * 128 : (n + 1) * 128].T
+        out[lax.rem(place[0] + n, 2)] = total[n * 128 : (n + 1) * 128].T
 
 
 def after(block, *arrived):
@@ -154,14 +159,21 @@
         out_specs=VMEM,
         compiler_params=pltpu.CompilerParams(vmem_limit_bytes=8 << 20),
     )(place, early, amp, id3, iu4)
+    third = pl.pallas_call(
+        third_kernel,
+        out_shape=jax.ShapeDtypeStruct((256, 384), FLOAT),
+        in_specs=[SMEM] + [VMEM] * 5,
+        out_specs=VMEM,
+        compiler_params=pltpu.CompilerParams(vmem_limit_bytes=8 << 20),
+    )(place, middle, held, ad3[None], id3, iu4)
     shares = pl.pallas_call(
         late_kernel,
         out_shape=jax.ShapeDtypeStruct((2, 384, 128), FLOAT),
-        in_specs=[SMEM] + [VMEM] * 6,
+        in_specs=[SMEM] + [VMEM] * 5,
         out_specs=VMEM,
         scratch_shapes=[pltpu.VMEM((256, 384), FLOAT)],
         compiler_params=pltpu.CompilerParams(vmem_limit_bytes=8 << 20),
-    )(place, middle, held, ad3[None], au4[None], id3, iu4)
+    )(place, third, held, au4[None], id3, iu4)
     shares = lax.all_to_all(
         shares.reshape(8, 96, 128), ("xl", "xh", "core"), 0, 0, tiled=True
     )

time: 114 us -> 113 us (level)
  waiting for transfers between devices: 22.8 us -> 21.5 us
    ppermute x8, waiting for transfers between devices: 22.8 us -> 21.5 us  [forth(): return lax.ppermute(after(block, *arrived), (axis, 'core'), FORTH)]
    pallas_call x0 -> x1, Pallas kernels: none -> 1.26 us  [local(): pl.pallas_call(third_kernel, out_shape=jax.ShapeDtypeStruct((256, 384), F...]
  transfers between devices with their start and end apart: 15 -> 15, of which waited for: 6 -> 6; matrix products, arithmetic and copies ran while one was open for 0% -> 0% of each run, Pallas kernels for 5% -> 6%
where the time goes in v9:
time: 113 us
  starting transfers between devices  67.9 us (60%)
  waiting for transfers between devices  21.5 us (19%)
  blocking collectives  12.9 us (11%)
  Pallas kernels  8.1 us (7%)
  local copies, waits for them, and re-layouts  1.15 us (1%)
    ppermute x8, starting transfers between devices, forth(): return lax.ppermute(after(block, *arrived), (axis, 'core'), FORTH)  54.7 us
    ppermute x8, waiting for transfers between devices, forth(): return lax.ppermute(after(block, *arrived), (axis, 'core'), FORTH)  21.5 us
    all_to_all x1, blocking collectives, local(): lax.all_to_all(shares.reshape(8, 96, 128), ('xl', 'xh', 'core'), 0, 0, ti...  12.9 us
    ppermute x6, starting transfers between devices, back(): return lax.ppermute(after(block, *arrived), (axis, 'core'), BACK)  11.5 us
    pallas_call x1, Pallas kernels, local(): pl.pallas_call(early_kernel, out_shape=(amp_shape, held_shape, jax.ShapeD...  4.13 us
  transfers between devices with their start and end apart: 15, of which 6 were waited for; matrix products, arithmetic and copies ran while one was open for 0% of the time, Pallas kernels for 6%

profile of v9, /device:TPU:1, one launch (start us, length us, event | category | flops | bytes accessed | tf_op | source)
XLA Modules:
  0.0 112.6 jit_solution(10748790597399341184)
XLA Ops:
  0.0 0.1 pad_add_fusion.place
  0.1 11.5 %collective-permute-start.1 = (bf16[16,64,384]{2,1,0:T(8,128)(2,1)}, bf16[16,64,384]{2,1,0:T(8,128)(2,1)S(1)}, u32[]{:S(2)}, u32[]{:S(2)}) collective-permute-start(bf16[16,64,384]{2,1,0:T(8,128)(2,1)} %refs_6_), channel_id=1, source_target_pairs={{0,4},{1,29},{4,8},{5,1},{8,12},{9,5},{12,16},{13,9},{16,20},{17,1... | collective-permute-start | bytes 2359304 | tf_op jit(solution)/shard_map/ppermute | solution.py:123
  11.6 1.7 %collective-permute-start = (bf16[16,128,128]{2,1,0:T(8,128)(2,1)}, bf16[16,128,128]{2,1,0:T(8,128)(2,1)S(1)}, u32[]{:S(2)}, u32[]{:S(2)}) collective-permute-start(bf16[16,128,128]{2,1,0:T(8,128)(2,1)} %param.6), channel_id=1, source_target_pairs={{0,0},{32,448},{64,64},{96,384},{128,128},{160,320},{192,192},{224... | collective-permute-start | bytes 1572872 | tf_op jit(solution)/shard_map/ppermute | solution.py:130
  13.3 1.9 %collective-permute-start.3 = (bf16[16,64,384]{2,1,0:T(8,128)(2,1)}, bf16[16,64,384]{2,1,0:T(8,128)(2,1)S(1)}, u32[]{:S(2)}, u32[]{:S(2)}) collective-permute-start(bf16[16,64,384]{2,1,0:T(8,128)(2,1)} %refs_6_), channel_id=1, source_target_pairs={{4,0},{29,1},{8,4},{1,5},{12,8},{5,9},{16,12},{9,13},{20,16},{13,1... | collective-permute-start | bytes 2359304 | tf_op jit(solution)/shard_map/ppermute | solution.py:126
  15.2 9.2 %collective-permute-done.1.refs_7_ = bf16[16,64,384]{2,1,0:T(8,128)(2,1)S(1)} collective-permute-done((bf16[16,64,384]{2,1,0:T(8,128)(2,1)}, bf16[16,64,384]{2,1,0:T(8,128)(2,1)S(1)}, u32[]{:S(2)}, u32[]{:S(2)}) %collective-permute-start.1) | collective-permute-done | bytes 786464 | tf_op jit(solution)/shard_map/ppermute | solution.py:123
  24.4 5.2 %collective-permute-start.9 = (bf16[16,64,384]{2,1,0:T(8,128)(2,1)S(1)}, bf16[16,64,384]{2,1,0:T(8,128)(2,1)S(1)}, u32[]{:S(2)}, u32[]{:S(2)}) collective-permute-start(bf16[16,64,384]{2,1,0:T(8,128)(2,1)S(1)} %collective-permute-done.1.refs_7_), channel_id=1, source_target_pairs={{0,4},{1,29},{4,8},{5,1},{8,12},{9,5},{12,16},{13,9},{16,20},{17,1... | collective-permute-start | bytes 2359304 | tf_op jit(solution)/shard_map/ppermute | solution.py:123
  29.6 10.9 %collective-permute-start.2 = (bf16[16,128,128]{2,1,0:T(8,128)(2,1)S(1)}, bf16[16,128,128]{2,1,0:T(8,128)(2,1)S(1)}, u32[]{:S(2)}, u32[]{:S(2)}) collective-permute-start(bf16[16,128,128]{2,1,0:T(8,128)(2,1)S(1)} %collective-permute-done.refs_0_), channel_id=1, source_target_pairs={{0,64},{1,449},{64,128},{65,1},{128,192},{129,65},{192,256},{193,1... | collective-permute-start | bytes 1572872 | tf_op jit(solution)/shard_map/ppermute | solution.py:123
  40.5 1.9 %collective-permute-start.5 = (bf16[16,64,384]{2,1,0:T(8,128)(2,1)S(1)}, bf16[16,64,384]{2,1,0:T(8,128)(2,1)S(1)}, u32[]{:S(2)}, u32[]{:S(2)}) collective-permute-start(bf16[16,64,384]{2,1,0:T(8,128)(2,1)S(1)} %collective-permute-done.3.refs_10_), channel_id=1, source_target_pairs={{4,0},{29,1},{8,4},{1,5},{12,8},{5,9},{16,12},{9,13},{20,16},{13,1... | collective-permute-start | bytes 2359304 | tf_op jit(solution)/shard_map/ppermute | solution.py:126
  42.5 1.9 %collective-permute-start.7 = (bf16[16,128,128]{2,1,0:T(8,128)(2,1)S(1)}, bf16[16,128,128]{2,1,0:T(8,128)(2,1)S(1)}, u32[]{:S(2)}, u32[]{:S(2)}) collective-permute-start(bf16[16,128,128]{2,1,0:T(8,128)(2,1)S(1)} %collective-permute-done.refs_0_), channel_id=1, source_target_pairs={{64,0},{449,1},{128,64},{1,65},{192,128},{65,129},{256,192},{129,1... | collective-permute-start | bytes 1572872 | tf_op jit(solution)/shard_map/ppermute | solution.py:126
  44.4 2.2 %collective-permute-done.2.refs_1_ = bf16[16,128,128]{2,1,0:T(8,128)(2,1)S(1)} collective-permute-done((bf16[16,128,128]{2,1,0:T(8,128)(2,1)S(1)}, bf16[16,128,128]{2,1,0:T(8,128)(2,1)S(1)}, u32[]{:S(2)}, u32[]{:S(2)}) %collective-permute-start.2) | collective-permute-done | bytes 524320 | tf_op jit(solution)/shard_map/ppermute | solution.py:123
  46.6 5.0 %collective-permute-start.4 = (bf16[16,128,128]{2,1,0:T(8,128)(2,1)S(1)}, bf16[16,128,128]{2,1,0:T(8,128)(2,1)S(1)}, u32[]{:S(2)}, u32[]{:S(2)}) collective-permute-start(bf16[16,128,128]{2,1,0:T(8,128)(2,1)S(1)} %collective-permute-done.2.refs_1_), channel_id=1, source_target_pairs={{0,64},{1,449},{64,128},{65,1},{128,192},{129,65},{192,256},{193,1... | collective-permute-start | bytes 1572872 | tf_op jit(solution)/shard_map/ppermute | solution.py:123
  51.7 7.2 %collective-permute-start.10 = (bf16[16,64,384]{2,1,0:T(8,128)(2,1)S(1)}, bf16[16,64,384]{2,1,0:T(8,128)(2,1)S(1)}, u32[]{:S(2)}, u32[]{:S(2)}) collective-permute-start(bf16[16,64,384]{2,1,0:T(8,128)(2,1)S(1)} %collective-permute-done.9.refs_8_), channel_id=1, source_target_pairs={{0,4},{1,29},{4,8},{5,1},{8,12},{9,5},{12,16},{13,9},{16,20},{17,1... | collective-permute-start | bytes 2359304 | tf_op jit(solution)/shard_map/ppermute | solution.py:123
  58.8 4.2 %collective-permute-done.4.refs_2_ = bf16[16,128,128]{2,1,0:T(8,128)(2,1)S(1)} collective-permute-done((bf16[16,128,128]{2,1,0:T(8,128)(2,1)S(1)}, bf16[16,128,128]{2,1,0:T(8,128)(2,1)S(1)}, u32[]{:S(2)}, u32[]{:S(2)}) %collective-permute-start.4) | collective-permute-done | bytes 524320 | tf_op jit(solution)/shard_map/ppermute | solution.py:123
  63.0 1.9 %collective-permute-start.8 = (bf16[16,128,128]{2,1,0:T(8,128)(2,1)S(1)}, bf16[16,128,128]{2,1,0:T(8,128)(2,1)S(1)}, u32[]{:S(2)}, u32[]{:S(2)}) collective-permute-start(bf16[16,128,128]{2,1,0:T(8,128)(2,1)S(1)} %collective-permute-done.7.refs_4_), channel_id=1, source_target_pairs={{64,0},{449,1},{128,64},{1,65},{192,128},{65,129},{256,192},{129,1... | collective-permute-start | bytes 1572872 | tf_op jit(solution)/shard_map/ppermute | solution.py:126
  65.0 5.3 %collective-permute-start.6 = (bf16[16,128,128]{2,1,0:T(8,128)(2,1)S(1)}, bf16[16,128,128]{2,1,0:T(8,128)(2,1)S(1)}, u32[]{:S(2)}, u32[]{:S(2)}) collective-permute-start(bf16[16,128,128]{2,1,0:T(8,128)(2,1)S(1)} %collective-permute-done.4.refs_2_), channel_id=1, source_target_pairs={{0,64},{1,449},{64,128},{65,1},{128,192},{129,65},{192,256},{193,1... | collective-permute-start | bytes 1572872 | tf_op jit(solution)/shard_map/ppermute | solution.py:123
  70.3 1.9 %collective-permute-start.11 = (bf16[16,64,384]{2,1,0:T(8,128)(2,1)S(1)}, bf16[16,64,384]{2,1,0:T(8,128)(2,1)S(1)}, u32[]{:S(2)}, u32[]{:S(2)}) collective-permute-start(bf16[16,64,384]{2,1,0:T(8,128)(2,1)S(1)} %collective-permute-done.5.refs_11_), channel_id=1, source_target_pairs={{4,0},{29,1},{8,4},{1,5},{12,8},{5,9},{16,12},{9,13},{20,16},{13,1... | collective-permute-start | bytes 2359304 | tf_op jit(solution)/shard_map/ppermute | solution.py:126
  72.2 4.6 %collective-permute-start.12 = (bf16[16,64,384]{2,1,0:T(8,128)(2,1)S(1)}, bf16[16,64,384]{2,1,0:T(8,128)(2,1)S(1)}, u32[]{:S(2)}, u32[]{:S(2)}) collective-permute-start(bf16[16,64,384]{2,1,0:T(8,128)(2,1)S(1)} %collective-permute-done.10.refs_9_), channel_id=1, source_target_pairs={{0,4},{1,29},{4,8},{5,1},{8,12},{9,5},{12,16},{13,9},{16,20},{17,1... | collective-permute-start | bytes 2359304 | tf_op jit(solution)/shard_map/ppermute | solution.py:123
  76.8 3.8 %collective-permute-done.6.refs_3_ = bf16[16,128,128]{2,1,0:T(8,128)(2,1)S(1)} collective-permute-done((bf16[16,128,128]{2,1,0:T(8,128)(2,1)S(1)}, bf16[16,128,128]{2,1,0:T(8,128)(2,1)S(1)}, u32[]{:S(2)}, u32[]{:S(2)}) %collective-permute-start.6) | collective-permute-done | bytes 524320 | tf_op jit(solution)/shard_map/ppermute | solution.py:123
  80.6 1.9 %collective-permute-start.13 = (bf16[16,128,128]{2,1,0:T(8,128)(2,1)S(1)}, bf16[16,128,128]{2,1,0:T(8,128)(2,1)S(1)}, u32[]{:S(2)}, u32[]{:S(2)}) collective-permute-start(bf16[16,128,128]{2,1,0:T(8,128)(2,1)S(1)} %collective-permute-done.8.refs_5_), channel_id=1, source_target_pairs={{64,0},{449,1},{128,64},{1,65},{192,128},{65,129},{256,192},{129,1... | collective-permute-start | bytes 1572872 | tf_op jit(solution)/shard_map/ppermute | solution.py:126
  82.5 5.0 %collective-permute-start.14 = (bf16[16,128,128]{2,1,0:T(8,128)(2,1)S(1)}, bf16[16,128,128]{2,1,0:T(8,128)(2,1)S(1)}, u32[]{:S(2)}, u32[]{:S(2)}) collective-permute-start(bf16[16,128,128]{2,1,0:T(8,128)(2,1)S(1)} %collective-permute-done.6.refs_3_), channel_id=1, source_target_pairs={{0,64},{1,449},{64,128},{65,1},{128,192},{129,65},{192,256},{193,1... | collective-permute-start | bytes 1572872 | tf_op jit(solution)/shard_map/ppermute | solution.py:123
  87.6 0.0 copy-start
  87.6 1.1 copy-done
  88.7 4.1 %shard_map.55 = (bf16[8,16,128,128]{3,2,1,0:T(8,128)(2,1)S(1)}, bf16[8,16,64,384]{3,2,1,0:T(8,128)(2,1)S(1)}, f32[256,384]{1,0:T(8,128)S(1)}) custom-call(s32[4]{0:T(128)S(1)} %pad_add_fusion.place, bf16[16,128,128]{2,1,0:T(8,128)(2,1)S(1)} %collective-permute-done.refs_0_, bf16[16,128,128]{2,1,0:T(8,128)(2,1)S(1)} %collective-permute-done.2.refs_1_, ...), custom_call_target="tpu_custom_call" | custom-call | flops 1073741824 | bytes 16777216 | tf_op jit(solution)/shard_map/pallas_call | solution.py:146
  92.9 1.3 %collective-permute-done.12.refs_1_.high = bf16[16,64,384]{2,1,0:T(8,128)(2,1)S(1)} collective-permute-done((bf16[16,64,384]{2,1,0:T(8,128)(2,1)S(1)}, bf16[16,64,384]{2,1,0:T(8,128)(2,1)S(1)}, u32[]{:S(2)}, u32[]{:S(2)}) %collective-permute-start.12) | collective-permute-done | bytes 786464 | tf_op jit(solution)/shard_map/ppermute | solution.py:123
  94.1 1.3 %shard_map.56.middle = f32[256,384]{1,0:T(8,128)S(1)} custom-call(s32[4]{0:T(128)S(1)} %pad_add_fusion.place, f32[256,384]{1,0:T(8,128)S(1)} %get-tuple-element.30.early, bf16[8,16,128,128]{3,2,1,0:T(8,128)(2,1)S(1)} %get-tuple-element.31.amp, bf16[16,64,384]{2,1,0:T(8,128)(2,1)S(1)} %collective-permute-done.11.refs_0_.low, ...), custom_call_target="tpu_custom_call" | custom-call | tf_op jit(solution)/shard_map/pallas_call | solution.py:155
  95.4 1.3 %shard_map.57.third = f32[256,384]{1,0:T(8,128)S(1)} custom-call(s32[4]{0:T(128)S(1)} %pad_add_fusion.place, f32[256,384]{1,0:T(8,128)S(1)} %shard_map.56.middle, bf16[8,16,64,384]{3,2,1,0:T(8,128)(2,1)S(1)} %get-tuple-element.34.held, bf16[1,16,128,128]{3,2,1,0:T(8,128)(2,1)S(1)} %bitcast.9, bf16[16,64,384]{2,1,0:T(8,128)(2,1)S(1)} %collective-permute-done.11.refs_0_.low, ...), custom_call_target="tpu_custom_call" | custom-call | tf_op jit(solution)/shard_map/pallas_call | solution.py:162
  96.7 0.0 copy-start.1
  96.7 0.0 copy-start.2
  96.8 0.8 collective-permute-done.14
  97.5 1.4 %shard_map.58 = f32[2,384,128]{2,1,0:T(8,128)S(1)} custom-call(s32[4]{0:T(128)S(1)} %pad_add_fusion.place, f32[256,384]{1,0:T(8,128)S(1)} %shard_map.57.third, bf16[8,16,64,384]{3,2,1,0:T(8,128)(2,1)S(1)} %get-tuple-element.34.held, bf16[1,16,128,128]{3,2,1,0:T(8,128)(2,1)S(1)} %bitcast.8, bf16[16,64,384]{2,1,0:T(8,128)(2,1)S(1)} %collective-permute-done.11.refs_0_.low, ...), custom_call_target="tpu_custom_call" | custom-call | tf_op jit(solution)/shard_map/pallas_call | solution.py:169
  98.9 12.9 %all_to_all.5 = f32[8,96,128]{2,1,0:T(8,128)S(1)} all-to-all(f32[8,96,128]{2,1,0:T(8,128)S(1)} %bitcast.7), channel_id=1, replica_groups=mesh['y'=8,'xl'=2,'z'=8,'xh'=2,'core'=2] {'xl','xh','core'}, dimensions={0} | all-to-all | bytes 786432 | tf_op jit(solution)/shard_map/all_to_all | solution.py:177
  111.9 0.7 add_divide_fusion
  (14 shorter events, 0.1 us)
Async XLA Ops:
  0.1 24.3 %collective-permute-start.1 = (bf16[16,64,384]{2,1,0:T(8,128)(2,1)}, bf16[16,64,384]{2,1,0:T(8,128)(2,1)S(1)}, u32[]{:S(2)}, u32[]{:S(2)}) collective-permute-start(bf16[16,64,384]{2,1,0:T(8,128)(2,1)} %refs_6_), channel_id=1, source_target_pairs={{0,4},{1,29},{4,8},{5,1},{8,12},{9,5},{12,16},{13,9},{16,20},{17,1... | collective-permute-start | bytes 2359304 | tf_op jit(solution)/shard_map/ppermute | solution.py:123
  11.6 18.0 %collective-permute-start = (bf16[16,128,128]{2,1,0:T(8,128)(2,1)}, bf16[16,128,128]{2,1,0:T(8,128)(2,1)S(1)}, u32[]{:S(2)}, u32[]{:S(2)}) collective-permute-start(bf16[16,128,128]{2,1,0:T(8,128)(2,1)} %param.6), channel_id=1, source_target_pairs={{0,0},{32,448},{64,64},{96,384},{128,128},{160,320},{192,192},{224... | collective-permute-start | bytes 1572872 | tf_op jit(solution)/shard_map/ppermute | solution.py:130
  13.3 27.2 %collective-permute-start.3 = (bf16[16,64,384]{2,1,0:T(8,128)(2,1)}, bf16[16,64,384]{2,1,0:T(8,128)(2,1)S(1)}, u32[]{:S(2)}, u32[]{:S(2)}) collective-permute-start(bf16[16,64,384]{2,1,0:T(8,128)(2,1)} %refs_6_), channel_id=1, source_target_pairs={{4,0},{29,1},{8,4},{1,5},{12,8},{5,9},{16,12},{9,13},{20,16},{13,1... | collective-permute-start | bytes 2359304 | tf_op jit(solution)/shard_map/ppermute | solution.py:126
  24.4 27.2 %collective-permute-start.9 = (bf16[16,64,384]{2,1,0:T(8,128)(2,1)S(1)}, bf16[16,64,384]{2,1,0:T(8,128)(2,1)S(1)}, u32[]{:S(2)}, u32[]{:S(2)}) collective-permute-start(bf16[16,64,384]{2,1,0:T(8,128)(2,1)S(1)} %collective-permute-done.1.refs_7_), channel_id=1, source_target_pairs={{0,4},{1,29},{4,8},{5,1},{8,12},{9,5},{12,16},{13,9},{16,20},{17,1... | collective-permute-start | bytes 2359304 | tf_op jit(solution)/shard_map/ppermute | solution.py:123
  29.6 17.0 %collective-permute-start.2 = (bf16[16,128,128]{2,1,0:T(8,128)(2,1)S(1)}, bf16[16,128,128]{2,1,0:T(8,128)(2,1)S(1)}, u32[]{:S(2)}, u32[]{:S(2)}) collective-permute-start(bf16[16,128,128]{2,1,0:T(8,128)(2,1)S(1)} %collective-permute-done.refs_0_), channel_id=1, source_target_pairs={{0,64},{1,449},{64,128},{65,1},{128,192},{129,65},{192,256},{193,1... | collective-permute-start | bytes 1572872 | tf_op jit(solution)/shard_map/ppermute | solution.py:123
  40.5 24.4 %collective-permute-start.5 = (bf16[16,64,384]{2,1,0:T(8,128)(2,1)S(1)}, bf16[16,64,384]{2,1,0:T(8,128)(2,1)S(1)}, u32[]{:S(2)}, u32[]{:S(2)}) collective-permute-start(bf16[16,64,384]{2,1,0:T(8,128)(2,1)S(1)} %collective-permute-done.3.refs_10_), channel_id=1, source_target_pairs={{4,0},{29,1},{8,4},{1,5},{12,8},{5,9},{16,12},{9,13},{20,16},{13,1... | collective-permute-start | bytes 2359304 | tf_op jit(solution)/shard_map/ppermute | solution.py:126
  42.5 16.4 %collective-permute-start.7 = (bf16[16,128,128]{2,1,0:T(8,128)(2,1)S(1)}, bf16[16,128,128]{2,1,0:T(8,128)(2,1)S(1)}, u32[]{:S(2)}, u32[]{:S(2)}) collective-permute-start(bf16[16,128,128]{2,1,0:T(8,128)(2,1)S(1)} %collective-permute-done.refs_0_), channel_id=1, source_target_pairs={{64,0},{449,1},{128,64},{1,65},{192,128},{65,129},{256,192},{129,1... | collective-permute-start | bytes 1572872 | tf_op jit(solution)/shard_map/ppermute | solution.py:126
  46.6 16.4 %collective-permute-start.4 = (bf16[16,128,128]{2,1,0:T(8,128)(2,1)S(1)}, bf16[16,128,128]{2,1,0:T(8,128)(2,1)S(1)}, u32[]{:S(2)}, u32[]{:S(2)}) collective-permute-start(bf16[16,128,128]{2,1,0:T(8,128)(2,1)S(1)} %collective-permute-done.2.refs_1_), channel_id=1, source_target_pairs={{0,64},{1,449},{64,128},{65,1},{128,192},{129,65},{192,256},{193,1... | collective-permute-start | bytes 1572872 | tf_op jit(solution)/shard_map/ppermute | solution.py:123
  51.7 20.6 %collective-permute-start.10 = (bf16[16,64,384]{2,1,0:T(8,128)(2,1)S(1)}, bf16[16,64,384]{2,1,0:T(8,128)(2,1)S(1)}, u32[]{:S(2)}, u32[]{:S(2)}) collective-permute-start(bf16[16,64,384]{2,1,0:T(8,128)(2,1)S(1)} %collective-permute-done.9.refs_8_), channel_id=1, source_target_pairs={{0,4},{1,29},{4,8},{5,1},{8,12},{9,5},{12,16},{13,9},{16,20},{17,1... | collective-permute-start | bytes 2359304 | tf_op jit(solution)/shard_map/ppermute | solution.py:123
  63.0 13.8 %collective-permute-start.8 = (bf16[16,128,128]{2,1,0:T(8,128)(2,1)S(1)}, bf16[16,128,128]{2,1,0:T(8,128)(2,1)S(1)}, u32[]{:S(2)}, u32[]{:S(2)}) collective-permute-start(bf16[16,128,128]{2,1,0:T(8,128)(2,1)S(1)} %collective-permute-done.7.refs_4_), channel_id=1, source_target_pairs={{64,0},{449,1},{128,64},{1,65},{192,128},{65,129},{256,192},{129,1... | collective-permute-start | bytes 1572872 | tf_op jit(solution)/shard_map/ppermute | solution.py:126
  65.0 15.7 %collective-permute-start.6 = (bf16[16,128,128]{2,1,0:T(8,128)(2,1)S(1)}, bf16[16,128,128]{2,1,0:T(8,128)(2,1)S(1)}, u32[]{:S(2)}, u32[]{:S(2)}) collective-permute-start(bf16[16,128,128]{2,1,0:T(8,128)(2,1)S(1)} %collective-permute-done.4.refs_2_), channel_id=1, source_target_pairs={{0,64},{1,449},{64,128},{65,1},{128,192},{129,65},{192,256},{193,1... | collective-permute-start | bytes 1572872 | tf_op jit(solution)/shard_map/ppermute | solution.py:123
  70.3 22.6 %collective-permute-start.11 = (bf16[16,64,384]{2,1,0:T(8,128)(2,1)S(1)}, bf16[16,64,384]{2,1,0:T(8,128)(2,1)S(1)}, u32[]{:S(2)}, u32[]{:S(2)}) collective-permute-start(bf16[16,64,384]{2,1,0:T(8,128)(2,1)S(1)} %collective-permute-done.5.refs_11_), channel_id=1, source_target_pairs={{4,0},{29,1},{8,4},{1,5},{12,8},{5,9},{16,12},{9,13},{20,16},{13,1... | collective-permute-start | bytes 2359304 | tf_op jit(solution)/shard_map/ppermute | solution.py:126
  72.2 21.9 %collective-permute-start.12 = (bf16[16,64,384]{2,1,0:T(8,128)(2,1)S(1)}, bf16[16,64,384]{2,1,0:T(8,128)(2,1)S(1)}, u32[]{:S(2)}, u32[]{:S(2)}) collective-permute-start(bf16[16,64,384]{2,1,0:T(8,128)(2,1)S(1)} %collective-permute-done.10.refs_9_), channel_id=1, source_target_pairs={{0,4},{1,29},{4,8},{5,1},{8,12},{9,5},{12,16},{13,9},{16,20},{17,1... | collective-permute-start | bytes 2359304 | tf_op jit(solution)/shard_map/ppermute | solution.py:123
  80.6 14.8 %collective-permute-start.13 = (bf16[16,128,128]{2,1,0:T(8,128)(2,1)S(1)}, bf16[16,128,128]{2,1,0:T(8,128)(2,1)S(1)}, u32[]{:S(2)}, u32[]{:S(2)}) collective-permute-start(bf16[16,128,128]{2,1,0:T(8,128)(2,1)S(1)} %collective-permute-done.8.refs_5_), channel_id=1, source_target_pairs={{64,0},{449,1},{128,64},{1,65},{192,128},{65,129},{256,192},{129,1... | collective-permute-start | bytes 1572872 | tf_op jit(solution)/shard_map/ppermute | solution.py:126
  82.5 15.0 %collective-permute-start.14 = (bf16[16,128,128]{2,1,0:T(8,128)(2,1)S(1)}, bf16[16,128,128]{2,1,0:T(8,128)(2,1)S(1)}, u32[]{:S(2)}, u32[]{:S(2)}) collective-permute-start(bf16[16,128,128]{2,1,0:T(8,128)(2,1)S(1)} %collective-permute-done.6.refs_3_), channel_id=1, source_target_pairs={{0,64},{1,449},{64,128},{65,1},{128,192},{129,65},{192,256},{193,1... | collective-permute-start | bytes 1572872 | tf_op jit(solution)/shard_map/ppermute | solution.py:123
  87.6 1.1 %copy-start = (bf16[16,64,384]{2,1,0:T(8,128)(2,1)S(1)}, bf16[16,64,384]{2,1,0:T(8,128)(2,1)}, u32[]{:S(2)}) copy-start(bf16[16,64,384]{2,1,0:T(8,128)(2,1)} %refs_6_) | copy-start | bytes 2359300
  96.7 15.1 %copy-start.1 = (bf16[96,128]{1,0:T(8,128)(2,1)S(1)}, bf16[96,128]{1,0:T(8,128)(2,1)}, u32[]{:S(2)}) copy-start(bf16[96,128]{1,0:T(8,128)(2,1)} %param.7) | copy-start | bytes 73732
  96.7 15.1 %copy-start.2 = (f32[128]{0:T(128)S(1)}, f32[128]{0:T(128)}, u32[]{:S(2)}) copy-start(f32[128]{0:T(128)} %param.9) | copy-start | bytes 1540
  96.7 15.1 %copy-start.3 = (f32[96]{0:T(128)S(1)}, f32[96]{0:T(128)}, u32[]{:S(2)}) copy-start(f32[96]{0:T(128)} %param.8) | copy-start | bytes 1156

commit v10 on v9

--- a/solution.py
+++ b/solution.py
@@ -56,11 +56,11 @@
         copy.wait()
     total = None
     for j, turn in enumerate(turns):
-        copies[count + j].wait()
-        source = lax.rem(z + turn, 8)
-        part = piece(x, amp, source, held[source])
+        part = piece(x, amp, lax.rem(z + turn, 8), blocks[j])
         total = part if total is None else total + part
     out[...] = total
+    for copy in copies[count:]:
+        copy.wait()
 
 
 def late_sources(place):
@@ -146,7 +146,7 @@
     amp, held, early = pl.pallas_call(
         early_kernel,
         out_shape=(amp_shape, held_shape, jax.ShapeDtypeStruct((256, 384), FLOAT)),
-        in_specs=[SMEM] + [ANY] * 12,
+        in_specs=[SMEM] + [ANY] * 6 + [VMEM] * 6,
         out_specs=(VMEM, VMEM, VMEM),
         scratch_shapes=[pltpu.SemaphoreType.DMA((12,))],
         compiler_params=pltpu.CompilerParams(vmem_limit_bytes=24 << 20),

time: 113 us -> 113 us (level)
  transfers between devices with their start and end apart: 15 -> 15, of which waited for: 6 -> 6; matrix products, arithmetic and copies ran while one was open for 0% -> 0% of each run, Pallas kernels for 6% -> 5%
where the time goes in v10:
time: 113 us
  starting transfers between devices  67.9 us (60%)
  waiting for transfers between devices  22.4 us (20%)
  blocking collectives  12.9 us (11%)
  Pallas kernels  7.22 us (6%)
  local copies, waits for them, and re-layouts  1.15 us (1%)
    ppermute x8, starting transfers between devices, forth(): return lax.ppermute(after(block, *arrived), (axis, 'core'), FORTH)  54.7 us
    ppermute x8, waiting for transfers between devices, forth(): return lax.ppermute(after(block, *arrived), (axis, 'core'), FORTH)  22.4 us
    all_to_all x1, blocking collectives, local(): lax.all_to_all(shares.reshape(8, 96, 128), ('xl', 'xh', 'core'), 0, 0, ti...  12.9 us
    ppermute x6, starting transfers between devices, back(): return lax.ppermute(after(block, *arrived), (axis, 'core'), BACK)  11.5 us
    pallas_call x1, Pallas kernels, local(): pl.pallas_call(early_kernel, out_shape=(amp_shape, held_shape, jax.ShapeD...  3.26 us
  transfers between devices with their start and end apart: 15, of which 6 were waited for; matrix products, arithmetic and copies ran while one was open for 0% of the time, Pallas kernels for 5%

profile of v10, /device:TPU:1, one launch (start us, length us, event | category | flops | bytes accessed | tf_op | source)
XLA Modules:
  0.0 112.6 jit_solution(5609932106875391240)
XLA Ops:
  0.0 0.1 pad_add_fusion.place
  0.1 11.5 %collective-permute-start.1 = (bf16[16,64,384]{2,1,0:T(8,128)(2,1)}, bf16[16,64,384]{2,1,0:T(8,128)(2,1)S(1)}, u32[]{:S(2)}, u32[]{:S(2)}) collective-permute-start(bf16[16,64,384]{2,1,0:T(8,128)(2,1)} %refs_6_), channel_id=1, source_target_pairs={{0,4},{1,29},{4,8},{5,1},{8,12},{9,5},{12,16},{13,9},{16,20},{17,1... | collective-permute-start | bytes 2359304 | tf_op jit(solution)/shard_map/ppermute | solution.py:123
  11.6 1.7 %collective-permute-start = (bf16[16,128,128]{2,1,0:T(8,128)(2,1)}, bf16[16,128,128]{2,1,0:T(8,128)(2,1)S(1)}, u32[]{:S(2)}, u32[]{:S(2)}) collective-permute-start(bf16[16,128,128]{2,1,0:T(8,128)(2,1)} %param.6), channel_id=1, source_target_pairs={{0,0},{32,448},{64,64},{96,384},{128,128},{160,320},{192,192},{224... | collective-permute-start | bytes 1572872 | tf_op jit(solution)/shard_map/ppermute | solution.py:130
  13.3 1.9 %collective-permute-start.3 = (bf16[16,64,384]{2,1,0:T(8,128)(2,1)}, bf16[16,64,384]{2,1,0:T(8,128)(2,1)S(1)}, u32[]{:S(2)}, u32[]{:S(2)}) collective-permute-start(bf16[16,64,384]{2,1,0:T(8,128)(2,1)} %refs_6_), channel_id=1, source_target_pairs={{4,0},{29,1},{8,4},{1,5},{12,8},{5,9},{16,12},{9,13},{20,16},{13,1... | collective-permute-start | bytes 2359304 | tf_op jit(solution)/shard_map/ppermute | solution.py:126
  15.2 9.2 %collective-permute-done.1.refs_7_ = bf16[16,64,384]{2,1,0:T(8,128)(2,1)S(1)} collective-permute-done((bf16[16,64,384]{2,1,0:T(8,128)(2,1)}, bf16[16,64,384]{2,1,0:T(8,128)(2,1)S(1)}, u32[]{:S(2)}, u32[]{:S(2)}) %collective-permute-start.1) | collective-permute-done | bytes 786464 | tf_op jit(solution)/shard_map/ppermute | solution.py:123
  24.4 5.2 %collective-permute-start.9 = (bf16[16,64,384]{2,1,0:T(8,128)(2,1)S(1)}, bf16[16,64,384]{2,1,0:T(8,128)(2,1)S(1)}, u32[]{:S(2)}, u32[]{:S(2)}) collective-permute-start(bf16[16,64,384]{2,1,0:T(8,128)(2,1)S(1)} %collective-permute-done.1.refs_7_), channel_id=1, source_target_pairs={{0,4},{1,29},{4,8},{5,1},{8,12},{9,5},{12,16},{13,9},{16,20},{17,1... | collective-permute-start | bytes 2359304 | tf_op jit(solution)/shard_map/ppermute | solution.py:123
  29.6 10.9 %collective-permute-start.2 = (bf16[16,128,128]{2,1,0:T(8,128)(2,1)S(1)}, bf16[16,128,128]{2,1,0:T(8,128)(2,1)S(1)}, u32[]{:S(2)}, u32[]{:S(2)}) collective-permute-start(bf16[16,128,128]{2,1,0:T(8,128)(2,1)S(1)} %collective-permute-done.refs_0_), channel_id=1, source_target_pairs={{0,64},{1,449},{64,128},{65,1},{128,192},{129,65},{192,256},{193,1... | collective-permute-start | bytes 1572872 | tf_op jit(solution)/shard_map/ppermute | solution.py:123
  40.5 1.9 %collective-permute-start.5 = (bf16[16,64,384]{2,1,0:T(8,128)(2,1)S(1)}, bf16[16,64,384]{2,1,0:T(8,128)(2,1)S(1)}, u32[]{:S(2)}, u32[]{:S(2)}) collective-permute-start(bf16[16,64,384]{2,1,0:T(8,128)(2,1)S(1)} %collective-permute-done.3.refs_10_), channel_id=1, source_target_pairs={{4,0},{29,1},{8,4},{1,5},{12,8},{5,9},{16,12},{9,13},{20,16},{13,1... | collective-permute-start | bytes 2359304 | tf_op jit(solution)/shard_map/ppermute | solution.py:126
  42.5 1.9 %collective-permute-start.7 = (bf16[16,128,128]{2,1,0:T(8,128)(2,1)S(1)}, bf16[16,128,128]{2,1,0:T(8,128)(2,1)S(1)}, u32[]{:S(2)}, u32[]{:S(2)}) collective-permute-start(bf16[16,128,128]{2,1,0:T(8,128)(2,1)S(1)} %collective-permute-done.refs_0_), channel_id=1, source_target_pairs={{64,0},{449,1},{128,64},{1,65},{192,128},{65,129},{256,192},{129,1... | collective-permute-start | bytes 1572872 | tf_op jit(solution)/shard_map/ppermute | solution.py:126
  44.4 2.2 %collective-permute-done.2.refs_1_ = bf16[16,128,128]{2,1,0:T(8,128)(2,1)S(1)} collective-permute-done((bf16[16,128,128]{2,1,0:T(8,128)(2,1)S(1)}, bf16[16,128,128]{2,1,0:T(8,128)(2,1)S(1)}, u32[]{:S(2)}, u32[]{:S(2)}) %collective-permute-start.2) | collective-permute-done | bytes 524320 | tf_op jit(solution)/shard_map/ppermute | solution.py:123
  46.6 5.0 %collective-permute-start.4 = (bf16[16,128,128]{2,1,0:T(8,128)(2,1)S(1)}, bf16[16,128,128]{2,1,0:T(8,128)(2,1)S(1)}, u32[]{:S(2)}, u32[]{:S(2)}) collective-permute-start(bf16[16,128,128]{2,1,0:T(8,128)(2,1)S(1)} %collective-permute-done.2.refs_1_), channel_id=1, source_target_pairs={{0,64},{1,449},{64,128},{65,1},{128,192},{129,65},{192,256},{193,1... | collective-permute-start | bytes 1572872 | tf_op jit(solution)/shard_map/ppermute | solution.py:123
  51.7 7.2 %collective-permute-start.10 = (bf16[16,64,384]{2,1,0:T(8,128)(2,1)S(1)}, bf16[16,64,384]{2,1,0:T(8,128)(2,1)S(1)}, u32[]{:S(2)}, u32[]{:S(2)}) collective-permute-start(bf16[16,64,384]{2,1,0:T(8,128)(2,1)S(1)} %collective-permute-done.9.refs_8_), channel_id=1, source_target_pairs={{0,4},{1,29},{4,8},{5,1},{8,12},{9,5},{12,16},{13,9},{16,20},{17,1... | collective-permute-start | bytes 2359304 | tf_op jit(solution)/shard_map/ppermute | solution.py:123
  58.8 4.2 %collective-permute-done.4.refs_2_ = bf16[16,128,128]{2,1,0:T(8,128)(2,1)S(1)} collective-permute-done((bf16[16,128,128]{2,1,0:T(8,128)(2,1)S(1)}, bf16[16,128,128]{2,1,0:T(8,128)(2,1)S(1)}, u32[]{:S(2)}, u32[]{:S(2)}) %collective-permute-start.4) | collective-permute-done | bytes 524320 | tf_op jit(solution)/shard_map/ppermute | solution.py:123
  63.0 1.9 %collective-permute-start.8 = (bf16[16,128,128]{2,1,0:T(8,128)(2,1)S(1)}, bf16[16,128,128]{2,1,0:T(8,128)(2,1)S(1)}, u32[]{:S(2)}, u32[]{:S(2)}) collective-permute-start(bf16[16,128,128]{2,1,0:T(8,128)(2,1)S(1)} %collective-permute-done.7.refs_4_), channel_id=1, source_target_pairs={{64,0},{449,1},{128,64},{1,65},{192,128},{65,129},{256,192},{129,1... | collective-permute-start | bytes 1572872 | tf_op jit(solution)/shard_map/ppermute | solution.py:126
  65.0 5.3 %collective-permute-start.6 = (bf16[16,128,128]{2,1,0:T(8,128)(2,1)S(1)}, bf16[16,128,128]{2,1,0:T(8,128)(2,1)S(1)}, u32[]{:S(2)}, u32[]{:S(2)}) collective-permute-start(bf16[16,128,128]{2,1,0:T(8,128)(2,1)S(1)} %collective-permute-done.4.refs_2_), channel_id=1, source_target_pairs={{0,64},{1,449},{64,128},{65,1},{128,192},{129,65},{192,256},{193,1... | collective-permute-start | bytes 1572872 | tf_op jit(solution)/shard_map/ppermute | solution.py:123
  70.3 1.9 %collective-permute-start.11 = (bf16[16,64,384]{2,1,0:T(8,128)(2,1)S(1)}, bf16[16,64,384]{2,1,0:T(8,128)(2,1)S(1)}, u32[]{:S(2)}, u32[]{:S(2)}) collective-permute-start(bf16[16,64,384]{2,1,0:T(8,128)(2,1)S(1)} %collective-permute-done.5.refs_11_), channel_id=1, source_target_pairs={{4,0},{29,1},{8,4},{1,5},{12,8},{5,9},{16,12},{9,13},{20,16},{13,1... | collective-permute-start | bytes 2359304 | tf_op jit(solution)/shard_map/ppermute | solution.py:126
  72.2 4.6 %collective-permute-start.12 = (bf16[16,64,384]{2,1,0:T(8,128)(2,1)S(1)}, bf16[16,64,384]{2,1,0:T(8,128)(2,1)S(1)}, u32[]{:S(2)}, u32[]{:S(2)}) collective-permute-start(bf16[16,64,384]{2,1,0:T(8,128)(2,1)S(1)} %collective-permute-done.10.refs_9_), channel_id=1, source_target_pairs={{0,4},{1,29},{4,8},{5,1},{8,12},{9,5},{12,16},{13,9},{16,20},{17,1... | collective-permute-start | bytes 2359304 | tf_op jit(solution)/shard_map/ppermute | solution.py:123
  76.8 3.8 %collective-permute-done.6.refs_3_ = bf16[16,128,128]{2,1,0:T(8,128)(2,1)S(1)} collective-permute-done((bf16[16,128,128]{2,1,0:T(8,128)(2,1)S(1)}, bf16[16,128,128]{2,1,0:T(8,128)(2,1)S(1)}, u32[]{:S(2)}, u32[]{:S(2)}) %collective-permute-start.6) | collective-permute-done | bytes 524320 | tf_op jit(solution)/shard_map/ppermute | solution.py:123
  80.6 1.9 %collective-permute-start.13 = (bf16[16,128,128]{2,1,0:T(8,128)(2,1)S(1)}, bf16[16,128,128]{2,1,0:T(8,128)(2,1)S(1)}, u32[]{:S(2)}, u32[]{:S(2)}) collective-permute-start(bf16[16,128,128]{2,1,0:T(8,128)(2,1)S(1)} %collective-permute-done.8.refs_5_), channel_id=1, source_target_pairs={{64,0},{449,1},{128,64},{1,65},{192,128},{65,129},{256,192},{129,1... | collective-permute-start | bytes 1572872 | tf_op jit(solution)/shard_map/ppermute | solution.py:126
  82.5 5.0 %collective-permute-start.14 = (bf16[16,128,128]{2,1,0:T(8,128)(2,1)S(1)}, bf16[16,128,128]{2,1,0:T(8,128)(2,1)S(1)}, u32[]{:S(2)}, u32[]{:S(2)}) collective-permute-start(bf16[16,128,128]{2,1,0:T(8,128)(2,1)S(1)} %collective-permute-done.6.refs_3_), channel_id=1, source_target_pairs={{0,64},{1,449},{64,128},{65,1},{128,192},{129,65},{192,256},{193,1... | collective-permute-start | bytes 1572872 | tf_op jit(solution)/shard_map/ppermute | solution.py:123
  87.6 0.0 copy-start
  87.6 1.1 copy-done
  88.7 3.3 %shard_map.55 = (bf16[8,16,128,128]{3,2,1,0:T(8,128)(2,1)S(1)}, bf16[8,16,64,384]{3,2,1,0:T(8,128)(2,1)S(1)}, f32[256,384]{1,0:T(8,128)S(1)}) custom-call(s32[4]{0:T(128)S(1)} %pad_add_fusion.place, bf16[16,128,128]{2,1,0:T(8,128)(2,1)S(1)} %collective-permute-done.refs_0_, bf16[16,128,128]{2,1,0:T(8,128)(2,1)S(1)} %collective-permute-done.2.refs_1_, ...), custom_call_target="tpu_custom_call" | custom-call | flops 1073741824 | bytes 16777216 | tf_op jit(solution)/shard_map/pallas_call | solution.py:146
  92.0 2.1 %collective-permute-done.12.refs_1_.high = bf16[16,64,384]{2,1,0:T(8,128)(2,1)S(1)} collective-permute-done((bf16[16,64,384]{2,1,0:T(8,128)(2,1)S(1)}, bf16[16,64,384]{2,1,0:T(8,128)(2,1)S(1)}, u32[]{:S(2)}, u32[]{:S(2)}) %collective-permute-start.12) | collective-permute-done | bytes 786464 | tf_op jit(solution)/shard_map/ppermute | solution.py:123
  94.1 1.3 %shard_map.56.middle = f32[256,384]{1,0:T(8,128)S(1)} custom-call(s32[4]{0:T(128)S(1)} %pad_add_fusion.place, f32[256,384]{1,0:T(8,128)S(1)} %get-tuple-element.30.early, bf16[8,16,128,128]{3,2,1,0:T(8,128)(2,1)S(1)} %get-tuple-element.31.amp, bf16[16,64,384]{2,1,0:T(8,128)(2,1)S(1)} %collective-permute-done.11.refs_0_.low, ...), custom_call_target="tpu_custom_call" | custom-call | tf_op jit(solution)/shard_map/pallas_call | solution.py:155
  95.4 1.3 %shard_map.57.third = f32[256,384]{1,0:T(8,128)S(1)} custom-call(s32[4]{0:T(128)S(1)} %pad_add_fusion.place, f32[256,384]{1,0:T(8,128)S(1)} %shard_map.56.middle, bf16[8,16,64,384]{3,2,1,0:T(8,128)(2,1)S(1)} %get-tuple-element.34.held, bf16[1,16,128,128]{3,2,1,0:T(8,128)(2,1)S(1)} %bitcast.9, bf16[16,64,384]{2,1,0:T(8,128)(2,1)S(1)} %collective-permute-done.11.refs_0_.low, ...), custom_call_target="tpu_custom_call" | custom-call | tf_op jit(solution)/shard_map/pallas_call | solution.py:162
  96.7 0.0 copy-start.1
  96.7 0.0 copy-start.2
  96.8 0.8 collective-permute-done.14
  97.5 1.4 %shard_map.58 = f32[2,384,128]{2,1,0:T(8,128)S(1)} custom-call(s32[4]{0:T(128)S(1)} %pad_add_fusion.place, f32[256,384]{1,0:T(8,128)S(1)} %shard_map.57.third, bf16[8,16,64,384]{3,2,1,0:T(8,128)(2,1)S(1)} %get-tuple-element.34.held, bf16[1,16,128,128]{3,2,1,0:T(8,128)(2,1)S(1)} %bitcast.8, bf16[16,64,384]{2,1,0:T(8,128)(2,1)S(1)} %collective-permute-done.11.refs_0_.low, ...), custom_call_target="tpu_custom_call" | custom-call | tf_op jit(solution)/shard_map/pallas_call | solution.py:169
  98.9 12.9 %all_to_all.5 = f32[8,96,128]{2,1,0:T(8,128)S(1)} all-to-all(f32[8,96,128]{2,1,0:T(8,128)S(1)} %bitcast.7), channel_id=1, replica_groups=mesh['y'=8,'xl'=2,'z'=8,'xh'=2,'core'=2] {'xl','xh','core'}, dimensions={0} | all-to-all | bytes 786432 | tf_op jit(solution)/shard_map/all_to_all | solution.py:177
  111.9 0.7 add_divide_fusion
  (14 shorter events, 0.1 us)
Async XLA Ops:
  0.1 24.3 %collective-permute-start.1 = (bf16[16,64,384]{2,1,0:T(8,128)(2,1)}, bf16[16,64,384]{2,1,0:T(8,128)(2,1)S(1)}, u32[]{:S(2)}, u32[]{:S(2)}) collective-permute-start(bf16[16,64,384]{2,1,0:T(8,128)(2,1)} %refs_6_), channel_id=1, source_target_pairs={{0,4},{1,29},{4,8},{5,1},{8,12},{9,5},{12,16},{13,9},{16,20},{17,1... | collective-permute-start | bytes 2359304 | tf_op jit(solution)/shard_map/ppermute | solution.py:123
  11.6 18.0 %collective-permute-start = (bf16[16,128,128]{2,1,0:T(8,128)(2,1)}, bf16[16,128,128]{2,1,0:T(8,128)(2,1)S(1)}, u32[]{:S(2)}, u32[]{:S(2)}) collective-permute-start(bf16[16,128,128]{2,1,0:T(8,128)(2,1)} %param.6), channel_id=1, source_target_pairs={{0,0},{32,448},{64,64},{96,384},{128,128},{160,320},{192,192},{224... | collective-permute-start | bytes 1572872 | tf_op jit(solution)/shard_map/ppermute | solution.py:130
  13.3 27.2 %collective-permute-start.3 = (bf16[16,64,384]{2,1,0:T(8,128)(2,1)}, bf16[16,64,384]{2,1,0:T(8,128)(2,1)S(1)}, u32[]{:S(2)}, u32[]{:S(2)}) collective-permute-start(bf16[16,64,384]{2,1,0:T(8,128)(2,1)} %refs_6_), channel_id=1, source_target_pairs={{4,0},{29,1},{8,4},{1,5},{12,8},{5,9},{16,12},{9,13},{20,16},{13,1... | collective-permute-start | bytes 2359304 | tf_op jit(solution)/shard_map/ppermute | solution.py:126
  24.4 27.2 %collective-permute-start.9 = (bf16[16,64,384]{2,1,0:T(8,128)(2,1)S(1)}, bf16[16,64,384]{2,1,0:T(8,128)(2,1)S(1)}, u32[]{:S(2)}, u32[]{:S(2)}) collective-permute-start(bf16[16,64,384]{2,1,0:T(8,128)(2,1)S(1)} %collective-permute-done.1.refs_7_), channel_id=1, source_target_pairs={{0,4},{1,29},{4,8},{5,1},{8,12},{9,5},{12,16},{13,9},{16,20},{17,1... | collective-permute-start | bytes 2359304 | tf_op jit(solution)/shard_map/ppermute | solution.py:123
  29.6 17.0 %collective-permute-start.2 = (bf16[16,128,128]{2,1,0:T(8,128)(2,1)S(1)}, bf16[16,128,128]{2,1,0:T(8,128)(2,1)S(1)}, u32[]{:S(2)}, u32[]{:S(2)}) collective-permute-start(bf16[16,128,128]{2,1,0:T(8,128)(2,1)S(1)} %collective-permute-done.refs_0_), channel_id=1, source_target_pairs={{0,64},{1,449},{64,128},{65,1},{128,192},{129,65},{192,256},{193,1... | collective-permute-start | bytes 1572872 | tf_op jit(solution)/shard_map/ppermute | solution.py:123
  40.5 24.4 %collective-permute-start.5 = (bf16[16,64,384]{2,1,0:T(8,128)(2,1)S(1)}, bf16[16,64,384]{2,1,0:T(8,128)(2,1)S(1)}, u32[]{:S(2)}, u32[]{:S(2)}) collective-permute-start(bf16[16,64,384]{2,1,0:T(8,128)(2,1)S(1)} %collective-permute-done.3.refs_10_), channel_id=1, source_target_pairs={{4,0},{29,1},{8,4},{1,5},{12,8},{5,9},{16,12},{9,13},{20,16},{13,1... | collective-permute-start | bytes 2359304 | tf_op jit(solution)/shard_map/ppermute | solution.py:126
  42.5 16.4 %collective-permute-start.7 = (bf16[16,128,128]{2,1,0:T(8,128)(2,1)S(1)}, bf16[16,128,128]{2,1,0:T(8,128)(2,1)S(1)}, u32[]{:S(2)}, u32[]{:S(2)}) collective-permute-start(bf16[16,128,128]{2,1,0:T(8,128)(2,1)S(1)} %collective-permute-done.refs_0_), channel_id=1, source_target_pairs={{64,0},{449,1},{128,64},{1,65},{192,128},{65,129},{256,192},{129,1... | collective-permute-start | bytes 1572872 | tf_op jit(solution)/shard_map/ppermute | solution.py:126
  46.6 16.4 %collective-permute-start.4 = (bf16[16,128,128]{2,1,0:T(8,128)(2,1)S(1)}, bf16[16,128,128]{2,1,0:T(8,128)(2,1)S(1)}, u32[]{:S(2)}, u32[]{:S(2)}) collective-permute-start(bf16[16,128,128]{2,1,0:T(8,128)(2,1)S(1)} %collective-permute-done.2.refs_1_), channel_id=1, source_target_pairs={{0,64},{1,449},{64,128},{65,1},{128,192},{129,65},{192,256},{193,1... | collective-permute-start | bytes 1572872 | tf_op jit(solution)/shard_map/ppermute | solution.py:123
  51.7 20.6 %collective-permute-start.10 = (bf16[16,64,384]{2,1,0:T(8,128)(2,1)S(1)}, bf16[16,64,384]{2,1,0:T(8,128)(2,1)S(1)}, u32[]{:S(2)}, u32[]{:S(2)}) collective-permute-start(bf16[16,64,384]{2,1,0:T(8,128)(2,1)S(1)} %collective-permute-done.9.refs_8_), channel_id=1, source_target_pairs={{0,4},{1,29},{4,8},{5,1},{8,12},{9,5},{12,16},{13,9},{16,20},{17,1... | collective-permute-start | bytes 2359304 | tf_op jit(solution)/shard_map/ppermute | solution.py:123
  63.0 13.8 %collective-permute-start.8 = (bf16[16,128,128]{2,1,0:T(8,128)(2,1)S(1)}, bf16[16,128,128]{2,1,0:T(8,128)(2,1)S(1)}, u32[]{:S(2)}, u32[]{:S(2)}) collective-permute-start(bf16[16,128,128]{2,1,0:T(8,128)(2,1)S(1)} %collective-permute-done.7.refs_4_), channel_id=1, source_target_pairs={{64,0},{449,1},{128,64},{1,65},{192,128},{65,129},{256,192},{129,1... | collective-permute-start | bytes 1572872 | tf_op jit(solution)/shard_map/ppermute | solution.py:126
  65.0 15.7 %collective-permute-start.6 = (bf16[16,128,128]{2,1,0:T(8,128)(2,1)S(1)}, bf16[16,128,128]{2,1,0:T(8,128)(2,1)S(1)}, u32[]{:S(2)}, u32[]{:S(2)}) collective-permute-start(bf16[16,128,128]{2,1,0:T(8,128)(2,1)S(1)} %collective-permute-done.4.refs_2_), channel_id=1, source_target_pairs={{0,64},{1,449},{64,128},{65,1},{128,192},{129,65},{192,256},{193,1... | collective-permute-start | bytes 1572872 | tf_op jit(solution)/shard_map/ppermute | solution.py:123
  70.3 21.7 %collective-permute-start.11 = (bf16[16,64,384]{2,1,0:T(8,128)(2,1)S(1)}, bf16[16,64,384]{2,1,0:T(8,128)(2,1)S(1)}, u32[]{:S(2)}, u32[]{:S(2)}) collective-permute-start(bf16[16,64,384]{2,1,0:T(8,128)(2,1)S(1)} %collective-permute-done.5.refs_11_), channel_id=1, source_target_pairs={{4,0},{29,1},{8,4},{1,5},{12,8},{5,9},{16,12},{9,13},{20,16},{13,1... | collective-permute-start | bytes 2359304 | tf_op jit(solution)/shard_map/ppermute | solution.py:126
  72.2 21.9 %collective-permute-start.12 = (bf16[16,64,384]{2,1,0:T(8,128)(2,1)S(1)}, bf16[16,64,384]{2,1,0:T(8,128)(2,1)S(1)}, u32[]{:S(2)}, u32[]{:S(2)}) collective-permute-start(bf16[16,64,384]{2,1,0:T(8,128)(2,1)S(1)} %collective-permute-done.10.refs_9_), channel_id=1, source_target_pairs={{0,4},{1,29},{4,8},{5,1},{8,12},{9,5},{12,16},{13,9},{16,20},{17,1... | collective-permute-start | bytes 2359304 | tf_op jit(solution)/shard_map/ppermute | solution.py:123
  80.6 14.8 %collective-permute-start.13 = (bf16[16,128,128]{2,1,0:T(8,128)(2,1)S(1)}, bf16[16,128,128]{2,1,0:T(8,128)(2,1)S(1)}, u32[]{:S(2)}, u32[]{:S(2)}) collective-permute-start(bf16[16,128,128]{2,1,0:T(8,128)(2,1)S(1)} %collective-permute-done.8.refs_5_), channel_id=1, source_target_pairs={{64,0},{449,1},{128,64},{1,65},{192,128},{65,129},{256,192},{129,1... | collective-permute-start | bytes 1572872 | tf_op jit(solution)/shard_map/ppermute | solution.py:126
  82.5 15.0 %collective-permute-start.14 = (bf16[16,128,128]{2,1,0:T(8,128)(2,1)S(1)}, bf16[16,128,128]{2,1,0:T(8,128)(2,1)S(1)}, u32[]{:S(2)}, u32[]{:S(2)}) collective-permute-start(bf16[16,128,128]{2,1,0:T(8,128)(2,1)S(1)} %collective-permute-done.6.refs_3_), channel_id=1, source_target_pairs={{0,64},{1,449},{64,128},{65,1},{128,192},{129,65},{192,256},{193,1... | collective-permute-start | bytes 1572872 | tf_op jit(solution)/shard_map/ppermute | solution.py:123
  87.6 1.1 %copy-start = (bf16[16,64,384]{2,1,0:T(8,128)(2,1)S(1)}, bf16[16,64,384]{2,1,0:T(8,128)(2,1)}, u32[]{:S(2)}) copy-start(bf16[16,64,384]{2,1,0:T(8,128)(2,1)} %refs_6_) | copy-start | bytes 2359300
  96.7 15.1 %copy-start.1 = (bf16[96,128]{1,0:T(8,128)(2,1)S(1)}, bf16[96,128]{1,0:T(8,128)(2,1)}, u32[]{:S(2)}) copy-start(bf16[96,128]{1,0:T(8,128)(2,1)} %param.7) | copy-start | bytes 73732
  96.7 15.1 %copy-start.2 = (f32[128]{0:T(128)S(1)}, f32[128]{0:T(128)}, u32[]{:S(2)}) copy-start(f32[128]{0:T(128)} %param.9) | copy-start | bytes 1540
  96.7 15.1 %copy-start.3 = (f32[96]{0:T(128)S(1)}, f32[96]{0:T(128)}, u32[]{:S(2)}) copy-start(f32[96]{0:T(128)} %param.8) | copy-start | bytes 1156
